TPU v7x, 32 devices: a whole 2x2x4 slice. The times are simulated.
32 devices in a mesh: expert: 16 (over z, y, x), tensor: 2 (over core).
Axes of the slice: x: 2, y: 2, z: 4, core: 2. Of those that a mesh axis runs over, the one named last changes fastest.
Arguments:
- tokens: bfloat16 [512, 4096], P('expert'), may hold values from -6 to 6
- routes: int32 [512, 8], P('expert'), may hold values from 0 to 15, all different within a row; in each aligned block of 32 rows (0 to 31, 32 to 63, ...) at most 24 rows name the same one
- route_weights: float32 [512, 8], P('expert'), may hold values from 0.1 to 1
- learner_weights: bfloat16 [16, 4096, 1536], P(None, 'expert', 'tensor'), may hold values from -5 to 5
Outputs:
- combined: bfloat16 [512, 1536], P('expert', 'tensor')
- expert_amax: float32 [16], P('expert')
Inputs may be any that keep to these rules, and one draw needn't show every extreme that they name: `routes`: each row names 8 different experts; within the 32 rows of one index of expert no expert is named by more than 24 rows, a bound that some block reaches there.
All inputs are finite; a program needn't handle non-finite values.
Results may differ from a plain program's by a relative error of at most 0.0049.
Values may be sent and summed in bfloat16 or wider, within the bound.
No kernel may reach another device: no remote copies, remote signals or barrier semaphores. Data moves between devices by JAX's collectives and lax.ppermute only.
A program may use at most 64 MiB of HBM per device.

v0:
```python
import jax
import jax.numpy as jnp
from jax import lax
from jax.sharding import PartitionSpec as P


def shards(tokens, routes, route_weights, learner_weights):
    expert_count = lax.axis_size("expert")
    row_count, width = tokens.shape
    choose_count = routes.shape[1]
    capacity = min(row_count, max(2, 3 * row_count * choose_count // (2 * expert_count)))
    flat_ids = routes.reshape(-1)
    one_hot = (flat_ids[:, None] == jnp.arange(expert_count, dtype=jnp.int32)[None, :]).astype(
        jnp.int32
    )
    slot_rank = jnp.sum(jnp.cumsum(one_hot, axis=0) * one_hot, axis=1) - 1
    slot_index = flat_ids * capacity + slot_rank
    token_of = jnp.arange(flat_ids.shape[0], dtype=jnp.int32) // choose_count
    relaid = lax.all_to_all(learner_weights, "expert", split_axis=0, concat_axis=1, tiled=True)
    own_weight = relaid[0]
    local_max = jnp.max(jnp.abs(own_weight)).astype(jnp.float32).reshape(1)
    expert_amax = lax.pmax(local_max, "tensor")
    quarter = width // lax.axis_size("tensor")
    columns = lax.dynamic_slice_in_dim(tokens, lax.axis_index("tensor") * quarter, quarter, 1)
    send_buffer = jnp.zeros((expert_count * capacity, quarter), jnp.bfloat16)
    send_buffer = (
        send_buffer.at[slot_index].set(columns[token_of]).reshape(expert_count, capacity, quarter)
    )
    results = jnp.einsum(
        "skd,df->skf",
        lax.all_gather(
            lax.all_to_all(send_buffer, "expert", split_axis=0, concat_axis=0, tiled=True),
            "tensor",
            axis=2,
            tiled=True,
        ),
        own_weight,
        preferred_element_type=jnp.float32,
    ).astype(jnp.bfloat16)
    returned = lax.all_to_all(results, "expert", split_axis=0, concat_axis=0, tiled=True)
    picked = returned.reshape(expert_count * capacity, -1)[slot_index].astype(jnp.float32)
    weighted = (picked * route_weights.reshape(-1, 1)).reshape(row_count, choose_count, -1)
    combined = jnp.sum(weighted, axis=1).astype(jnp.bfloat16)
    return (combined, expert_amax)


def solution(mesh):
    return jax.shard_map(
        shards,
        mesh=mesh,
        in_specs=(
            P("expert", None),
            P("expert", None),
            P("expert", None),
            P(None, "expert", "tensor"),
        ),
        out_specs=(P("expert", "tensor"), P("expert")),
        check_vma=False,
    )
```

profile of v0, /device:TPU:0, one launch (start us, length us, event | category | flops | bytes accessed | tf_op | source)
XLA Modules:
  0.0 241.1 jit_solution(534507781039737360)
XLA Ops:
  7.2 0.8 copy.8
  8.0 0.1 eq.29
  8.1 0.1 eq.25
  8.2 0.7 broadcast_multiply_fusion
  8.9 0.6 reduce-window.6
  9.5 0.2 slice_reduce_fusion
  9.7 0.1 fusion.5
  9.8 0.1 copy.7
  9.9 0.1 mul.33
  10.0 5.9 %scatter_custom_fusion = bf16[384,2048]{1,0:T(8,128)(2,1)S(1)} fusion(s32[256]{0:T(256)S(1)} %bitcast.32, bf16[32,2048]{1,0:T(8,128)(2,1)S(1)} %constant_dynamic-slice_fusion, s32[1024]{0:T(1024)S(1)} %pad_clamp_fusion.1, bf16[]{:T(256)} %constant.16.clone.1), kind=kCustom, calls=%fused_computation.5 | custom fusion | bytes 1572866 | tf_op jit(solution)/shard_map/scatter | solution.py:27
  16.0 45.8 %all_to_all.19 = bf16[16,24,2048]{2,1,0:T(8,128)(2,1)} all-to-all(bf16[16,24,2048]{2,1,0:T(8,128)(2,1)S(1)} %bitcast.31), channel_id=1, replica_groups=mesh['expert'=16,'tensor'=2] {'expert'}, dimensions={0} | all-to-all | bytes 3145728 | tf_op jit(solution)/shard_map/all_to_all | solution.py:32
  61.8 4.6 %all-to-all-start.1 = ((bf16[16,256,768]{2,1,0:T(8,128)(2,1)}), bf16[16,256,768]{2,1,0:T(8,128)(2,1)}, u32[]{:S(2)}, u32[]{:S(2)}) async-start(bf16[16,256,768]{2,1,0:T(8,128)(2,1)} %param.7), calls=%async_computation.1 | async-start | bytes 12582912 | tf_op jit(solution)/shard_map/all_to_all | solution.py:19
  66.4 0.0 all-gather.2.cloned.1.call-start
  66.5 0.7 all-gather.2.cloned.1.call-update
  67.2 15.0 %all-gather.2.cloned.1.call-done = bf16[16,24,4096]{2,1,0:T(8,128)(2,1)} async-done(((bf16[16,24,2048]{2,1,0:T(8,128)(2,1)}), bf16[16,24,4096]{2,1,0:T(8,128)(2,1)}) %all-gather.2.cloned.1.call-update) | async-done | bytes 3145744 | tf_op jit(solution)/shard_map/all_gather | solution.py:31
  82.2 99.1 %all-to-all-done.1 = bf16[16,256,768]{2,1,0:T(8,128)(2,1)} async-done(((bf16[16,256,768]{2,1,0:T(8,128)(2,1)}), bf16[16,256,768]{2,1,0:T(8,128)(2,1)}, u32[]{:S(2)}, u32[]{:S(2)}) %all-to-all-start.1) | async-done | bytes 6291488 | tf_op jit(solution)/shard_map/all_to_all | solution.py:19
  181.2 7.2 %convolution_convert_fusion = bf16[16,24,768]{2,1,0:T(8,128)(2,1)} fusion(bf16[16,24,4096]{2,1,0:T(8,128)(2,1)} %all-gather.2.cloned.1.call-done, bf16[4096,768,1]{1,0,2:T(8,128)(2,1)} %bitcast.6), kind=kOutput, calls=%fused_computation.4 | convolution fusion | flops 2416214016 | bytes 10027008 | tf_op jit(solution)/shard_map/skd,df->skf/dot_general | solution.py:29
  188.4 28.3 %all-to-all-start.2 = ((bf16[16,24,768]{2,1,0:T(8,128)(2,1)}), bf16[16,24,768]{2,1,0:T(8,128)(2,1)S(1)}, u32[]{:S(2)}, u32[]{:S(2)}) async-start(bf16[16,24,768]{2,1,0:T(8,128)(2,1)} %convolution_convert_fusion), calls=%async_computation.2 | async-start | bytes 1179648 | tf_op jit(solution)/shard_map/all_to_all | solution.py:40
  216.7 0.1 copy.11
  216.8 4.2 %abs_reduce_fusion = bf16[]{:T(256)} fusion(bf16[16,256,768]{2,1,0:T(8,128)(2,1)} %all-to-all-done.1), kind=kLoop, calls=%fused_computation.3 | loop fusion | flops 6291455 | bytes 6291458 | tf_op jit(solution)/shard_map/reduce_max | solution.py:21
  221.0 3.1 %pmax.7 = f32[1]{0:T(128)} all-reduce(bf16[1]{0:T(256)(128)(2,1)} %bitcast.12), channel_id=1, replica_groups=mesh['expert'=16,'tensor'=2] {'tensor'}, use_global_device_ids=true, to_apply=%region_6.7 | all-reduce | flops 1 | bytes 6 | tf_op jit(solution)/shard_map/pmax | solution.py:22
  224.1 8.1 %all-to-all-done.2 = bf16[16,24,768]{2,1,0:T(8,128)(2,1)S(1)} async-done(((bf16[16,24,768]{2,1,0:T(8,128)(2,1)}), bf16[16,24,768]{2,1,0:T(8,128)(2,1)S(1)}, u32[]{:S(2)}, u32[]{:S(2)}) %all-to-all-start.2) | async-done | bytes 589856 | tf_op jit(solution)/shard_map/all_to_all | solution.py:40
  232.2 1.2 gather_fusion
  233.4 0.9 fusion.2
  (13 shorter events, 0.1 us)
Async XLA Ops:
  7.2 2.8 %copy-start = (bf16[32,4096]{1,0:T(8,128)(2,1)S(1)}, bf16[32,4096]{1,0:T(8,128)(2,1)}, u32[]{:S(2)}) copy-start(bf16[32,4096]{1,0:T(8,128)(2,1)} %param.4) | copy-start | bytes 786436
  61.8 119.4 %all-to-all-start.1 = ((bf16[16,256,768]{2,1,0:T(8,128)(2,1)}), bf16[16,256,768]{2,1,0:T(8,128)(2,1)}, u32[]{:S(2)}, u32[]{:S(2)}) async-start(bf16[16,256,768]{2,1,0:T(8,128)(2,1)} %param.7), calls=%async_computation.1 | async-start | bytes 12582912 | tf_op jit(solution)/shard_map/all_to_all | solution.py:19
  66.4 15.7 %all-gather.2.cloned.1.call-start = ((), (), s32[]{:S(2)}) async-start(), calls=%async_computation.3 | async-start | bytes 4718592 | tf_op jit(solution)/shard_map/all_gather | solution.py:31
  181.2 35.5 %copy-start.1 = (f32[32,8]{0,1:T(8,128)S(1)}, f32[32,8]{0,1:T(8,128)}, u32[]{:S(2)}) copy-start(f32[32,8]{0,1:T(8,128)} %param.6) | copy-start | bytes 3076
  188.4 43.8 %all-to-all-start.2 = ((bf16[16,24,768]{2,1,0:T(8,128)(2,1)}), bf16[16,24,768]{2,1,0:T(8,128)(2,1)S(1)}, u32[]{:S(2)}, u32[]{:S(2)}) async-start(bf16[16,24,768]{2,1,0:T(8,128)(2,1)} %convolution_convert_fusion), calls=%async_computation.2 | async-start | bytes 1179648 | tf_op jit(solution)/shard_map/all_to_all | solution.py:40
Sparse Core Ops, SparseCore 0:
  68.8 13.3 all-gather.1
where the time goes:
time: 242 us; the launch traced here: 241 us
  waiting for transfers between devices  123 us (51%)
  blocking collectives  48.9 us (20%)
  starting transfers between devices  33 us (14%)
  between operations  14.1 us (6%)
  local copies, waits for them, and re-layouts  8.55 us (4%)
  matrix products  7.18 us (3%)
  other arithmetic  6.58 us (3%)
    all_to_all x1, waiting for transfers between devices, shards(): lax.all_to_all(learner_weights, 'expert', split_axis=0, concat_axis=1, ti...  99.1 us
    all_to_all x1, blocking collectives, shards(): lax.all_to_all(send_buffer, 'expert', split_axis=0, concat_axis=0, tiled=...  45.8 us
    all_to_all x1, starting transfers between devices, shards(): lax.all_to_all(results, 'expert', split_axis=0, concat_axis=0, tiled=True)  28.3 us
    all_gather x1, waiting for transfers between devices, shards(): lax.all_gather(lax.all_to_all(send_buffer, 'expert', split_axis=0, concat...  15 us
    all_to_all x1, waiting for transfers between devices, shards(): lax.all_to_all(results, 'expert', split_axis=0, concat_axis=0, tiled=True)  8.07 us
    dot_general x1, matrix products, shards(): jnp.einsum('skd,df->skf', lax.all_gather(lax.all_to_all(send_buffer, 'exp...  7.18 us
    scatter x1, local copies, waits for them, and re-layouts, shards(): send_buffer.at[slot_index].set(columns[token_of])  5.92 us
  transfers between devices with their start and end apart: 3, of which 3 were waited for; matrix products, arithmetic and copies ran while one was open for 2% of the time, Pallas kernels for 0%

commit v1 on v0

v1 whole, which is shorter than its diff:
```python
import jax
import jax.numpy as jnp
from jax import lax
from jax.sharding import PartitionSpec as P


def shards(tokens, routes, route_weights, learner_weights):
    n = lax.axis_size("expert")
    rows, width = tokens.shape
    experts, depth, ff = learner_weights.shape
    local_max = lax.pmax(
        jnp.max(jnp.abs(learner_weights), axis=(1, 2)).astype(jnp.float32), "tensor"
    )
    chosen = routes[:, :, None] == jnp.arange(experts, dtype=jnp.int32)
    gate = jnp.sum(jnp.where(chosen, route_weights[:, :, None], 0.0), axis=1)
    high = lax.reduce_precision(gate, 8, 7)
    low = gate - high
    extras = jnp.concatenate([high, low], axis=1).astype(jnp.bfloat16)
    columns = tokens.reshape(rows, n, depth).transpose(1, 0, 2)
    largest = jnp.broadcast_to(local_max.astype(jnp.bfloat16)[:, None, None], (n, rows, 1))
    send = jnp.concatenate(
        [columns, jnp.broadcast_to(extras, (n, rows, 2 * experts)), largest], axis=2
    )
    got = lax.all_to_all(send, "expert", split_axis=0, concat_axis=0, tiled=True)
    expert_amax = jnp.max(got[:, 0, depth + 2 * experts]).astype(jnp.float32).reshape(1)
    x = got[:, :, :depth].reshape(n * rows, depth).astype(jnp.float32)
    extras = got[:, :, depth : depth + 2 * experts].astype(jnp.float32).reshape(n * rows, -1)
    gates = extras[:, :experts] + extras[:, experts:]
    scaled = (x[:, None, :] * gates[:, :, None]).astype(jnp.bfloat16)
    partial = jnp.dot(
        scaled.reshape(n * rows, experts * depth),
        learner_weights.reshape(experts * depth, ff),
        preferred_element_type=jnp.float32,
    ).astype(jnp.bfloat16)
    back = lax.all_to_all(
        partial.reshape(n, rows, ff), "expert", split_axis=0, concat_axis=0, tiled=True
    )
    combined = jnp.sum(back.astype(jnp.float32), axis=0).astype(jnp.bfloat16)
    return (combined, expert_amax)


def solution(mesh):
    return jax.shard_map(
        shards,
        mesh=mesh,
        in_specs=(
            P("expert", None),
            P("expert", None),
            P("expert", None),
            P(None, "expert", "tensor"),
        ),
        out_specs=(P("expert", "tensor"), P("expert")),
        check_vma=False,
    )
```

time: 242 us -> 61.4 us (0.25)
  waiting for transfers between devices: 123 us -> 17.8 us
  starting transfers between devices: 33 us -> 3.63 us
  blocking collectives: 48.9 us -> 23.5 us
  between operations: 14.1 us -> 2.54 us
  local copies, waits for them, and re-layouts: 8.55 us -> 0.71 us
    all_to_all x2 -> x1, waiting for transfers between devices: 107 us -> 17.8 us  [shards(): lax.all_to_all(partial.reshape(n, rows, ff), 'expert', split_axis=0, conc...]
    all_to_all x2 -> x1, starting transfers between devices: 32.9 us -> 3.63 us  [shards(): lax.all_to_all(partial.reshape(n, rows, ff), 'expert', split_axis=0, conc...]
    all_to_all x1, blocking collectives: 45.8 us -> 20.9 us  [shards(): lax.all_to_all(send, 'expert', split_axis=0, concat_axis=0, tiled=True)]
    all_gather x1 -> x0, waiting for transfers between devices: 15 us -> none  [shards(): lax.all_gather(lax.all_to_all(send_buffer, 'expert', split_axis=0, concat...]
    scatter x1 -> x0, local copies, waits for them, and re-layouts: 5.92 us -> none  [shards(): send_buffer.at[slot_index].set(columns[token_of])]
  transfers between devices with their start and end apart: 3 -> 1, of which waited for: 3 -> 1; matrix products, arithmetic and copies ran while one was open for 2% -> 1% of each run, Pallas kernels for 0% -> 0%
where the time goes in v1:
time: 61.4 us; the launch traced here: 61.1 us
  blocking collectives  23.5 us (38%)
  waiting for transfers between devices  17.8 us (29%)
  matrix products  7.13 us (12%)
  other arithmetic  5.73 us (9%)
  starting transfers between devices  3.63 us (6%)
  between operations  2.54 us (4%)
  local copies, waits for them, and re-layouts  0.71 us (1%)
    all_to_all x1, blocking collectives, shards(): lax.all_to_all(send, 'expert', split_axis=0, concat_axis=0, tiled=True)  20.9 us
    all_to_all x1, waiting for transfers between devices, shards(): lax.all_to_all(partial.reshape(n, rows, ff), 'expert', split_axis=0, conc...  17.8 us
    dot_general x1, matrix products, shards(): jnp.dot(scaled.reshape(n * rows, experts * depth), learner_weights.reshap...  7.13 us
    reduce_max x1, other arithmetic, shards(): jnp.max(jnp.abs(learner_weights), axis=(1, 2)).astype(jnp.float32)  4.07 us
    all_to_all x1, starting transfers between devices, shards(): lax.all_to_all(partial.reshape(n, rows, ff), 'expert', split_axis=0, conc...  3.63 us
    pmax x1, blocking collectives, shards(): lax.pmax(jnp.max(jnp.abs(learner_weights), axis=(1, 2)).astype(jnp.float3...  2.58 us
  transfers between devices with their start and end apart: 1, of which 1 were waited for; matrix products, arithmetic and copies ran while one was open for 1% of the time, Pallas kernels for 0%

profile of v1, /device:TPU:0, one launch (start us, length us, event | category | flops | bytes accessed | tf_op | source)
XLA Modules:
  0.0 61.1 jit_solution(11957211165234408191)
XLA Ops:
  0.6 0.0 copy-start.1
  0.6 0.0 copy-start.2
  0.6 0.0 copy-start
  0.7 4.1 %abs_reduce_fusion = bf16[16]{0:T(256)(128)(2,1)S(1)} fusion(bf16[16,256,768]{2,1,0:T(8,128)(2,1)} %param.7), kind=kLoop, calls=%fused_computation.1 | loop fusion | flops 6291440 | bytes 6291488 | tf_op jit(solution)/shard_map/reduce_max | solution.py:12
  4.7 2.6 %pmax.7 = bf16[16]{0:T(256)(128)(2,1)S(1)} all-reduce(bf16[16]{0:T(256)(128)(2,1)S(1)} %abs_reduce_fusion), channel_id=1, replica_groups=mesh['expert'=16,'tensor'=2] {'tensor'}, use_global_device_ids=true, to_apply=%region_2.3 | all-reduce | flops 16 | bytes 64 | tf_op jit(solution)/shard_map/pmax | solution.py:11
  7.3 0.0 copy-done.1
  7.3 0.0 copy-done.2
  7.4 0.1 copy.19
  7.4 0.0 copy-done
  7.5 0.1 copy.25
  7.5 0.1 broadcast_in_dim.29
  7.6 0.1 pad_maximum_fusion
  7.7 0.1 copy.20
  7.8 20.9 %all_to_all.10 = bf16[16,32,289]{2,1,0:T(8,128)(2,1)S(1)} all-to-all(bf16[16,32,289]{2,1,0:T(8,128)(2,1)S(1)} %copy.20), channel_id=1, replica_groups=mesh['expert'=16,'tensor'=2] {'expert'}, dimensions={0} | all-to-all | bytes 591872 | tf_op jit(solution)/shard_map/all_to_all | solution.py:24
  28.8 0.1 bitcast_convert_fusion.1
  28.9 0.1 fusion.4
  29.0 0.1 copy.24
  29.1 0.1 copy.23
  29.3 7.1 %bitcast_convert_fusion = bf16[512,768]{1,0:T(8,128)(2,1)} fusion(bf16[16,256,768]{2,1,0:T(8,128)(2,1)} %param.7, f32[512,16]{0,1:T(8,128)S(1)} %add.3, f32[512,256]{1,0:T(8,128)S(1)} %bitcast_convert_fusion.1), kind=kOutput, calls=%fused_computation.5 | convolution fusion | flops 3225812992 | bytes 7634944 | tf_op jit(solution)/shard_map/dot_general | solution.py:30
  36.4 3.6 %all-to-all-start.1 = ((bf16[16,32,768]{2,1,0:T(8,128)(2,1)}), bf16[16,32,768]{2,1,0:T(8,128)(2,1)S(1)}, u32[]{:S(2)}, u32[]{:S(2)}) async-start(bf16[16,32,768]{2,1,0:T(8,128)(2,1)} %bitcast.5), calls=%async_computation.1 | async-start | bytes 1572864 | tf_op jit(solution)/shard_map/all_to_all | solution.py:35
  40.0 0.7 %slice_reduce_fusion = bf16[]{:T(256)} fusion(bf16[16,32,289]{2,1,0:T(8,128)(2,1)S(1)} %all_to_all.10), kind=kLoop, calls=%fused_computation.14 | loop fusion | flops 15 | bytes 34 | tf_op jit(solution)/shard_map/reduce_max | solution.py:25
  41.4 17.8 %all-to-all-done.1 = bf16[16,32,768]{2,1,0:T(8,128)(2,1)S(1)} async-done(((bf16[16,32,768]{2,1,0:T(8,128)(2,1)}), bf16[16,32,768]{2,1,0:T(8,128)(2,1)S(1)}, u32[]{:S(2)}, u32[]{:S(2)}) %all-to-all-start.1) | async-done | bytes 786464 | tf_op jit(solution)/shard_map/all_to_all | solution.py:35
  59.2 0.7 %reduce_sum.22 = bf16[32,768]{1,0:T(8,128)(2,1)} reduce(bf16[16,32,768]{2,1,0:T(8,128)(2,1)S(1)} %all-to-all-done.1, bf16[]{:T(256)} %constant.5.clone.1), dimensions={0}, to_apply=%region_3.4 | reduce | flops 368640 | bytes 835586 | tf_op jit(solution)/shard_map/reduce_sum | solution.py:38
  (8 shorter events, 0.1 us)
Async XLA Ops:
  0.6 6.7 %copy-start.1 = (f32[32,8]{0,1:T(8,128)S(1)}, f32[32,8]{0,1:T(8,128)}, u32[]{:S(2)}) copy-start(f32[32,8]{0,1:T(8,128)} %param.6) | copy-start | bytes 3076
  0.6 6.7 %copy-start.2 = (s32[32,8]{0,1:T(8,128)S(1)}, s32[32,8]{0,1:T(8,128)}, u32[]{:S(2)}) copy-start(s32[32,8]{0,1:T(8,128)} %param.5) | copy-start | bytes 3076
  0.6 6.8 %copy-start = (bf16[32,4096]{1,0:T(8,128)(2,1)S(1)}, bf16[32,4096]{1,0:T(8,128)(2,1)}, u32[]{:S(2)}) copy-start(bf16[32,4096]{1,0:T(8,128)(2,1)} %param.4) | copy-start | bytes 786436
  36.4 22.8 %all-to-all-start.1 = ((bf16[16,32,768]{2,1,0:T(8,128)(2,1)}), bf16[16,32,768]{2,1,0:T(8,128)(2,1)S(1)}, u32[]{:S(2)}, u32[]{:S(2)}) async-start(bf16[16,32,768]{2,1,0:T(8,128)(2,1)} %bitcast.5), calls=%async_computation.1 | async-start | bytes 1572864 | tf_op jit(solution)/shard_map/all_to_all | solution.py:35

commit v2 on v1

v2 whole, which is shorter than its diff:
```python
import functools

import jax
import jax.numpy as jnp
from jax import lax
from jax.experimental import pallas as pl
from jax.experimental.pallas import tpu as pltpu
from jax.sharding import PartitionSpec as P

LANES = 128


def partial_kernel(got_ref, weight_ref, *rest, n, rows, depth, experts, other):
    tail_ref, out_ref, scaled_ref = rest if other else (None, *rest)
    half = n // 2
    ff = weight_ref.shape[1]
    mine = (lax.axis_index("expert") >= half).astype(jnp.int32)
    first = (1 - mine if other else mine) * half
    step = max(1, 64 // rows)
    for r in range(0, half, step):
        count = step * rows
        block = got_ref[pl.ds(first + r, step)].reshape(count, -1)
        x = block[:, :depth].astype(jnp.float32)
        extras = block[:, depth:].astype(jnp.float32)
        gates = extras[:, :experts] + extras[:, experts : 2 * experts]
        for e in range(experts):
            scaled_ref[r * rows : r * rows + count, e * depth : (e + 1) * depth] = (
                x * gates[:, e : e + 1]
            ).astype(jnp.bfloat16)
    product = jnp.dot(scaled_ref[...], weight_ref[...], preferred_element_type=jnp.float32)
    out_ref[:, :, :ff] = product.astype(jnp.bfloat16).reshape(half, rows, ff)
    if other:
        out_ref[:, :, ff:] = tail_ref[...]


def partials(got, weight, tail, n, rows, depth, experts):
    half, ff = n // 2, weight.shape[1]
    width = ff + (0 if tail is None else tail.shape[2])
    operands = (got, weight) if tail is None else (got, weight, tail)
    return pl.pallas_call(
        functools.partial(
            partial_kernel,
            n=n,
            rows=rows,
            depth=depth,
            experts=experts,
            other=tail is not None,
        ),
        out_shape=jax.ShapeDtypeStruct((half, rows, width), jnp.bfloat16),
        in_specs=[pl.BlockSpec(memory_space=pltpu.VMEM)] * len(operands),
        out_specs=pl.BlockSpec(memory_space=pltpu.VMEM),
        scratch_shapes=[pltpu.VMEM((half * rows, experts * depth), jnp.bfloat16)],
        compiler_params=pltpu.CompilerParams(vmem_limit_bytes=24 << 20),
        cost_estimate=pl.CostEstimate(
            flops=2 * half * rows * experts * depth * ff,
            bytes_accessed=weight.size * 2,
            transcendentals=0,
        ),
    )(*operands)


def plain_partials(got, weight, tail, n, rows, depth, experts):
    half, ff = n // 2, weight.shape[1]
    mine = (lax.axis_index("expert") >= half).astype(jnp.int32)
    first = (mine if tail is None else 1 - mine) * half
    blocks = lax.dynamic_slice_in_dim(got, first, half, 0)

    def one(block):
        block = block.astype(jnp.float32)
        gates = block[:, depth : depth + experts] + block[:, depth + experts : depth + 2 * experts]
        scaled = (block[:, None, :depth] * gates[:, :, None]).astype(jnp.bfloat16)
        product = jnp.dot(
            scaled.reshape(rows, experts * depth), weight, preferred_element_type=jnp.float32
        )
        return product.astype(jnp.bfloat16)

    out = lax.map(one, blocks)
    return out if tail is None else jnp.concatenate([out, tail], axis=2)


def shards(tokens, routes, route_weights, learner_weights):
    n, pair = lax.axis_size("expert"), lax.axis_size("tensor")
    rows, width = tokens.shape
    experts, depth, ff = learner_weights.shape
    half = n // 2
    halves = [list(range(half)), list(range(half, n))]
    weight = learner_weights.reshape(experts * depth, ff)
    chosen = routes[:, :, None] == jnp.arange(experts, dtype=jnp.int32)
    gate = jnp.sum(jnp.where(chosen, route_weights[:, :, None], 0.0), axis=1)
    high = lax.reduce_precision(gate, 8, 7)
    low = gate - high
    extras = jnp.concatenate([high, low], axis=1).astype(jnp.bfloat16)
    extras = jnp.pad(extras, ((0, 0), (0, -(2 * experts) % LANES)))
    columns = tokens.reshape(rows, n, depth).transpose(1, 0, 2)
    send = jnp.concatenate([columns, jnp.broadcast_to(extras, (n, *extras.shape))], axis=2)
    got = lax.all_to_all(send, "expert", split_axis=0, concat_axis=0, tiled=True)
    largest = jnp.max(jnp.abs(learner_weights), axis=(1, 2))
    if pair == 2:
        largest = jnp.maximum(largest, lax.ppermute(largest, "tensor", [(0, 1), (1, 0)]))
    else:
        largest = lax.pmax(largest, "tensor")
    mine = (lax.axis_index("expert") >= half).astype(jnp.int32)
    theirs_max = lax.dynamic_slice_in_dim(largest, (1 - mine) * half, half, 0)
    mine_max = lax.dynamic_slice_in_dim(largest, mine * half, half, 0)
    tail = jnp.concatenate(
        [
            jnp.broadcast_to(part[:, None, None], (half, rows // 2, LANES))
            for part in (theirs_max, mine_max)
        ],
        axis=1,
    )
    compute = partials if depth % LANES == 0 and ff % LANES == 0 else plain_partials
    shape = (n, rows, depth, experts)
    other = compute(got, weight, tail, *shape)
    other = lax.all_to_all(
        other, "expert", split_axis=0, concat_axis=0, tiled=True, axis_index_groups=halves
    )
    near = compute(got, weight, None, *shape)
    near = lax.all_to_all(
        near, "expert", split_axis=0, concat_axis=0, tiled=True, axis_index_groups=halves
    )
    merged_max = jnp.max(other[:, :, ff:], axis=0)
    merged = jnp.sum(other[:, :, :ff].astype(jnp.float32), axis=0).astype(jnp.bfloat16)
    merged = jnp.concatenate([merged, merged_max], axis=1)
    crossed = lax.ppermute(merged, "expert", [(i, (i + half) % n) for i in range(n)])
    combined = jnp.sum(near.astype(jnp.float32), axis=0) + crossed[:, :ff].astype(jnp.float32)
    expert_amax = jnp.maximum(merged_max[rows - 1, :1], crossed[0, ff : ff + 1])
    return (combined.astype(jnp.bfloat16), expert_amax.astype(jnp.float32))


def solution(mesh):
    return jax.shard_map(
        shards,
        mesh=mesh,
        in_specs=(
            P("expert", None),
            P("expert", None),
            P("expert", None),
            P(None, "expert", "tensor"),
        ),
        out_specs=(P("expert", "tensor"), P("expert")),
        check_vma=False,
    )
```

time: 61.4 us -> 56.2 us (0.915)
  blocking collectives: 23.5 us -> 0 us
  starting transfers between devices: 3.63 us -> 16.7 us
  local copies, waits for them, and re-layouts: 0.71 us -> 7.91 us
  matrix products: 7.13 us -> 0 us
  Pallas kernels: 0 us -> 5.82 us
  waiting for transfers between devices: 17.8 us -> 15.7 us
  between operations: 2.54 us -> 3.2 us
    all_to_all x1 -> x0, blocking collectives: 20.9 us -> none  [shards(): lax.all_to_all(send, 'expert', split_axis=0, concat_axis=0, tiled=True)]
    all_to_all x1 -> x3, starting transfers between devices: 3.63 us -> 15.2 us  [the longest x1 8.31 us: shards(): lax.all_to_all(send, 'expert', split_axis=0, concat_axis=0, tiled=True)]
    dot_general x1 -> x0, matrix products: 7.13 us -> none  [shards(): jnp.dot(scaled.reshape(n * rows, experts * depth), learner_weights.reshap...]
    pallas_call x0 -> x2, Pallas kernels: none -> 5.82 us  [partials(): pl.pallas_call(functools.partial(partial_kernel, n=n, rows=rows, depth=de...]
    unnamed x9 -> x5, local copies, waits for them, and re-layouts: 0.27 us -> 5.65 us
    all_to_all x1 -> x3, waiting for transfers between devices: 17.8 us -> 14.6 us  [the longest x1 7.18 us: shards(): lax.all_to_all(send, 'expert', split_axis=0, concat_axis=0, tiled=True)]
    pmax x1 -> x0, blocking collectives: 2.58 us -> none  [shards(): lax.pmax(jnp.max(jnp.abs(learner_weights), axis=(1, 2)).astype(jnp.float3...]
    ppermute x0 -> x2, starting transfers between devices: none -> 1.44 us  [the longest x1 1.38 us: shards(): lax.ppermute(merged, 'expert', [(i, (i + half) % n) for i in range(n)])]
  transfers between devices with their start and end apart: 1 -> 5, of which waited for: 1 -> 4; matrix products, arithmetic and copies ran while one was open for 1% -> 9% of each run, Pallas kernels for 0% -> 5%
where the time goes in v2:
time: 56.2 us; the launch traced here: 55.6 us
  starting transfers between devices  16.7 us (30%)
  waiting for transfers between devices  15.7 us (28%)
  local copies, waits for them, and re-layouts  7.91 us (14%)
  other arithmetic  6.32 us (11%)
  Pallas kernels  5.82 us (10%)
  between operations  3.2 us (6%)
    all_to_all x1, starting transfers between devices, shards(): lax.all_to_all(send, 'expert', split_axis=0, concat_axis=0, tiled=True)  8.31 us
    all_to_all x1, waiting for transfers between devices, shards(): lax.all_to_all(send, 'expert', split_axis=0, concat_axis=0, tiled=True)  7.18 us
    pallas_call x2, Pallas kernels, partials(): pl.pallas_call(functools.partial(partial_kernel, n=n, rows=rows, depth=de...  5.82 us
    all_to_all x1, waiting for transfers between devices, shards(): lax.all_to_all(near, 'expert', split_axis=0, concat_axis=0, tiled=True, a...  5.77 us
    unnamed x5, local copies, waits for them, and re-layouts  5.65 us
    reduce_max x1, other arithmetic, shards(): largest = jnp.max(jnp.abs(learner_weights), axis=(1, 2))  4.03 us
    all_to_all x1, starting transfers between devices, shards(): lax.all_to_all(other, 'expert', split_axis=0, concat_axis=0, tiled=True,...  3.47 us
    all_to_all x1, starting transfers between devices, shards(): lax.all_to_all(near, 'expert', split_axis=0, concat_axis=0, tiled=True, a...  3.45 us
  transfers between devices with their start and end apart: 5, of which 4 were waited for; matrix products, arithmetic and copies ran while one was open for 9% of the time, Pallas kernels for 5%

profile of v2, /device:TPU:0, one launch (start us, length us, event | category | flops | bytes accessed | tf_op | source)
XLA Modules:
  0.0 55.6 jit_solution(5794198765475064670)
XLA Ops:
  0.6 0.7 %select_reduce_fusion = f32[32,16]{0,1:T(8,128)S(1)} fusion(f32[32,8]{0,1:T(8,128)} %param.6, s32[32,8]{0,1:T(8,128)} %param.5), kind=kLoop, calls=%fused_computation.8 | loop fusion | flops 11776 | bytes 4096 | tf_op jit(solution)/shard_map/reduce_sum | solution.py:89
  1.4 0.1 copy.13
  1.5 1.0 %copy.16 = bf16[4,16,8,256]{3,2,0,1:T(8,128)(2,1)S(1)} copy(bf16[4,16,8,256]{3,2,1,0:T(8,128)(2,1)} %bitcast.13) | data formatting | bytes 524288 | tf_op jit(solution)/shard_map/reshape | solution.py:94
  2.5 0.8 %pad_maximum_fusion = bf16[16,32,384]{2,1,0:T(8,128)(2,1)} fusion(bf16[16,32,128]{2,1,0:T(8,128)(2,1)S(1)} %broadcast_in_dim.32, bf16[16,32,256]{2,1,0:T(8,128)(2,1)S(1)} %bitcast.12), kind=kLoop, calls=%fused_computation.3 | loop fusion | flops 786432 | bytes 786432 | tf_op jit(solution)/shard_map/concatenate | solution.py:95
  3.3 8.3 %all-to-all-start = ((bf16[16,32,384]{2,1,0:T(8,128)(2,1)}), bf16[16,32,384]{2,1,0:T(8,128)(2,1)S(1)}, u32[]{:S(2)}, u32[]{:S(2)}) async-start(bf16[16,32,384]{2,1,0:T(8,128)(2,1)} %pad_maximum_fusion), calls=%async_computation | async-start | bytes 786432 | tf_op jit(solution)/shard_map/all_to_all | solution.py:96
  11.6 4.0 %abs_reduce_fusion = bf16[16]{0:T(256)(128)(2,1)S(1)} fusion(bf16[16,256,768]{2,1,0:T(8,128)(2,1)} %param.7), kind=kLoop, calls=%fused_computation | loop fusion | flops 6291440 | bytes 6291488 | tf_op jit(solution)/shard_map/reduce_max | solution.py:97
  15.7 1.1 %collective-permute-done = bf16[16]{0:T(256)(128)(2,1)S(1)} collective-permute-done((bf16[16]{0:T(256)(128)(2,1)S(1)}, bf16[16]{0:T(256)(128)(2,1)S(1)}, u32[]{:S(2)}, u32[]{:S(2)}) %collective-permute-start) | collective-permute-done | bytes 64 | tf_op jit(solution)/shard_map/ppermute | solution.py:99
  16.8 0.1 fusion.1
  16.9 0.1 broadcast_in_dim.34
  17.0 0.1 broadcast_in_dim.33
  17.0 7.2 %all-to-all-done.got_ref = bf16[16,32,384]{2,1,0:T(8,128)(2,1)S(1)} async-done(((bf16[16,32,384]{2,1,0:T(8,128)(2,1)}), bf16[16,32,384]{2,1,0:T(8,128)(2,1)S(1)}, u32[]{:S(2)}, u32[]{:S(2)}) %all-to-all-start) | async-done | bytes 393248 | tf_op jit(solution)/shard_map/all_to_all | solution.py:96
  24.2 2.8 %copy-done = bf16[16,256,768]{2,1,0:T(8,128)(2,1)S(1)} copy-done((bf16[16,256,768]{2,1,0:T(8,128)(2,1)S(1)}, bf16[16,256,768]{2,1,0:T(8,128)(2,1)}, u32[]{:S(2)}) %copy-start) | copy-done | bytes 6291480
  27.0 2.9 %shard_map.60 = bf16[8,32,896]{2,1,0:T(8,128)(2,1)} custom-call(bf16[16,32,384]{2,1,0:T(8,128)(2,1)S(1)} %all-to-all-done.got_ref, bf16[4096,768]{1,0:T(8,128)(2,1)S(1)} %bitcast.10, bf16[8,32,128]{2,1,0:T(8,128)(2,1)S(1)} %pad_maximum_fusion.1.rest_0_), custom_call_target="tpu_custom_call" | custom-call | flops 1610612736 | bytes 6291456 | tf_op jit(solution)/shard_map/pallas_call | solution.py:40
  29.9 3.5 %all-to-all-start.2 = ((bf16[8,32,896]{2,1,0:T(8,128)(2,1)}), bf16[8,32,896]{2,1,0:T(8,128)(2,1)S(1)}, u32[]{:S(2)}, u32[]{:S(2)}) async-start(bf16[8,32,896]{2,1,0:T(8,128)(2,1)} %shard_map.60), calls=%async_computation.2 | async-start | bytes 917504 | tf_op jit(solution)/shard_map/all_to_all | solution.py:115
  33.4 2.8 %copy-done.1 = bf16[16,256,768]{2,1,0:T(8,128)(2,1)S(1)} copy-done((bf16[16,256,768]{2,1,0:T(8,128)(2,1)S(1)}, bf16[16,256,768]{2,1,0:T(8,128)(2,1)}, u32[]{:S(2)}) %copy-start.1) | copy-done | bytes 6291480
  36.2 2.9 %shard_map.59 = bf16[8,32,768]{2,1,0:T(8,128)(2,1)} custom-call(bf16[16,32,384]{2,1,0:T(8,128)(2,1)S(1)} %all-to-all-done.got_ref, bf16[4096,768]{1,0:T(8,128)(2,1)S(1)} %bitcast.11), custom_call_target="tpu_custom_call" | custom-call | flops 1610612736 | bytes 6291456 | tf_op jit(solution)/shard_map/pallas_call | solution.py:40
  39.1 1.7 %all-to-all-done.2 = bf16[8,32,896]{2,1,0:T(8,128)(2,1)S(1)} async-done(((bf16[8,32,896]{2,1,0:T(8,128)(2,1)}), bf16[8,32,896]{2,1,0:T(8,128)(2,1)S(1)}, u32[]{:S(2)}, u32[]{:S(2)}) %all-to-all-start.2) | async-done | bytes 458784 | tf_op jit(solution)/shard_map/all_to_all | solution.py:115
  40.8 3.5 %all-to-all-start.1 = ((bf16[8,32,768]{2,1,0:T(8,128)(2,1)}), bf16[8,32,768]{2,1,0:T(8,128)(2,1)S(1)}, u32[]{:S(2)}, u32[]{:S(2)}) async-start(bf16[8,32,768]{2,1,0:T(8,128)(2,1)} %shard_map.59), calls=%async_computation.1 | async-start | bytes 786432 | tf_op jit(solution)/shard_map/all_to_all | solution.py:119
  44.2 0.1 slice_reduce_fusion
  44.3 1.4 %collective-permute-start.1 = (bf16[32,896]{1,0:T(8,128)(2,1)S(1)}, bf16[32,896]{1,0:T(8,128)(2,1)S(1)}, u32[]{:S(2)}, u32[]{:S(2)}) collective-permute-start(bf16[32,896]{1,0:T(8,128)(2,1)S(1)} %pad_maximum_fusion.2), channel_id=1, source_target_pairs={{0,16},{2,18},{4,20},{6,22},{8,24},{10,26},{12,28},{14,30},{16,0},... | collective-permute-start | bytes 172040 | tf_op jit(solution)/shard_map/ppermute | solution.py:125
  45.7 5.8 %all-to-all-done.1 = bf16[8,32,768]{2,1,0:T(8,128)(2,1)S(1)} async-done(((bf16[8,32,768]{2,1,0:T(8,128)(2,1)}), bf16[8,32,768]{2,1,0:T(8,128)(2,1)S(1)}, u32[]{:S(2)}, u32[]{:S(2)}) %all-to-all-start.1) | async-done | bytes 393248 | tf_op jit(solution)/shard_map/all_to_all | solution.py:119
  51.5 0.5 slice.23
  52.1 0.5 slice.24
  53.9 0.6 %add_convert_fusion = bf16[32,768]{1,0:T(8,128)(2,1)} fusion(f32[32,768]{1,0:T(8,128)S(1)} %convert_reduce_fusion, bf16[32,896]{1,0:T(8,128)(2,1)S(1)} %collective-permute-done.1), kind=kLoop, calls=%fused_computation.5 | loop fusion | flops 73728 | bytes 196608 | tf_op jit(solution)/shard_map/convert_element_type | solution.py:128
  (13 shorter events, 0.2 us)
Async XLA Ops:
  3.3 21.0 %all-to-all-start = ((bf16[16,32,384]{2,1,0:T(8,128)(2,1)}), bf16[16,32,384]{2,1,0:T(8,128)(2,1)S(1)}, u32[]{:S(2)}, u32[]{:S(2)}) async-start(bf16[16,32,384]{2,1,0:T(8,128)(2,1)} %pad_maximum_fusion), calls=%async_computation | async-start | bytes 786432 | tf_op jit(solution)/shard_map/all_to_all | solution.py:96
  15.6 1.2 %collective-permute-start = (bf16[16]{0:T(256)(128)(2,1)S(1)}, bf16[16]{0:T(256)(128)(2,1)S(1)}, u32[]{:S(2)}, u32[]{:S(2)}) collective-permute-start(bf16[16]{0:T(256)(128)(2,1)S(1)} %abs_reduce_fusion), channel_id=1, source_target_pairs={{0,1},{1,0},{2,3},{3,2},{4,5},{5,4},{6,7},{7,6},{8,9},{9,8},{10,11... | collective-permute-start | bytes 104 | tf_op jit(solution)/shard_map/ppermute | solution.py:99
  24.2 2.8 %copy-start = (bf16[16,256,768]{2,1,0:T(8,128)(2,1)S(1)}, bf16[16,256,768]{2,1,0:T(8,128)(2,1)}, u32[]{:S(2)}) copy-start(bf16[16,256,768]{2,1,0:T(8,128)(2,1)} %param.7) | copy-start | bytes 18874372
  29.9 10.8 %all-to-all-start.2 = ((bf16[8,32,896]{2,1,0:T(8,128)(2,1)}), bf16[8,32,896]{2,1,0:T(8,128)(2,1)S(1)}, u32[]{:S(2)}, u32[]{:S(2)}) async-start(bf16[8,32,896]{2,1,0:T(8,128)(2,1)} %shard_map.60), calls=%async_computation.2 | async-start | bytes 917504 | tf_op jit(solution)/shard_map/all_to_all | solution.py:115
  33.4 2.8 %copy-start.1 = (bf16[16,256,768]{2,1,0:T(8,128)(2,1)S(1)}, bf16[16,256,768]{2,1,0:T(8,128)(2,1)}, u32[]{:S(2)}) copy-start(bf16[16,256,768]{2,1,0:T(8,128)(2,1)} %param.7) | copy-start | bytes 18874372
  40.8 10.7 %all-to-all-start.1 = ((bf16[8,32,768]{2,1,0:T(8,128)(2,1)}), bf16[8,32,768]{2,1,0:T(8,128)(2,1)S(1)}, u32[]{:S(2)}, u32[]{:S(2)}) async-start(bf16[8,32,768]{2,1,0:T(8,128)(2,1)} %shard_map.59), calls=%async_computation.1 | async-start | bytes 786432 | tf_op jit(solution)/shard_map/all_to_all | solution.py:119
  44.3 7.7 %collective-permute-start.1 = (bf16[32,896]{1,0:T(8,128)(2,1)S(1)}, bf16[32,896]{1,0:T(8,128)(2,1)S(1)}, u32[]{:S(2)}, u32[]{:S(2)}) collective-permute-start(bf16[32,896]{1,0:T(8,128)(2,1)S(1)} %pad_maximum_fusion.2), channel_id=1, source_target_pairs={{0,16},{2,18},{4,20},{6,22},{8,24},{10,26},{12,28},{14,30},{16,0},... | collective-permute-start | bytes 172040 | tf_op jit(solution)/shard_map/ppermute | solution.py:125

commit v3 on v1

v3 whole, which is shorter than its diff:
```python
import functools

import jax
import jax.numpy as jnp
from jax import lax
from jax.experimental import pallas as pl
from jax.experimental.pallas import tpu as pltpu
from jax.sharding import PartitionSpec as P

LANES = 128
SUBLANES = 8
VMEM = pl.BlockSpec(memory_space=pltpu.VMEM)
HBM = pl.BlockSpec(memory_space=pltpu.HBM)
TILE = 256


def params(mebibytes):
    return pltpu.CompilerParams(vmem_limit_bytes=mebibytes << 20)


def pack_kernel(tokens_ref, routes_ref, weights_ref, send_ref, routes_buf, weights_buf, sem):
    n, _, depth = send_ref.shape
    choices, rows = routes_ref.shape
    copies = [
        pltpu.make_async_copy(routes_ref, routes_buf, sem.at[n]),
        pltpu.make_async_copy(weights_ref, weights_buf, sem.at[n + 1]),
    ]
    copies += [
        pltpu.make_async_copy(
            tokens_ref.at[:, pl.ds(i * depth, depth)], send_ref.at[i, pl.ds(0, rows)], sem.at[i]
        )
        for i in range(n)
    ]
    for copy in copies:
        copy.start()
    for copy in copies[:2]:
        copy.wait()
    expert = lax.broadcasted_iota(jnp.int32, (n, rows), 0)
    gate = jnp.zeros((n, rows), jnp.float32)
    for k in range(choices):
        chosen = routes_buf[k : k + 1, :] == expert
        gate += jnp.where(chosen, weights_buf[k : k + 1, :], 0.0)
    gate = gate.T
    high = gate.astype(jnp.bfloat16).astype(jnp.float32)
    low = gate - high
    terms = []
    for r in range(0, rows, SUBLANES):
        terms += [high[r : r + SUBLANES], low[r : r + SUBLANES]]
    spare = depth - len(terms) * n
    if spare:
        terms.append(jnp.zeros((SUBLANES, spare), jnp.float32))
    packed = jnp.concatenate(terms, axis=1).astype(jnp.bfloat16)
    for i in range(n):
        send_ref[i, rows:, :] = packed
    for copy in copies[2:]:
        copy.wait()


def pack(tokens, routes, route_weights, n, depth):
    rows, choices = routes.shape
    return pl.pallas_call(
        pack_kernel,
        out_shape=jax.ShapeDtypeStruct((n, rows + SUBLANES, depth), jnp.bfloat16),
        in_specs=[HBM] * 3,
        out_specs=VMEM,
        scratch_shapes=[
            pltpu.VMEM((choices, rows), jnp.int32),
            pltpu.VMEM((choices, rows), jnp.float32),
            pltpu.SemaphoreType.DMA((n + 2,)),
        ],
        compiler_params=params(60),
    )(tokens, routes.T, route_weights.T)


def largest_kernel(weight_ref, held_ref, largest_ref, rest_ref, sem):
    experts = weight_ref.shape[0]
    kept = held_ref.shape[0]
    places = [held_ref.at[e] if e < kept else rest_ref.at[e - kept] for e in range(experts)]
    copies = [
        pltpu.make_async_copy(weight_ref.at[e], place, sem.at[e]) for e, place in enumerate(places)
    ]
    for copy in copies:
        copy.start()
    for e, copy in enumerate(copies):
        copy.wait()
        block = jnp.abs(places[e][...].astype(jnp.float32))
        row = jnp.max(block, axis=0, keepdims=True)
        top = jnp.max(row, axis=1, keepdims=True)
        largest_ref[e : e + 1, :] = jnp.broadcast_to(top, (1, LANES))


def hold(weights):
    experts, depth, ff = weights.shape
    kept = experts // 2
    return pl.pallas_call(
        largest_kernel,
        out_shape=(
            pltpu.VMEM((kept, depth, ff), weights.dtype),
            jax.ShapeDtypeStruct((experts, LANES), jnp.float32),
        ),
        in_specs=[HBM],
        out_specs=(VMEM, VMEM),
        scratch_shapes=[
            pltpu.VMEM((experts - kept, depth, ff), weights.dtype),
            pltpu.SemaphoreType.DMA((experts,)),
        ],
        compiler_params=params(12),
        cost_estimate=pl.CostEstimate(
            flops=2 * weights.size, bytes_accessed=2 * weights.size, transcendentals=0
        ),
    )(pltpu.with_memory_space_constraint(weights, pltpu.HBM))


def partial_kernel(got_ref, weight_ref, *rest, rows, experts, other):
    if other:
        held_ref, tail_ref, out_ref, scaled_ref, total_ref, rest_ref, sem = rest
        parts = [held_ref, rest_ref.at[0]]
    else:
        out_ref, scaled_ref, total_ref, rest_ref, sem = rest
        parts = [rest_ref.at[0], rest_ref.at[1]]
    n, _, depth = got_ref.shape
    half, ff = n // 2, weight_ref.shape[1]
    mine = (lax.axis_index("expert") >= half).astype(jnp.int32) * half
    theirs = half - mine
    first = theirs if other else mine
    deep = experts // 2 * depth
    copies = [
        None
        if other and i == 0
        else pltpu.make_async_copy(weight_ref.at[pl.ds(i * deep, deep)], part, sem.at[i])
        for i, part in enumerate(parts)
    ]
    for copy in copies:
        if copy is not None:
            copy.start()
    step = max(1, 64 // rows)
    for r in range(0, half, step):
        count = step * rows
        block = got_ref[pl.ds(first + r, step)]
        x = block[:, :rows].reshape(count, depth).astype(jnp.float32)
        packed = block[:, rows:].astype(jnp.float32)
        gates = jnp.concatenate(
            [
                packed[:, :, at : at + experts] + packed[:, :, at + experts : at + 2 * experts]
                for at in range(0, rows // SUBLANES * 2 * experts, 2 * experts)
            ],
            axis=1,
        ).reshape(count, experts)
        for e in range(experts):
            scaled_ref[r * rows : r * rows + count, e * depth : (e + 1) * depth] = (
                x * gates[:, e : e + 1]
            ).astype(jnp.bfloat16)
    for i, (part, copy) in enumerate(zip(parts, copies)):
        if copy is not None:
            copy.wait()
        for at in range(0, ff, TILE):
            product = jnp.dot(
                scaled_ref[:, i * deep : (i + 1) * deep],
                part[:, at : at + TILE],
                preferred_element_type=jnp.float32,
            )
            if i == 0:
                total_ref[:, at : at + TILE] = product
            else:
                product += total_ref[:, at : at + TILE]
                out_ref[:, :, at : at + TILE] = product.astype(jnp.bfloat16).reshape(
                    half, rows, TILE
                )
    if other:
        for r in range(half):
            for at, owner in ((0, theirs + r), (rows // 2, mine + r)):
                out_ref[r, at : at + rows // 2, ff:] = jnp.broadcast_to(
                    tail_ref[pl.ds(owner, 1), :], (rows // 2, LANES)
                ).astype(jnp.bfloat16)


def partials(got, weight, held, tail, rows, experts):
    n, _, depth = got.shape
    half, ff = n // 2, weight.shape[1]
    deep = experts // 2 * depth
    other = held is not None
    operands = (got, pltpu.with_memory_space_constraint(weight, pltpu.HBM))
    if other:
        held = pltpu.with_memory_space_constraint(held.reshape(deep, ff), pltpu.VMEM)
        operands += (held, tail)
    return pl.pallas_call(
        functools.partial(partial_kernel, rows=rows, experts=experts, other=other),
        out_shape=jax.ShapeDtypeStruct((half, rows, ff + LANES * other), jnp.bfloat16),
        in_specs=[VMEM, HBM, VMEM, VMEM][: len(operands)],
        out_specs=VMEM,
        scratch_shapes=[
            pltpu.VMEM((half * rows, experts * depth), jnp.bfloat16),
            pltpu.VMEM((half * rows, ff), jnp.float32),
            pltpu.VMEM((1 if other else 2, deep, ff), weight.dtype),
            pltpu.SemaphoreType.DMA((2,)),
        ],
        compiler_params=params(24),
        cost_estimate=pl.CostEstimate(
            flops=2 * half * rows * experts * depth * ff,
            bytes_accessed=2 * weight.size,
            transcendentals=0,
        ),
    )(*operands)


def finish_kernel(near_ref, merged_ref, crossed_ref, out_ref, largest_ref):
    rows, ff = out_ref.shape
    total = crossed_ref[:, :ff].astype(jnp.float32)
    for i in range(near_ref.shape[0]):
        total += near_ref[i].astype(jnp.float32)
    out_ref[...] = total.astype(jnp.bfloat16)
    own = merged_ref[rows // 2 :, ff:].astype(jnp.float32)
    theirs = crossed_ref[: rows // 2, ff:].astype(jnp.float32)
    largest_ref[0] = jnp.max(jnp.maximum(own, theirs))


def finish(near, merged, crossed):
    _, rows, ff = near.shape
    return pl.pallas_call(
        finish_kernel,
        out_shape=(
            jax.ShapeDtypeStruct((rows, ff), jnp.bfloat16),
            jax.ShapeDtypeStruct((1,), jnp.float32),
        ),
        in_specs=[VMEM] * 3,
        out_specs=(VMEM, pl.BlockSpec(memory_space=pltpu.SMEM)),
        compiler_params=params(8),
    )(near, merged, crossed)


def halves_of(n):
    return [list(range(n // 2)), list(range(n // 2, n))]


def exchange(block, groups=None):
    return lax.all_to_all(
        block, "expert", split_axis=0, concat_axis=0, tiled=True, axis_index_groups=groups
    )


def over_tensor(largest):
    if lax.axis_size("tensor") == 2:
        return jnp.maximum(largest, lax.ppermute(largest, "tensor", [(0, 1), (1, 0)]))
    return lax.pmax(largest, "tensor")


def kernels(tokens, routes, route_weights, learner_weights):
    n = lax.axis_size("expert")
    rows = tokens.shape[0]
    experts, depth, ff = learner_weights.shape
    got = exchange(pack(tokens, routes, route_weights, n, depth))
    held, largest = hold(learner_weights)
    largest = over_tensor(largest)
    weight = learner_weights.reshape(experts * depth, ff)
    other = exchange(partials(got, weight, held, largest, rows, experts), halves_of(n))
    near = exchange(partials(got, weight, None, None, rows, experts), halves_of(n))
    merged_max = jnp.max(other[:, :, ff:], axis=0)
    merged = jnp.sum(other[:, :, :ff].astype(jnp.float32), axis=0).astype(jnp.bfloat16)
    merged = jnp.concatenate([merged, merged_max], axis=1)
    crossed = lax.ppermute(merged, "expert", [(i, (i + n // 2) % n) for i in range(n)])
    return finish(near, merged, crossed)


def plain(tokens, routes, route_weights, learner_weights):
    n = lax.axis_size("expert")
    rows = tokens.shape[0]
    experts, depth, ff = learner_weights.shape
    largest = over_tensor(jnp.max(jnp.abs(learner_weights), axis=(1, 2)))
    chosen = routes[:, :, None] == jnp.arange(experts, dtype=jnp.int32)
    gate = jnp.sum(jnp.where(chosen, route_weights[:, :, None], 0.0), axis=1)
    high = lax.reduce_precision(gate, 8, 7)
    terms = jnp.concatenate([high, gate - high], axis=1).astype(jnp.bfloat16)
    columns = tokens.reshape(rows, n, depth).transpose(1, 0, 2)
    top = jnp.broadcast_to(largest[:, None, None], (n, rows, 1))
    got = exchange(
        jnp.concatenate([columns, jnp.broadcast_to(terms, (n, *terms.shape)), top], axis=2)
    )
    weight = learner_weights.reshape(experts * depth, ff)

    def one(block):
        block = block.astype(jnp.float32)
        gates = block[:, depth : depth + experts] + block[:, depth + experts : depth + 2 * experts]
        scaled = (block[:, None, :depth] * gates[:, :, None]).astype(jnp.bfloat16)
        product = jnp.dot(
            scaled.reshape(rows, experts * depth), weight, preferred_element_type=jnp.float32
        )
        return product.astype(jnp.bfloat16)

    back = exchange(lax.map(one, got))
    combined = jnp.sum(back.astype(jnp.float32), axis=0).astype(jnp.bfloat16)
    expert_amax = jnp.max(got[:, 0, depth + 2 * experts]).astype(jnp.float32).reshape(1)
    return (combined, expert_amax)


def shards(tokens, routes, route_weights, learner_weights):
    n, rows = lax.axis_size("expert"), tokens.shape[0]
    experts, depth, ff = learner_weights.shape
    aligned = depth % LANES == 0 and ff % TILE == 0 and rows % 32 == 0 and n % 2 == 0
    fits = rows // SUBLANES * 2 * experts <= depth
    small = experts * depth * ff <= 4 << 20 and n * rows <= 1024
    form = kernels if aligned and fits and small and experts == n else plain
    return form(tokens, routes, route_weights, learner_weights)


def solution(mesh):
    return jax.shard_map(
        shards,
        mesh=mesh,
        in_specs=(
            P("expert", None),
            P("expert", None),
            P("expert", None),
            P(None, "expert", "tensor"),
        ),
        out_specs=(P("expert", "tensor"), P("expert")),
        check_vma=False,
    )
```

time: 61.4 us -> 49.1 us (0.80)
  blocking collectives: 23.5 us -> 0 us
  Pallas kernels: 0 us -> 14.2 us
  starting transfers between devices: 3.63 us -> 16.7 us
  matrix products: 7.13 us -> 0 us
  other arithmetic: 5.73 us -> 0.08 us
  between operations: 2.54 us -> 0.73 us
  waiting for transfers between devices: 17.8 us -> 16.1 us
    all_to_all x1 -> x0, blocking collectives: 20.9 us -> none  [shards(): lax.all_to_all(send, 'expert', split_axis=0, concat_axis=0, tiled=True)]
    pallas_call x0 -> x5, Pallas kernels: none -> 14.2 us  [the longest x2 8.51 us: partials(): pl.pallas_call(functools.partial(partial_kernel, rows=rows, experts=exper...]
    all_to_all x1 -> x3, starting transfers between devices: 3.63 us -> 15.2 us  [exchange(): lax.all_to_all(block, 'expert', split_axis=0, concat_axis=0, tiled=True,...]
    dot_general x1 -> x0, matrix products: 7.13 us -> none  [shards(): jnp.dot(scaled.reshape(n * rows, experts * depth), learner_weights.reshap...]
    reduce_max x2 -> x1, other arithmetic: 4.76 us -> 0.01 us  [kernels(): merged_max = jnp.max(other[:, :, ff:], axis=0)]
    all_to_all x1 -> x3, waiting for transfers between devices: 17.8 us -> 15 us  [exchange(): lax.all_to_all(block, 'expert', split_axis=0, concat_axis=0, tiled=True,...]
    pmax x1 -> x0, blocking collectives: 2.58 us -> none  [shards(): lax.pmax(jnp.max(jnp.abs(learner_weights), axis=(1, 2)).astype(jnp.float3...]
    ppermute x0 -> x2, starting transfers between devices: none -> 1.47 us  [the longest x1 1.39 us: kernels(): lax.ppermute(merged, 'expert', [(i, (i + n // 2) % n) for i in range(n)])]
  transfers between devices with their start and end apart: 1 -> 5, of which waited for: 1 -> 4; matrix products, arithmetic and copies ran while one was open for 1% -> 0% of each run, Pallas kernels for 0% -> 17%
where the time goes in v3:
time: 49.1 us; the launch traced here: 48.6 us
  starting transfers between devices  16.7 us (34%)
  waiting for transfers between devices  16.1 us (33%)
  Pallas kernels  14.2 us (29%)
  local copies, waits for them, and re-layouts  0.76 us (2%)
  between operations  0.73 us (1%)
    all_to_all x3, starting transfers between devices, exchange(): lax.all_to_all(block, 'expert', split_axis=0, concat_axis=0, tiled=True,...  15.2 us
    all_to_all x3, waiting for transfers between devices, exchange(): lax.all_to_all(block, 'expert', split_axis=0, concat_axis=0, tiled=True,...  15 us
    pallas_call x2, Pallas kernels, partials(): pl.pallas_call(functools.partial(partial_kernel, rows=rows, experts=exper...  8.51 us
    pallas_call x1, Pallas kernels, hold(): pl.pallas_call(largest_kernel, out_shape=(pltpu.VMEM((kept, depth, ff), w...  3.17 us
    pallas_call x1, Pallas kernels, pack(): pl.pallas_call(pack_kernel, out_shape=jax.ShapeDtypeStruct((n, rows + SUB...  1.78 us
    ppermute x1, starting transfers between devices, kernels(): lax.ppermute(merged, 'expert', [(i, (i + n // 2) % n) for i in range(n)])  1.39 us
    ppermute x1, waiting for transfers between devices, over_tensor(): lax.ppermute(largest, 'tensor', [(0, 1), (1, 0)])  1.16 us
  transfers between devices with their start and end apart: 5, of which 4 were waited for; matrix products, arithmetic and copies ran while one was open for 0% of the time, Pallas kernels for 17%

profile of v3, /device:TPU:0, one launch (start us, length us, event | category | flops | bytes accessed | tf_op | source)
XLA Modules:
  0.0 48.6 jit_solution(1263307468138705060)
XLA Ops:
  0.6 1.8 %shard_map.59 = bf16[16,40,256]{2,1,0:T(8,128)(2,1)} custom-call(bf16[32,4096]{1,0:T(8,128)(2,1)} %tokens_ref.1, s32[8,32]{1,0:T(8,128)} %bitcast.7, f32[8,32]{1,0:T(8,128)} %bitcast.8), custom_call_target="tpu_custom_call" | custom-call | tf_op jit(solution)/shard_map/pallas_call | solution.py:61
  2.4 8.3 %all-to-all-start = ((bf16[16,40,256]{2,1,0:T(8,128)(2,1)}), bf16[16,40,256]{2,1,0:T(8,128)(2,1)S(1)}, u32[]{:S(2)}, u32[]{:S(2)}) async-start(bf16[16,40,256]{2,1,0:T(8,128)(2,1)} %shard_map.59), calls=%async_computation | async-start | bytes 655360 | tf_op jit(solution)/shard_map/all_to_all | solution.py:236
  10.7 3.2 %shard_map.61 = (bf16[8,256,768]{2,1,0:T(8,128)(2,1)S(1)}, f32[16,128]{1,0:T(8,128)S(1)}) custom-call(bf16[16,256,768]{2,1,0:T(8,128)(2,1)} %weight_ref.1), custom_call_target="tpu_custom_call" | custom-call | flops 6291456 | bytes 6291456 | tf_op jit(solution)/shard_map/pallas_call | solution.py:95
  13.9 0.1 collective-permute-start
  14.0 1.2 %collective-permute-done = f32[16,128]{1,0:T(8,128)S(1)} collective-permute-done((f32[16,128]{1,0:T(8,128)S(1)}, f32[16,128]{1,0:T(8,128)S(1)}, u32[]{:S(2)}, u32[]{:S(2)}) %collective-permute-start) | collective-permute-done | bytes 8224 | tf_op jit(solution)/shard_map/ppermute | solution.py:243
  15.2 6.9 %all-to-all-done.got_ref = bf16[16,40,256]{2,1,0:T(8,128)(2,1)S(1)} async-done(((bf16[16,40,256]{2,1,0:T(8,128)(2,1)}), bf16[16,40,256]{2,1,0:T(8,128)(2,1)S(1)}, u32[]{:S(2)}, u32[]{:S(2)}) %all-to-all-start) | async-done | bytes 327712 | tf_op jit(solution)/shard_map/all_to_all | solution.py:236
  22.1 3.5 %shard_map.62 = bf16[8,32,896]{2,1,0:T(8,128)(2,1)S(1)} custom-call(bf16[16,40,256]{2,1,0:T(8,128)(2,1)S(1)} %all-to-all-done.got_ref, bf16[4096,768]{1,0:T(8,128)(2,1)} %bitcast.5, bf16[2048,768]{1,0:T(8,128)(2,1)S(1)} %bitcast.4, f32[16,128]{1,0:T(8,128)S(1)} %max.3.rest_1_), custom_call_target="tpu_custom_call" | custom-call | flops 1610612736 | bytes 6291456 | tf_op jit(solution)/shard_map/pallas_call | solution.py:186
  25.6 0.0 copy-start
  25.6 0.8 %copy-done = bf16[8,32,896]{2,1,0:T(8,128)(2,1)} copy-done((bf16[8,32,896]{2,1,0:T(8,128)(2,1)}, bf16[8,32,896]{2,1,0:T(8,128)(2,1)S(1)}, u32[]{:S(2)}) %copy-start) | copy-done | bytes 458776
  26.3 3.5 %all-to-all-start.2 = ((bf16[8,32,896]{2,1,0:T(8,128)(2,1)}), bf16[8,32,896]{2,1,0:T(8,128)(2,1)S(1)}, u32[]{:S(2)}, u32[]{:S(2)}) async-start(bf16[8,32,896]{2,1,0:T(8,128)(2,1)} %copy-done), calls=%async_computation.2 | async-start | bytes 917504 | tf_op jit(solution)/shard_map/all_to_all | solution.py:236
  29.8 5.0 %shard_map.60 = bf16[8,32,768]{2,1,0:T(8,128)(2,1)} custom-call(bf16[16,40,256]{2,1,0:T(8,128)(2,1)S(1)} %all-to-all-done.got_ref, bf16[4096,768]{1,0:T(8,128)(2,1)} %bitcast.6), custom_call_target="tpu_custom_call" | custom-call | flops 1610612736 | bytes 6291456 | tf_op jit(solution)/shard_map/pallas_call | solution.py:186
  34.8 2.3 %all-to-all-done.2 = bf16[8,32,896]{2,1,0:T(8,128)(2,1)S(1)} async-done(((bf16[8,32,896]{2,1,0:T(8,128)(2,1)}), bf16[8,32,896]{2,1,0:T(8,128)(2,1)S(1)}, u32[]{:S(2)}, u32[]{:S(2)}) %all-to-all-start.2) | async-done | bytes 458784 | tf_op jit(solution)/shard_map/all_to_all | solution.py:236
  37.1 3.5 %all-to-all-start.1 = ((bf16[8,32,768]{2,1,0:T(8,128)(2,1)}), bf16[8,32,768]{2,1,0:T(8,128)(2,1)S(1)}, u32[]{:S(2)}, u32[]{:S(2)}) async-start(bf16[8,32,768]{2,1,0:T(8,128)(2,1)} %shard_map.60), calls=%async_computation.1 | async-start | bytes 786432 | tf_op jit(solution)/shard_map/all_to_all | solution.py:236
  40.6 0.1 slice_reduce_fusion
  40.7 1.4 %collective-permute-start.1 = (bf16[32,896]{1,0:T(8,128)(2,1)S(1)}, bf16[32,896]{1,0:T(8,128)(2,1)S(1)}, u32[]{:S(2)}, u32[]{:S(2)}) collective-permute-start(bf16[32,896]{1,0:T(8,128)(2,1)S(1)} %pad_maximum_fusion.merged_ref), channel_id=1, source_target_pairs={{0,16},{2,18},{4,20},{6,22},{8,24},{10,26},{12,28},{14,30},{16,0},... | collective-permute-start | bytes 172040 | tf_op jit(solution)/shard_map/ppermute | solution.py:260
  42.1 5.8 %all-to-all-done.1.near_ref = bf16[8,32,768]{2,1,0:T(8,128)(2,1)S(1)} async-done(((bf16[8,32,768]{2,1,0:T(8,128)(2,1)}), bf16[8,32,768]{2,1,0:T(8,128)(2,1)S(1)}, u32[]{:S(2)}, u32[]{:S(2)}) %all-to-all-start.1) | async-done | bytes 393248 | tf_op jit(solution)/shard_map/all_to_all | solution.py:236
  47.9 0.0 collective-permute-done.1.crossed_ref
  47.9 0.7 %shard_map.63 = (bf16[32,768]{1,0:T(8,128)(2,1)}, f32[1]{0:T(128)}) custom-call(bf16[8,32,768]{2,1,0:T(8,128)(2,1)S(1)} %all-to-all-done.1.near_ref, bf16[32,896]{1,0:T(8,128)(2,1)S(1)} %pad_maximum_fusion.merged_ref, bf16[32,896]{1,0:T(8,128)(2,1)S(1)} %collective-permute-done.1.crossed_ref), custom_call_target="tpu_custom_call" | custom-call | tf_op jit(solution)/shard_map/pallas_call | solution.py:219
  (3 shorter events, 0.0 us)
Async XLA Ops:
  2.4 19.6 %all-to-all-start = ((bf16[16,40,256]{2,1,0:T(8,128)(2,1)}), bf16[16,40,256]{2,1,0:T(8,128)(2,1)S(1)}, u32[]{:S(2)}, u32[]{:S(2)}) async-start(bf16[16,40,256]{2,1,0:T(8,128)(2,1)} %shard_map.59), calls=%async_computation | async-start | bytes 655360 | tf_op jit(solution)/shard_map/all_to_all | solution.py:236
  13.9 1.2 %collective-permute-start = (f32[16,128]{1,0:T(8,128)S(1)}, f32[16,128]{1,0:T(8,128)S(1)}, u32[]{:S(2)}, u32[]{:S(2)}) collective-permute-start(f32[16,128]{1,0:T(8,128)S(1)} %get-tuple-element.5), channel_id=1, source_target_pairs={{0,1},{1,0},{2,3},{3,2},{4,5},{5,4},{6,7},{7,6},{8,9},{9,8},{10,11... | collective-permute-start | bytes 24584 | tf_op jit(solution)/shard_map/ppermute | solution.py:243
  25.6 0.8 %copy-start = (bf16[8,32,896]{2,1,0:T(8,128)(2,1)}, bf16[8,32,896]{2,1,0:T(8,128)(2,1)S(1)}, u32[]{:S(2)}) copy-start(bf16[8,32,896]{2,1,0:T(8,128)(2,1)S(1)} %shard_map.62) | copy-start | bytes 1376260
  26.3 10.8 %all-to-all-start.2 = ((bf16[8,32,896]{2,1,0:T(8,128)(2,1)}), bf16[8,32,896]{2,1,0:T(8,128)(2,1)S(1)}, u32[]{:S(2)}, u32[]{:S(2)}) async-start(bf16[8,32,896]{2,1,0:T(8,128)(2,1)} %copy-done), calls=%async_computation.2 | async-start | bytes 917504 | tf_op jit(solution)/shard_map/all_to_all | solution.py:236
  37.1 10.7 %all-to-all-start.1 = ((bf16[8,32,768]{2,1,0:T(8,128)(2,1)}), bf16[8,32,768]{2,1,0:T(8,128)(2,1)S(1)}, u32[]{:S(2)}, u32[]{:S(2)}) async-start(bf16[8,32,768]{2,1,0:T(8,128)(2,1)} %shard_map.60), calls=%async_computation.1 | async-start | bytes 786432 | tf_op jit(solution)/shard_map/all_to_all | solution.py:236
  40.7 7.2 %collective-permute-start.1 = (bf16[32,896]{1,0:T(8,128)(2,1)S(1)}, bf16[32,896]{1,0:T(8,128)(2,1)S(1)}, u32[]{:S(2)}, u32[]{:S(2)}) collective-permute-start(bf16[32,896]{1,0:T(8,128)(2,1)S(1)} %pad_maximum_fusion.merged_ref), channel_id=1, source_target_pairs={{0,16},{2,18},{4,20},{6,22},{8,24},{10,26},{12,28},{14,30},{16,0},... | collective-permute-start | bytes 172040 | tf_op jit(solution)/shard_map/ppermute | solution.py:260

commit v4 on v3

--- a/solution.py
+++ b/solution.py
@@ -18,16 +18,21 @@
     return pltpu.CompilerParams(vmem_limit_bytes=mebibytes << 20)
 
 
-def pack_kernel(tokens_ref, routes_ref, weights_ref, send_ref, routes_buf, weights_buf, sem):
-    n, _, depth = send_ref.shape
+def pack_kernel(
+    tokens_ref, routes_ref, weights_ref, send_ref, block_ref, routes_buf, weights_buf, sem, out_sem
+):
+    n, _, width = block_ref.shape
     choices, rows = routes_ref.shape
+    core = lax.axis_index("tensor")
     copies = [
         pltpu.make_async_copy(routes_ref, routes_buf, sem.at[n]),
         pltpu.make_async_copy(weights_ref, weights_buf, sem.at[n + 1]),
     ]
     copies += [
         pltpu.make_async_copy(
-            tokens_ref.at[:, pl.ds(i * depth, depth)], send_ref.at[i, pl.ds(0, rows)], sem.at[i]
+            tokens_ref.at[:, pl.ds(pl.multiple_of((2 * (n - 1 - i) + core) * width, LANES), width)],
+            block_ref.at[i, pl.ds(0, rows)],
+            sem.at[i],
         )
         for i in range(n)
     ]
@@ -46,30 +51,42 @@
     terms = []
     for r in range(0, rows, SUBLANES):
         terms += [high[r : r + SUBLANES], low[r : r + SUBLANES]]
-    spare = depth - len(terms) * n
+    spare = width - len(terms) * n
     if spare:
         terms.append(jnp.zeros((SUBLANES, spare), jnp.float32))
     packed = jnp.concatenate(terms, axis=1).astype(jnp.bfloat16)
     for i in range(n):
-        send_ref[i, rows:, :] = packed
-    for copy in copies[2:]:
-        copy.wait()
-
-
-def pack(tokens, routes, route_weights, n, depth):
+        block_ref[i, rows:, :] = packed
+    group = n // 4
+    outs = []
+    for i in range(4):
+        part = pl.ds(i * group, group)
+        for copy in copies[2 + i * group : 2 + (i + 1) * group]:
+            copy.wait()
+        outs.append(pltpu.make_async_copy(block_ref.at[part], send_ref.at[part], out_sem.at[i]))
+        outs[-1].start()
+    for out in outs:
+        out.wait()
+
+
+def pack(tokens, routes, route_weights, n, width):
     rows, choices = routes.shape
+    shape = (n, rows + SUBLANES, width)
+    operands = (tokens, routes.T, route_weights.T)
     return pl.pallas_call(
         pack_kernel,
-        out_shape=jax.ShapeDtypeStruct((n, rows + SUBLANES, depth), jnp.bfloat16),
+        out_shape=pltpu.HBM(shape, jnp.bfloat16),
         in_specs=[HBM] * 3,
-        out_specs=VMEM,
+        out_specs=HBM,
         scratch_shapes=[
+            pltpu.VMEM(shape, jnp.bfloat16),
             pltpu.VMEM((choices, rows), jnp.int32),
             pltpu.VMEM((choices, rows), jnp.float32),
             pltpu.SemaphoreType.DMA((n + 2,)),
+            pltpu.SemaphoreType.DMA((4,)),
         ],
-        compiler_params=params(60),
-    )(tokens, routes.T, route_weights.T)
+        compiler_params=params(8),
+    )(*(pltpu.with_memory_space_constraint(operand, pltpu.HBM) for operand in operands))
 
 
 def largest_kernel(weight_ref, held_ref, largest_ref, rest_ref, sem):
@@ -111,18 +128,19 @@
     )(pltpu.with_memory_space_constraint(weights, pltpu.HBM))
 
 
-def partial_kernel(got_ref, weight_ref, *rest, rows, experts, other):
+def partial_kernel(kept_ref, swapped_ref, weight_ref, *rest, rows, experts, other):
     if other:
-        held_ref, tail_ref, out_ref, scaled_ref, total_ref, rest_ref, sem = rest
+        held_ref, tail_ref, out_ref, scaled_ref, total_ref, rest_ref, block_ref, sem, out_sem = rest
         parts = [held_ref, rest_ref.at[0]]
     else:
-        out_ref, scaled_ref, total_ref, rest_ref, sem = rest
+        out_ref, scaled_ref, total_ref, rest_ref, block_ref, sem, out_sem = rest
         parts = [rest_ref.at[0], rest_ref.at[1]]
-    n, _, depth = got_ref.shape
-    half, ff = n // 2, weight_ref.shape[1]
+    n, _, width = kept_ref.shape
+    half, ff, depth = n // 2, weight_ref.shape[1], 2 * width
     mine = (lax.axis_index("expert") >= half).astype(jnp.int32) * half
     theirs = half - mine
-    first = theirs if other else mine
+    first = mine if other else theirs
+    left = lax.axis_index("tensor") == 0
     deep = experts // 2 * depth
     copies = [
         None
@@ -133,12 +151,34 @@
     for copy in copies:
         if copy is not None:
             copy.start()
+    outs = []
+
+    def send(at, size):
+        lanes = pl.ds(at, size)
+        outs.append(
+            pltpu.make_async_copy(
+                block_ref.at[:, :, lanes], out_ref.at[:, :, lanes], out_sem.at[len(outs)]
+            )
+        )
+        outs[-1].start()
+
+    if other:
+        for r in range(half):
+            for at, owner in ((0, theirs + half - 1 - r), (rows // 2, mine + half - 1 - r)):
+                block_ref[r, at : at + rows // 2, ff:] = jnp.broadcast_to(
+                    tail_ref[pl.ds(owner, 1), :], (rows // 2, LANES)
+                ).astype(jnp.bfloat16)
+        send(ff, LANES)
     step = max(1, 64 // rows)
     for r in range(0, half, step):
         count = step * rows
-        block = got_ref[pl.ds(first + r, step)]
-        x = block[:, :rows].reshape(count, depth).astype(jnp.float32)
-        packed = block[:, rows:].astype(jnp.float32)
+        kept = kept_ref[pl.ds(first + r, step)].astype(jnp.float32)
+        swapped = swapped_ref[pl.ds(first + r, step), :rows].astype(jnp.float32)
+        own = kept[:, :rows]
+        x = jnp.concatenate(
+            [jnp.where(left, own, swapped), jnp.where(left, swapped, own)], axis=2
+        ).reshape(count, depth)
+        packed = kept[:, rows:]
         gates = jnp.concatenate(
             [
                 packed[:, :, at : at + experts] + packed[:, :, at + experts : at + 2 * experts]
@@ -163,36 +203,36 @@
                 total_ref[:, at : at + TILE] = product
             else:
                 product += total_ref[:, at : at + TILE]
-                out_ref[:, :, at : at + TILE] = product.astype(jnp.bfloat16).reshape(
+                block_ref[:, :, at : at + TILE] = product.astype(jnp.bfloat16).reshape(
                     half, rows, TILE
                 )
-    if other:
-        for r in range(half):
-            for at, owner in ((0, theirs + r), (rows // 2, mine + r)):
-                out_ref[r, at : at + rows // 2, ff:] = jnp.broadcast_to(
-                    tail_ref[pl.ds(owner, 1), :], (rows // 2, LANES)
-                ).astype(jnp.bfloat16)
+                send(at, TILE)
+    for out in outs:
+        out.wait()
 
 
 def partials(got, weight, held, tail, rows, experts):
-    n, _, depth = got.shape
-    half, ff = n // 2, weight.shape[1]
+    n, _, width = got[0].shape
+    half, ff, depth = n // 2, weight.shape[1], 2 * width
     deep = experts // 2 * depth
     other = held is not None
-    operands = (got, pltpu.with_memory_space_constraint(weight, pltpu.HBM))
+    operands = (*got, pltpu.with_memory_space_constraint(weight, pltpu.HBM))
     if other:
         held = pltpu.with_memory_space_constraint(held.reshape(deep, ff), pltpu.VMEM)
         operands += (held, tail)
+    shape = (half, rows, ff + LANES * other)
     return pl.pallas_call(
         functools.partial(partial_kernel, rows=rows, experts=experts, other=other),
-        out_shape=jax.ShapeDtypeStruct((half, rows, ff + LANES * other), jnp.bfloat16),
-        in_specs=[VMEM, HBM, VMEM, VMEM][: len(operands)],
-        out_specs=VMEM,
+        out_shape=pltpu.HBM(shape, jnp.bfloat16),
+        in_specs=[VMEM, VMEM, HBM, VMEM, VMEM][: len(operands)],
+        out_specs=HBM,
         scratch_shapes=[
             pltpu.VMEM((half * rows, experts * depth), jnp.bfloat16),
             pltpu.VMEM((half * rows, ff), jnp.float32),
             pltpu.VMEM((1 if other else 2, deep, ff), weight.dtype),
+            pltpu.VMEM(shape, jnp.bfloat16),
             pltpu.SemaphoreType.DMA((2,)),
+            pltpu.SemaphoreType.DMA((ff // TILE + 1,)),
         ],
         compiler_params=params(24),
         cost_estimate=pl.CostEstimate(
@@ -228,11 +268,10 @@
     )(near, merged, crossed)
 
 
-def halves_of(n):
-    return [list(range(n // 2)), list(range(n // 2, n))]
-
-
-def exchange(block, groups=None):
+def exchange(block, parts):
+    n = lax.axis_size("expert")
+    size = n // parts
+    groups = [list(range(first + size - 1, first - 1, -1)) for first in range(0, n, size)]
     return lax.all_to_all(
         block, "expert", split_axis=0, concat_axis=0, tiled=True, axis_index_groups=groups
     )
@@ -248,12 +287,14 @@
     n = lax.axis_size("expert")
     rows = tokens.shape[0]
     experts, depth, ff = learner_weights.shape
-    got = exchange(pack(tokens, routes, route_weights, n, depth))
+    got = exchange(pack(tokens, routes, route_weights, n, depth // 2), 1)
     held, largest = hold(learner_weights)
     largest = over_tensor(largest)
+    got, held, largest = lax.optimization_barrier((got, held, largest))
+    got = (got, lax.ppermute(got, "tensor", [(0, 1), (1, 0)]))
     weight = learner_weights.reshape(experts * depth, ff)
-    other = exchange(partials(got, weight, held, largest, rows, experts), halves_of(n))
-    near = exchange(partials(got, weight, None, None, rows, experts), halves_of(n))
+    other = exchange(partials(got, weight, held, largest, rows, experts), 2)
+    near = exchange(partials(got, weight, None, None, rows, experts), 2)
     merged_max = jnp.max(other[:, :, ff:], axis=0)
     merged = jnp.sum(other[:, :, :ff].astype(jnp.float32), axis=0).astype(jnp.bfloat16)
     merged = jnp.concatenate([merged, merged_max], axis=1)
@@ -270,10 +311,10 @@
     gate = jnp.sum(jnp.where(chosen, route_weights[:, :, None], 0.0), axis=1)
     high = lax.reduce_precision(gate, 8, 7)
     terms = jnp.concatenate([high, gate - high], axis=1).astype(jnp.bfloat16)
-    columns = tokens.reshape(rows, n, depth).transpose(1, 0, 2)
-    top = jnp.broadcast_to(largest[:, None, None], (n, rows, 1))
+    columns = tokens.reshape(rows, n, depth).transpose(1, 0, 2)[::-1]
+    top = jnp.broadcast_to(largest[::-1, None, None], (n, rows, 1))
     got = exchange(
-        jnp.concatenate([columns, jnp.broadcast_to(terms, (n, *terms.shape)), top], axis=2)
+        jnp.concatenate([columns, jnp.broadcast_to(terms, (n, *terms.shape)), top], axis=2), 1
     )
     weight = learner_weights.reshape(experts * depth, ff)
 
@@ -286,7 +327,7 @@
         )
         return product.astype(jnp.bfloat16)
 
-    back = exchange(lax.map(one, got))
+    back = exchange(lax.map(one, got), 1)
     combined = jnp.sum(back.astype(jnp.float32), axis=0).astype(jnp.bfloat16)
     expert_amax = jnp.max(got[:, 0, depth + 2 * experts]).astype(jnp.float32).reshape(1)
     return (combined, expert_amax)
@@ -295,8 +336,8 @@
 def shards(tokens, routes, route_weights, learner_weights):
     n, rows = lax.axis_size("expert"), tokens.shape[0]
     experts, depth, ff = learner_weights.shape
-    aligned = depth % LANES == 0 and ff % TILE == 0 and rows % 32 == 0 and n % 2 == 0
-    fits = rows // SUBLANES * 2 * experts <= depth
+    aligned = depth % (2 * LANES) == 0 and ff % TILE == 0 and rows % 32 == 0 and n % 4 == 0
+    fits = lax.axis_size("tensor") == 2 and rows // SUBLANES * 2 * experts <= depth // 2
     small = experts * depth * ff <= 4 << 20 and n * rows <= 1024
     form = kernels if aligned and fits and small and experts == n else plain
     return form(tokens, routes, route_weights, learner_weights)

time: 49.1 us -> 47.5 us (0.967)
  waiting for transfers between devices: 16.1 us -> 7.59 us
  starting transfers between devices: 16.7 us -> 24.1 us
  local copies, waits for them, and re-layouts: 0.76 us -> 0 us
    all_to_all x3, waiting for transfers between devices: 15 us -> 5.04 us  [exchange(): lax.all_to_all(block, 'expert', split_axis=0, concat_axis=0, tiled=True,...]
    all_to_all x3, starting transfers between devices: 15.2 us -> 22 us  [exchange(): lax.all_to_all(block, 'expert', split_axis=0, concat_axis=0, tiled=True,...]
    ppermute x0 -> x1, waiting for transfers between devices: none -> 1.39 us  [kernels(): got = (got, lax.ppermute(got, 'tensor', [(0, 1), (1, 0)]))]
    unnamed x2 -> x0, local copies, waits for them, and re-layouts: 0.76 us -> none
    ppermute x1, starting transfers between devices: 1.39 us -> 1.99 us  [kernels(): lax.ppermute(merged, 'expert', [(i, (i + n // 2) % n) for i in range(n)])]
  transfers between devices with their start and end apart: 5 -> 6, of which waited for: 4 -> 5; matrix products, arithmetic and copies ran while one was open for 0% -> 0% of each run, Pallas kernels for 17% -> 18%
where the time goes in v4:
time: 47.5 us; the launch traced here: 47 us
  starting transfers between devices  24.1 us (51%)
  Pallas kernels  14.5 us (31%)
  waiting for transfers between devices  7.59 us (16%)
  between operations  0.69 us (1%)
    all_to_all x3, starting transfers between devices, exchange(): lax.all_to_all(block, 'expert', split_axis=0, concat_axis=0, tiled=True,...  22 us
    pallas_call x2, Pallas kernels, partials(): pl.pallas_call(functools.partial(partial_kernel, rows=rows, experts=exper...  8.96 us
    all_to_all x3, waiting for transfers between devices, exchange(): lax.all_to_all(block, 'expert', split_axis=0, concat_axis=0, tiled=True,...  5.04 us
    pallas_call x1, Pallas kernels, hold(): pl.pallas_call(largest_kernel, out_shape=(pltpu.VMEM((kept, depth, ff), w...  3.17 us
    ppermute x1, starting transfers between devices, kernels(): lax.ppermute(merged, 'expert', [(i, (i + n // 2) % n) for i in range(n)])  1.99 us
    pallas_call x1, Pallas kernels, pack(): pl.pallas_call(pack_kernel, out_shape=pltpu.HBM(shape, jnp.bfloat16), in_...  1.72 us
    ppermute x1, waiting for transfers between devices, kernels(): got = (got, lax.ppermute(got, 'tensor', [(0, 1), (1, 0)]))  1.39 us
    ppermute x1, waiting for transfers between devices, over_tensor(): lax.ppermute(largest, 'tensor', [(0, 1), (1, 0)])  1.16 us
  transfers between devices with their start and end apart: 6, of which 5 were waited for; matrix products, arithmetic and copies ran while one was open for 0% of the time, Pallas kernels for 18%

profile of v4, /device:TPU:0, one launch (start us, length us, event | category | flops | bytes accessed | tf_op | source)
XLA Modules:
  0.0 47.0 jit_solution(4412055995948064182)
XLA Ops:
  0.6 1.7 %shard_map.59 = bf16[16,40,128]{2,1,0:T(8,128)(2,1)} custom-call(bf16[32,4096]{1,0:T(8,128)(2,1)} %tokens_ref.1, s32[8,32]{1,0:T(8,128)} %bitcast.7, f32[8,32]{1,0:T(8,128)} %bitcast.8), custom_call_target="tpu_custom_call" | custom-call | tf_op jit(solution)/shard_map/pallas_call | solution.py:76
  2.4 10.3 %all-to-all-start = ((bf16[16,40,128]{2,1,0:T(8,128)(2,1)}), bf16[16,40,128]{2,1,0:T(8,128)(2,1)S(1)}, u32[]{:S(2)}, u32[]{:S(2)}) async-start(bf16[16,40,128]{2,1,0:T(8,128)(2,1)} %shard_map.59), calls=%async_computation | async-start | bytes 327680 | tf_op jit(solution)/shard_map/all_to_all | solution.py:275
  12.7 3.2 %shard_map.60 = (bf16[8,256,768]{2,1,0:T(8,128)(2,1)S(1)}, f32[16,128]{1,0:T(8,128)S(1)}) custom-call(bf16[16,256,768]{2,1,0:T(8,128)(2,1)} %weight_ref.1), custom_call_target="tpu_custom_call" | custom-call | flops 6291456 | bytes 6291456 | tf_op jit(solution)/shard_map/pallas_call | solution.py:112
  15.9 0.1 collective-permute-start
  16.0 1.2 %collective-permute-done = f32[16,128]{1,0:T(8,128)S(1)} collective-permute-done((f32[16,128]{1,0:T(8,128)S(1)}, f32[16,128]{1,0:T(8,128)S(1)}, u32[]{:S(2)}, u32[]{:S(2)}) %collective-permute-start) | collective-permute-done | bytes 8224 | tf_op jit(solution)/shard_map/ppermute | solution.py:282
  17.1 0.2 all-to-all-done.kept_ref
  17.3 0.0 collective-permute-start.1
  17.3 1.4 %collective-permute-done.1.swapped_ref = bf16[16,40,128]{2,1,0:T(8,128)(2,1)S(1)} collective-permute-done((bf16[16,40,128]{2,1,0:T(8,128)(2,1)S(1)}, bf16[16,40,128]{2,1,0:T(8,128)(2,1)S(1)}, u32[]{:S(2)}, u32[]{:S(2)}) %collective-permute-start.1) | collective-permute-done | bytes 163872 | tf_op jit(solution)/shard_map/ppermute | solution.py:294
  18.7 3.9 %shard_map.62 = bf16[8,32,896]{2,1,0:T(8,128)(2,1)} custom-call(bf16[16,40,128]{2,1,0:T(8,128)(2,1)S(1)} %all-to-all-done.kept_ref, bf16[16,40,128]{2,1,0:T(8,128)(2,1)S(1)} %collective-permute-done.1.swapped_ref, bf16[4096,768]{1,0:T(8,128)(2,1)} %bitcast.5, bf16[2048,768]{1,0:T(8,128)(2,1)S(1)} %bitcast.4, f32[16,128]{1,0:T(8,128)S(1)} %max.3.rest_1_), custom_call_target="tpu_custom_call" | custom-call | flops 1610612736 | bytes 6291456 | tf_op jit(solution)/shard_map/pallas_call | solution.py:224
  22.6 5.7 %all-to-all-start.2 = ((bf16[8,32,896]{2,1,0:T(8,128)(2,1)}), bf16[8,32,896]{2,1,0:T(8,128)(2,1)S(1)}, u32[]{:S(2)}, u32[]{:S(2)}) async-start(bf16[8,32,896]{2,1,0:T(8,128)(2,1)} %shard_map.62), calls=%async_computation.2 | async-start | bytes 917504 | tf_op jit(solution)/shard_map/all_to_all | solution.py:275
  28.3 5.1 %shard_map.61 = bf16[8,32,768]{2,1,0:T(8,128)(2,1)} custom-call(bf16[16,40,128]{2,1,0:T(8,128)(2,1)S(1)} %all-to-all-done.kept_ref, bf16[16,40,128]{2,1,0:T(8,128)(2,1)S(1)} %collective-permute-done.1.swapped_ref, bf16[4096,768]{1,0:T(8,128)(2,1)} %bitcast.6), custom_call_target="tpu_custom_call" | custom-call | flops 1610612736 | bytes 6291456 | tf_op jit(solution)/shard_map/pallas_call | solution.py:224
  33.3 1.4 %all-to-all-done.2 = bf16[8,32,896]{2,1,0:T(8,128)(2,1)S(1)} async-done(((bf16[8,32,896]{2,1,0:T(8,128)(2,1)}), bf16[8,32,896]{2,1,0:T(8,128)(2,1)S(1)}, u32[]{:S(2)}, u32[]{:S(2)}) %all-to-all-start.2) | async-done | bytes 458784 | tf_op jit(solution)/shard_map/all_to_all | solution.py:275
  34.7 6.0 %all-to-all-start.1 = ((bf16[8,32,768]{2,1,0:T(8,128)(2,1)}), bf16[8,32,768]{2,1,0:T(8,128)(2,1)S(1)}, u32[]{:S(2)}, u32[]{:S(2)}) async-start(bf16[8,32,768]{2,1,0:T(8,128)(2,1)} %shard_map.61), calls=%async_computation.1 | async-start | bytes 786432 | tf_op jit(solution)/shard_map/all_to_all | solution.py:275
  40.7 0.1 slice_reduce_fusion
  40.8 2.0 %collective-permute-start.2 = (bf16[32,896]{1,0:T(8,128)(2,1)S(1)}, bf16[32,896]{1,0:T(8,128)(2,1)S(1)}, u32[]{:S(2)}, u32[]{:S(2)}) collective-permute-start(bf16[32,896]{1,0:T(8,128)(2,1)S(1)} %pad_maximum_fusion.merged_ref), channel_id=1, source_target_pairs={{0,16},{2,18},{4,20},{6,22},{8,24},{10,26},{12,28},{14,30},{16,0},... | collective-permute-start | bytes 172040 | tf_op jit(solution)/shard_map/ppermute | solution.py:301
  42.8 3.5 %all-to-all-done.1.near_ref = bf16[8,32,768]{2,1,0:T(8,128)(2,1)S(1)} async-done(((bf16[8,32,768]{2,1,0:T(8,128)(2,1)}), bf16[8,32,768]{2,1,0:T(8,128)(2,1)S(1)}, u32[]{:S(2)}, u32[]{:S(2)}) %all-to-all-start.1) | async-done | bytes 393248 | tf_op jit(solution)/shard_map/all_to_all | solution.py:275
  46.3 0.0 collective-permute-done.2.crossed_ref
  46.3 0.7 %shard_map.63 = (bf16[32,768]{1,0:T(8,128)(2,1)}, f32[1]{0:T(128)}) custom-call(bf16[8,32,768]{2,1,0:T(8,128)(2,1)S(1)} %all-to-all-done.1.near_ref, bf16[32,896]{1,0:T(8,128)(2,1)S(1)} %pad_maximum_fusion.merged_ref, bf16[32,896]{1,0:T(8,128)(2,1)S(1)} %collective-permute-done.2.crossed_ref), custom_call_target="tpu_custom_call" | custom-call | tf_op jit(solution)/shard_map/pallas_call | solution.py:259
  (3 shorter events, 0.0 us)
Async XLA Ops:
  2.4 14.9 %all-to-all-start = ((bf16[16,40,128]{2,1,0:T(8,128)(2,1)}), bf16[16,40,128]{2,1,0:T(8,128)(2,1)S(1)}, u32[]{:S(2)}, u32[]{:S(2)}) async-start(bf16[16,40,128]{2,1,0:T(8,128)(2,1)} %shard_map.59), calls=%async_computation | async-start | bytes 327680 | tf_op jit(solution)/shard_map/all_to_all | solution.py:275
  15.9 1.2 %collective-permute-start = (f32[16,128]{1,0:T(8,128)S(1)}, f32[16,128]{1,0:T(8,128)S(1)}, u32[]{:S(2)}, u32[]{:S(2)}) collective-permute-start(f32[16,128]{1,0:T(8,128)S(1)} %get-tuple-element.8), channel_id=1, source_target_pairs={{0,1},{1,0},{2,3},{3,2},{4,5},{5,4},{6,7},{7,6},{8,9},{9,8},{10,11... | collective-permute-start | bytes 24584 | tf_op jit(solution)/shard_map/ppermute | solution.py:282
  17.3 1.4 %collective-permute-start.1 = (bf16[16,40,128]{2,1,0:T(8,128)(2,1)S(1)}, bf16[16,40,128]{2,1,0:T(8,128)(2,1)S(1)}, u32[]{:S(2)}, u32[]{:S(2)}) collective-permute-start(bf16[16,40,128]{2,1,0:T(8,128)(2,1)S(1)} %all-to-all-done.kept_ref), channel_id=1, source_target_pairs={{0,1},{1,0},{2,3},{3,2},{4,5},{5,4},{6,7},{7,6},{8,9},{9,8},{10,11... | collective-permute-start | bytes 491528 | tf_op jit(solution)/shard_map/ppermute | solution.py:294
  22.6 12.1 %all-to-all-start.2 = ((bf16[8,32,896]{2,1,0:T(8,128)(2,1)}), bf16[8,32,896]{2,1,0:T(8,128)(2,1)S(1)}, u32[]{:S(2)}, u32[]{:S(2)}) async-start(bf16[8,32,896]{2,1,0:T(8,128)(2,1)} %shard_map.62), calls=%async_computation.2 | async-start | bytes 917504 | tf_op jit(solution)/shard_map/all_to_all | solution.py:275
  34.7 11.5 %all-to-all-start.1 = ((bf16[8,32,768]{2,1,0:T(8,128)(2,1)}), bf16[8,32,768]{2,1,0:T(8,128)(2,1)S(1)}, u32[]{:S(2)}, u32[]{:S(2)}) async-start(bf16[8,32,768]{2,1,0:T(8,128)(2,1)} %shard_map.61), calls=%async_computation.1 | async-start | bytes 786432 | tf_op jit(solution)/shard_map/all_to_all | solution.py:275
  40.8 5.5 %collective-permute-start.2 = (bf16[32,896]{1,0:T(8,128)(2,1)S(1)}, bf16[32,896]{1,0:T(8,128)(2,1)S(1)}, u32[]{:S(2)}, u32[]{:S(2)}) collective-permute-start(bf16[32,896]{1,0:T(8,128)(2,1)S(1)} %pad_maximum_fusion.merged_ref), channel_id=1, source_target_pairs={{0,16},{2,18},{4,20},{6,22},{8,24},{10,26},{12,28},{14,30},{16,0},... | collective-permute-start | bytes 172040 | tf_op jit(solution)/shard_map/ppermute | solution.py:301

commit v5 on v4

--- a/solution.py
+++ b/solution.py
@@ -9,6 +9,7 @@
 
 LANES = 128
 SUBLANES = 8
+PLANE = 4
 VMEM = pl.BlockSpec(memory_space=pltpu.VMEM)
 HBM = pl.BlockSpec(memory_space=pltpu.HBM)
 TILE = 256
@@ -128,71 +129,65 @@
     )(pltpu.with_memory_space_constraint(weights, pltpu.HBM))
 
 
-def partial_kernel(kept_ref, swapped_ref, weight_ref, *rest, rows, experts, other):
-    if other:
-        held_ref, tail_ref, out_ref, scaled_ref, total_ref, rest_ref, block_ref, sem, out_sem = rest
-        parts = [held_ref, rest_ref.at[0]]
+def place(column, plane):
+    index = lax.axis_index("expert")
+    planes = lax.axis_size("expert") // PLANE
+    beyond = lax.rem(lax.div(index, PLANE) + plane, planes)
+    return beyond * PLANE + jnp.bitwise_xor(lax.rem(index, PLANE), column)
+
+
+def partial_kernel(*refs, rows, experts, columns, load):
+    kept_ref, swapped_ref, tail_ref, held_ref, rest_ref, *refs = refs
+    away = columns != (0,)
+    count = len(columns)
+    if load:
+        weight_ref, (rest_ref, *refs) = rest_ref, refs
+    if away:
+        out_refs, (scaled_ref, total_ref, block_ref, sem, out_sem) = refs[:count], refs[count:]
     else:
-        out_ref, scaled_ref, total_ref, rest_ref, block_ref, sem, out_sem = rest
-        parts = [rest_ref.at[0], rest_ref.at[1]]
+        own_ref, largest_ref, scaled_ref, total_ref, sem = refs
     n, _, width = kept_ref.shape
-    half, ff, depth = n // 2, weight_ref.shape[1], 2 * width
-    mine = (lax.axis_index("expert") >= half).astype(jnp.int32) * half
-    theirs = half - mine
-    first = mine if other else theirs
+    ff, depth, planes = held_ref.shape[1], 2 * width, n // PLANE
+    chips = [[place(column, plane) for plane in range(planes)] for column in columns]
     left = lax.axis_index("tensor") == 0
     deep = experts // 2 * depth
-    copies = [
-        None
-        if other and i == 0
-        else pltpu.make_async_copy(weight_ref.at[pl.ds(i * deep, deep)], part, sem.at[i])
-        for i, part in enumerate(parts)
-    ]
-    for copy in copies:
-        if copy is not None:
-            copy.start()
-    outs = []
-
-    def send(at, size):
-        lanes = pl.ds(at, size)
-        outs.append(
-            pltpu.make_async_copy(
-                block_ref.at[:, :, lanes], out_ref.at[:, :, lanes], out_sem.at[len(outs)]
+    if load:
+        fetch = pltpu.make_async_copy(weight_ref.at[pl.ds(deep, deep)], rest_ref, sem)
+        fetch.start()
+    for i, column in enumerate(chips):
+        row = lax.broadcasted_iota(jnp.int32, (SUBLANES, LANES), 0)
+        top = jnp.zeros((SUBLANES, LANES), jnp.float32)
+        for plane, chip in enumerate(column):
+            value = jnp.broadcast_to(tail_ref[pl.ds(chip, 1), :], (SUBLANES, LANES))
+            top = jnp.where(row == plane, value, top)
+        if away:
+            block_ref[i, planes * rows :, :LANES] = top.astype(jnp.bfloat16)
+            block_ref[i, planes * rows :, LANES:] = jnp.zeros(
+                (SUBLANES, ff - LANES), jnp.bfloat16
             )
-        )
-        outs[-1].start()
-
-    if other:
-        for r in range(half):
-            for at, owner in ((0, theirs + half - 1 - r), (rows // 2, mine + half - 1 - r)):
-                block_ref[r, at : at + rows // 2, ff:] = jnp.broadcast_to(
-                    tail_ref[pl.ds(owner, 1), :], (rows // 2, LANES)
-                ).astype(jnp.bfloat16)
-        send(ff, LANES)
-    step = max(1, 64 // rows)
-    for r in range(0, half, step):
-        count = step * rows
-        kept = kept_ref[pl.ds(first + r, step)].astype(jnp.float32)
-        swapped = swapped_ref[pl.ds(first + r, step), :rows].astype(jnp.float32)
-        own = kept[:, :rows]
-        x = jnp.concatenate(
-            [jnp.where(left, own, swapped), jnp.where(left, swapped, own)], axis=2
-        ).reshape(count, depth)
-        packed = kept[:, rows:]
+        else:
+            largest_ref[...] = top
+    for i, chip in enumerate([chip for column in chips for chip in column]):
+        kept = kept_ref[n - 1 - chip].astype(jnp.float32)
+        swapped = swapped_ref[n - 1 - chip, :rows].astype(jnp.float32)
+        own = kept[:rows]
+        x = jnp.concatenate([jnp.where(left, own, swapped), jnp.where(left, swapped, own)], axis=1)
+        packed = kept[rows:]
         gates = jnp.concatenate(
             [
-                packed[:, :, at : at + experts] + packed[:, :, at + experts : at + 2 * experts]
+                packed[:, at : at + experts] + packed[:, at + experts : at + 2 * experts]
                 for at in range(0, rows // SUBLANES * 2 * experts, 2 * experts)
             ],
-            axis=1,
-        ).reshape(count, experts)
+            axis=0,
+        )
         for e in range(experts):
-            scaled_ref[r * rows : r * rows + count, e * depth : (e + 1) * depth] = (
+            scaled_ref[i * rows : (i + 1) * rows, e * depth : (e + 1) * depth] = (
                 x * gates[:, e : e + 1]
             ).astype(jnp.bfloat16)
-    for i, (part, copy) in enumerate(zip(parts, copies)):
-        if copy is not None:
-            copy.wait()
+    outs = []
+    for i, part in enumerate((held_ref, rest_ref)):
+        if load and i == 1:
+            fetch.wait()
         for at in range(0, ff, TILE):
             product = jnp.dot(
                 scaled_ref[:, i * deep : (i + 1) * deep],
@@ -201,71 +196,106 @@
             )
             if i == 0:
                 total_ref[:, at : at + TILE] = product
-            else:
-                product += total_ref[:, at : at + TILE]
-                block_ref[:, :, at : at + TILE] = product.astype(jnp.bfloat16).reshape(
-                    half, rows, TILE
+                continue
+            product += total_ref[:, at : at + TILE]
+            if not away:
+                own_ref[:, at : at + TILE] = product
+                continue
+            lanes = pl.ds(at, TILE)
+            for c, out_ref in enumerate(out_refs):
+                block_ref[c, : planes * rows, at : at + TILE] = product[
+                    c * planes * rows : (c + 1) * planes * rows
+                ].astype(jnp.bfloat16)
+                outs.append(
+                    pltpu.make_async_copy(
+                        block_ref.at[c, :, lanes], out_ref.at[:, lanes], out_sem.at[len(outs)]
+                    )
                 )
-                send(at, TILE)
+                outs[-1].start()
     for out in outs:
         out.wait()
 
 
-def partials(got, weight, held, tail, rows, experts):
+def partials(got, tail, weights, rows, experts, columns, load=False):
     n, _, width = got[0].shape
-    half, ff, depth = n // 2, weight.shape[1], 2 * width
-    deep = experts // 2 * depth
-    other = held is not None
-    operands = (*got, pltpu.with_memory_space_constraint(weight, pltpu.HBM))
-    if other:
-        held = pltpu.with_memory_space_constraint(held.reshape(deep, ff), pltpu.VMEM)
-        operands += (held, tail)
-    shape = (half, rows, ff + LANES * other)
+    depth, planes = 2 * width, n // PLANE
+    held, rest = weights
+    deep, ff = held.shape
+    away = columns != (0,)
+    count = planes * rows * len(columns)
+    held = pltpu.with_memory_space_constraint(held, pltpu.VMEM)
+    rest = pltpu.with_memory_space_constraint(rest, pltpu.HBM if load else pltpu.VMEM)
+    operands = (*got, tail, held, rest)
+    out_shape, out_specs = (), ()
+    if load:
+        out_shape += (pltpu.VMEM((deep, ff), rest.dtype),)
+        out_specs += (VMEM,)
+    scratch = [
+        pltpu.VMEM((count, experts * depth), jnp.bfloat16),
+        pltpu.VMEM((count, ff), jnp.float32),
+    ]
+    if away:
+        shape = (planes * rows + SUBLANES, ff)
+        out_shape += (pltpu.HBM(shape, jnp.bfloat16),) * len(columns)
+        out_specs += (HBM,) * len(columns)
+        scratch += [
+            pltpu.VMEM((len(columns), *shape), jnp.bfloat16),
+            pltpu.SemaphoreType.DMA,
+            pltpu.SemaphoreType.DMA((ff // TILE * len(columns),)),
+        ]
+    else:
+        out_shape += (
+            jax.ShapeDtypeStruct((count, ff), jnp.float32),
+            jax.ShapeDtypeStruct((SUBLANES, LANES), jnp.float32),
+        )
+        out_specs += (VMEM, VMEM)
+        scratch += [pltpu.SemaphoreType.DMA]
     return pl.pallas_call(
-        functools.partial(partial_kernel, rows=rows, experts=experts, other=other),
-        out_shape=pltpu.HBM(shape, jnp.bfloat16),
-        in_specs=[VMEM, VMEM, HBM, VMEM, VMEM][: len(operands)],
-        out_specs=HBM,
-        scratch_shapes=[
-            pltpu.VMEM((half * rows, experts * depth), jnp.bfloat16),
-            pltpu.VMEM((half * rows, ff), jnp.float32),
-            pltpu.VMEM((1 if other else 2, deep, ff), weight.dtype),
-            pltpu.VMEM(shape, jnp.bfloat16),
-            pltpu.SemaphoreType.DMA((2,)),
-            pltpu.SemaphoreType.DMA((ff // TILE + 1,)),
-        ],
-        compiler_params=params(24),
+        functools.partial(
+            partial_kernel, rows=rows, experts=experts, columns=columns, load=load
+        ),
+        out_shape=out_shape,
+        in_specs=[VMEM, VMEM, VMEM, VMEM, HBM if load else VMEM],
+        out_specs=out_specs,
+        scratch_shapes=scratch,
+        compiler_params=params(16),
         cost_estimate=pl.CostEstimate(
-            flops=2 * half * rows * experts * depth * ff,
-            bytes_accessed=2 * weight.size,
+            flops=2 * count * experts * depth * ff,
+            bytes_accessed=4 * held.size,
             transcendentals=0,
         ),
     )(*operands)
 
 
-def finish_kernel(near_ref, merged_ref, crossed_ref, out_ref, largest_ref):
+def finish_kernel(own_ref, largest_ref, *refs, planes):
+    plane_refs, crossed_refs = refs[: PLANE - 1], refs[PLANE - 1 : -2]
+    out_ref, top_ref = refs[-2:]
     rows, ff = out_ref.shape
-    total = crossed_ref[:, :ff].astype(jnp.float32)
-    for i in range(near_ref.shape[0]):
-        total += near_ref[i].astype(jnp.float32)
+    total = own_ref[:rows]
+    top = largest_ref[:1]
+    for ref in plane_refs:
+        total += ref[:rows].astype(jnp.float32)
+        maxima = ref[planes * rows :, :LANES].astype(jnp.float32)
+        top = jnp.maximum(top, maxima[:1])
+    for ref in crossed_refs:
+        total += ref[:, :ff].astype(jnp.float32)
+        top = jnp.maximum(top, ref[:, ff:].astype(jnp.float32)[:1])
     out_ref[...] = total.astype(jnp.bfloat16)
-    own = merged_ref[rows // 2 :, ff:].astype(jnp.float32)
-    theirs = crossed_ref[: rows // 2, ff:].astype(jnp.float32)
-    largest_ref[0] = jnp.max(jnp.maximum(own, theirs))
-
-
-def finish(near, merged, crossed):
-    _, rows, ff = near.shape
+    top_ref[0] = jnp.max(top)
+
+
+def finish(own, largest, near, crossed, rows):
+    operands = (own, largest, *near, *crossed)
     return pl.pallas_call(
-        finish_kernel,
+        functools.partial(finish_kernel, planes=len(crossed) + 1),
         out_shape=(
-            jax.ShapeDtypeStruct((rows, ff), jnp.bfloat16),
+            jax.ShapeDtypeStruct((rows, own.shape[1]), jnp.bfloat16),
             jax.ShapeDtypeStruct((1,), jnp.float32),
         ),
-        in_specs=[VMEM] * 3,
+        in_specs=[VMEM] * len(operands),
         out_specs=(VMEM, pl.BlockSpec(memory_space=pltpu.SMEM)),
         compiler_params=params(8),
-    )(near, merged, crossed)
+    )(*operands)
 
 
 def exchange(block, parts):
@@ -292,14 +322,28 @@
     largest = over_tensor(largest)
     got, held, largest = lax.optimization_barrier((got, held, largest))
     got = (got, lax.ppermute(got, "tensor", [(0, 1), (1, 0)]))
+    held = held.reshape(-1, ff)
     weight = learner_weights.reshape(experts * depth, ff)
-    other = exchange(partials(got, weight, held, largest, rows, experts), 2)
-    near = exchange(partials(got, weight, None, None, rows, experts), 2)
-    merged_max = jnp.max(other[:, :, ff:], axis=0)
-    merged = jnp.sum(other[:, :, :ff].astype(jnp.float32), axis=0).astype(jnp.bfloat16)
-    merged = jnp.concatenate([merged, merged_max], axis=1)
-    crossed = lax.ppermute(merged, "expert", [(i, (i + n // 2) % n) for i in range(n)])
-    return finish(near, merged, crossed)
+    rest, far = partials(got, largest, (held, weight), rows, experts, (3,), load=True)
+    side, front = partials(got, largest, (held, rest), rows, experts, (1, 2))
+    own, own_largest = partials(got, largest, (held, rest), rows, experts, (0,))
+    near = [
+        lax.ppermute(block, "expert", [(i, i ^ column) for i in range(n)])
+        for column, block in ((1, side), (2, front), (3, far))
+    ]
+    planes = n // PLANE
+    crossed = []
+    for plane in range(1, planes):
+        begin = plane * rows
+        total = own[begin : begin + rows]
+        top = own_largest[plane]
+        for block in near:
+            total += block[begin : begin + rows].astype(jnp.float32)
+            top = jnp.maximum(top, block[planes * rows + plane, :LANES].astype(jnp.float32))
+        merged = jnp.concatenate([total, jnp.broadcast_to(top, (rows, LANES))], axis=1)
+        pairs = [(i, (i + plane * PLANE) % n) for i in range(n)]
+        crossed.append(lax.ppermute(merged.astype(jnp.bfloat16), "expert", pairs))
+    return finish(own, own_largest, near, crossed, rows)
 
 
 def plain(tokens, routes, route_weights, learner_weights):
@@ -336,9 +380,9 @@
 def shards(tokens, routes, route_weights, learner_weights):
     n, rows = lax.axis_size("expert"), tokens.shape[0]
     experts, depth, ff = learner_weights.shape
-    aligned = depth % (2 * LANES) == 0 and ff % TILE == 0 and rows % 32 == 0 and n % 4 == 0
+    aligned = depth % (2 * LANES) == 0 and ff % TILE == 0 and rows % 32 == 0 and n % PLANE == 0
     fits = lax.axis_size("tensor") == 2 and rows // SUBLANES * 2 * experts <= depth // 2
-    small = experts * depth * ff <= 4 << 20 and n * rows <= 1024
+    small = experts * depth * ff <= 4 << 20 and n * rows <= 1024 and n <= PLANE * SUBLANES
     form = kernels if aligned and fits and small and experts == n else plain
     return form(tokens, routes, route_weights, learner_weights)
 

time: 47.5 us -> 44 us (0.926)
  starting transfers between devices: 24.1 us -> 18.7 us
  waiting for transfers between devices: 7.59 us -> 11.1 us
  Pallas kernels: 14.5 us -> 13 us
    all_to_all x3 -> x1, starting transfers between devices: 22 us -> 10.3 us  [exchange(): lax.all_to_all(block, 'expert', split_axis=0, concat_axis=0, tiled=True,...]
    ppermute x1 -> x6, waiting for transfers between devices: 0.01 us -> 8.37 us  [the longest x3 5.13 us: kernels(): lax.ppermute(block, 'expert', [(i, i ^ column) for i in range(n)])]
    ppermute x1 -> x6, starting transfers between devices: 1.99 us -> 8.25 us  [the longest x3 4.63 us: kernels(): crossed.append(lax.ppermute(merged.astype(jnp.bfloat16), 'expert', pairs))]
    all_to_all x3 -> x1, waiting for transfers between devices: 5.04 us -> 0.19 us  [exchange(): lax.all_to_all(block, 'expert', split_axis=0, concat_axis=0, tiled=True,...]
    pallas_call x2 -> x3, Pallas kernels: 8.96 us -> 7.45 us  [partials(): pl.pallas_call(functools.partial(partial_kernel, rows=rows, experts=exper...]
  transfers between devices with their start and end apart: 6 -> 9, of which waited for: 5 -> 9; matrix products, arithmetic and copies ran while one was open for 0% -> 0% of each run, Pallas kernels for 18% -> 17%
where the time goes in v5:
time: 44 us; the launch traced here: 43.7 us
  starting transfers between devices  18.7 us (42%)
  Pallas kernels  13 us (30%)
  waiting for transfers between devices  11.1 us (25%)
  between operations  0.73 us (2%)
    all_to_all x1, starting transfers between devices, exchange(): lax.all_to_all(block, 'expert', split_axis=0, concat_axis=0, tiled=True,...  10.3 us
    pallas_call x3, Pallas kernels, partials(): pl.pallas_call(functools.partial(partial_kernel, rows=rows, experts=exper...  7.45 us
    ppermute x3, waiting for transfers between devices, kernels(): lax.ppermute(block, 'expert', [(i, i ^ column) for i in range(n)])  5.13 us
    ppermute x3, starting transfers between devices, kernels(): crossed.append(lax.ppermute(merged.astype(jnp.bfloat16), 'expert', pairs))  4.63 us
    ppermute x3, starting transfers between devices, kernels(): lax.ppermute(block, 'expert', [(i, i ^ column) for i in range(n)])  3.62 us
    ppermute x3, waiting for transfers between devices, kernels(): crossed.append(lax.ppermute(merged.astype(jnp.bfloat16), 'expert', pairs))  3.24 us
    pallas_call x1, Pallas kernels, hold(): pl.pallas_call(largest_kernel, out_shape=(pltpu.VMEM((kept, depth, ff), w...  3.17 us
    pallas_call x1, Pallas kernels, pack(): pl.pallas_call(pack_kernel, out_shape=pltpu.HBM(shape, jnp.bfloat16), in_...  1.73 us
  transfers between devices with their start and end apart: 9, of which 9 were waited for; matrix products, arithmetic and copies ran while one was open for 0% of the time, Pallas kernels for 17%

profile of v5, /device:TPU:0, one launch (start us, length us, event | category | flops | bytes accessed | tf_op | source)
XLA Modules:
  0.0 43.7 jit_solution(1429405619851066215)
XLA Ops:
  0.6 1.7 %shard_map.59 = bf16[16,40,128]{2,1,0:T(8,128)(2,1)} custom-call(bf16[32,4096]{1,0:T(8,128)(2,1)} %tokens_ref.1, s32[8,32]{1,0:T(8,128)} %bitcast.14, f32[8,32]{1,0:T(8,128)} %bitcast.15), custom_call_target="tpu_custom_call" | custom-call | tf_op jit(solution)/shard_map/pallas_call | solution.py:77
  2.4 10.3 %all-to-all-start = ((bf16[16,40,128]{2,1,0:T(8,128)(2,1)}), bf16[16,40,128]{2,1,0:T(8,128)(2,1)S(1)}, u32[]{:S(2)}, u32[]{:S(2)}) async-start(bf16[16,40,128]{2,1,0:T(8,128)(2,1)} %shard_map.59), calls=%async_computation | async-start | bytes 327680 | tf_op jit(solution)/shard_map/all_to_all | solution.py:305
  12.7 3.2 %shard_map.60 = (bf16[8,256,768]{2,1,0:T(8,128)(2,1)S(1)}, f32[16,128]{1,0:T(8,128)S(1)}) custom-call(bf16[16,256,768]{2,1,0:T(8,128)(2,1)} %weight_ref.1), custom_call_target="tpu_custom_call" | custom-call | flops 6291456 | bytes 6291456 | tf_op jit(solution)/shard_map/pallas_call | solution.py:113
  15.9 0.1 collective-permute-start
  16.0 1.2 %collective-permute-done = f32[16,128]{1,0:T(8,128)S(1)} collective-permute-done((f32[16,128]{1,0:T(8,128)S(1)}, f32[16,128]{1,0:T(8,128)S(1)}, u32[]{:S(2)}, u32[]{:S(2)}) %collective-permute-start) | collective-permute-done | bytes 8224 | tf_op jit(solution)/shard_map/ppermute | solution.py:312
  17.1 0.2 all-to-all-done.refs_0_
  17.3 1.4 %collective-permute-done.1.refs_1_ = bf16[16,40,128]{2,1,0:T(8,128)(2,1)S(1)} collective-permute-done((bf16[16,40,128]{2,1,0:T(8,128)(2,1)S(1)}, bf16[16,40,128]{2,1,0:T(8,128)(2,1)S(1)}, u32[]{:S(2)}, u32[]{:S(2)}) %collective-permute-start.1) | collective-permute-done | bytes 163872 | tf_op jit(solution)/shard_map/ppermute | solution.py:324
  18.7 3.3 %shard_map.61 = (bf16[2048,768]{1,0:T(8,128)(2,1)S(1)}, bf16[136,768]{1,0:T(8,128)(2,1)}) custom-call(bf16[16,40,128]{2,1,0:T(8,128)(2,1)S(1)} %all-to-all-done.refs_0_, bf16[16,40,128]{2,1,0:T(8,128)(2,1)S(1)} %collective-permute-done.1.refs_1_, f32[16,128]{1,0:T(8,128)S(1)} %max.45.refs_2_, bf16[2048,768]{1,0:T(8,128)(2,1)S(1)} %bitcast.10, ...), custom_call_target="tpu_custom_call" | custom-call | flops 805306368 | bytes 6291456 | tf_op jit(solution)/shard_map/pallas_call | solution.py:253
  22.1 2.2 %collective-permute-start.4 = (bf16[136,768]{1,0:T(8,128)(2,1)}, bf16[136,768]{1,0:T(8,128)(2,1)S(1)}, u32[]{:S(2)}, u32[]{:S(2)}) collective-permute-start(bf16[136,768]{1,0:T(8,128)(2,1)} %get-tuple-element.23), channel_id=1, source_target_pairs={{0,6},{2,4},{4,2},{6,0},{8,14},{10,12},{12,10},{14,8},{16,22},{18,... | collective-permute-start | bytes 626696 | tf_op jit(solution)/shard_map/ppermute | solution.py:331
  24.3 2.9 %shard_map.63 = (bf16[136,768]{1,0:T(8,128)(2,1)}, bf16[136,768]{1,0:T(8,128)(2,1)}) custom-call(bf16[16,40,128]{2,1,0:T(8,128)(2,1)S(1)} %all-to-all-done.refs_0_, bf16[16,40,128]{2,1,0:T(8,128)(2,1)S(1)} %collective-permute-done.1.refs_1_, f32[16,128]{1,0:T(8,128)S(1)} %max.45.refs_2_, bf16[2048,768]{1,0:T(8,128)(2,1)S(1)} %bitcast.11, ...), custom_call_target="tpu_custom_call" | custom-call | flops 1610612736 | bytes 6291456 | tf_op jit(solution)/shard_map/pallas_call | solution.py:253
  27.2 0.6 %collective-permute-start.2 = (bf16[136,768]{1,0:T(8,128)(2,1)}, bf16[136,768]{1,0:T(8,128)(2,1)S(1)}, u32[]{:S(2)}, u32[]{:S(2)}) collective-permute-start(bf16[136,768]{1,0:T(8,128)(2,1)} %get-tuple-element.21), channel_id=1, source_target_pairs={{0,2},{2,0},{4,6},{6,4},{8,10},{10,8},{12,14},{14,12},{16,18},{18,... | collective-permute-start | bytes 626696 | tf_op jit(solution)/shard_map/ppermute | solution.py:331
  27.8 0.8 %collective-permute-start.3 = (bf16[136,768]{1,0:T(8,128)(2,1)}, bf16[136,768]{1,0:T(8,128)(2,1)S(1)}, u32[]{:S(2)}, u32[]{:S(2)}) collective-permute-start(bf16[136,768]{1,0:T(8,128)(2,1)} %get-tuple-element.22), channel_id=1, source_target_pairs={{0,4},{2,6},{4,0},{6,2},{8,12},{10,14},{12,8},{14,10},{16,20},{18,... | collective-permute-start | bytes 626696 | tf_op jit(solution)/shard_map/ppermute | solution.py:331
  28.6 1.2 %shard_map.62 = (f32[128,768]{1,0:T(8,128)S(1)}, f32[8,128]{1,0:T(8,128)S(1)}) custom-call(bf16[16,40,128]{2,1,0:T(8,128)(2,1)S(1)} %all-to-all-done.refs_0_, bf16[16,40,128]{2,1,0:T(8,128)(2,1)S(1)} %collective-permute-done.1.refs_1_, f32[16,128]{1,0:T(8,128)S(1)} %max.45.refs_2_, bf16[2048,768]{1,0:T(8,128)(2,1)S(1)} %bitcast.12, ...), custom_call_target="tpu_custom_call" | custom-call | flops 805306368 | bytes 6291456 | tf_op jit(solution)/shard_map/pallas_call | solution.py:253
  29.8 0.9 %collective-permute-done.4.refs_2_ = bf16[136,768]{1,0:T(8,128)(2,1)S(1)} collective-permute-done((bf16[136,768]{1,0:T(8,128)(2,1)}, bf16[136,768]{1,0:T(8,128)(2,1)S(1)}, u32[]{:S(2)}, u32[]{:S(2)}) %collective-permute-start.4) | collective-permute-done | bytes 208928 | tf_op jit(solution)/shard_map/ppermute | solution.py:331
  30.7 4.0 %collective-permute-done.2.refs_0_ = bf16[136,768]{1,0:T(8,128)(2,1)S(1)} collective-permute-done((bf16[136,768]{1,0:T(8,128)(2,1)}, bf16[136,768]{1,0:T(8,128)(2,1)S(1)}, u32[]{:S(2)}, u32[]{:S(2)}) %collective-permute-start.2) | collective-permute-done | bytes 208928 | tf_op jit(solution)/shard_map/ppermute | solution.py:331
  34.7 0.2 collective-permute-done.3.refs_1_
  35.0 0.1 add_convert_fusion
  35.1 0.8 %collective-permute-start.5 = (bf16[32,896]{1,0:T(8,128)(2,1)S(1)}, bf16[32,896]{1,0:T(8,128)(2,1)S(1)}, u32[]{:S(2)}, u32[]{:S(2)}) collective-permute-start(bf16[32,896]{1,0:T(8,128)(2,1)S(1)} %pad_maximum_fusion), channel_id=1, source_target_pairs={{0,8},{2,10},{4,12},{6,14},{8,16},{10,18},{12,20},{14,22},{16,24},... | collective-permute-start | bytes 172040 | tf_op jit(solution)/shard_map/ppermute | solution.py:345
  35.9 2.4 %collective-permute-start.6 = (bf16[32,896]{1,0:T(8,128)(2,1)S(1)}, bf16[32,896]{1,0:T(8,128)(2,1)S(1)}, u32[]{:S(2)}, u32[]{:S(2)}) collective-permute-start(bf16[32,896]{1,0:T(8,128)(2,1)S(1)} %pad_maximum_fusion.1), channel_id=1, source_target_pairs={{0,16},{2,18},{4,20},{6,22},{8,24},{10,26},{12,28},{14,30},{16,0},... | collective-permute-start | bytes 172040 | tf_op jit(solution)/shard_map/ppermute | solution.py:345
  38.3 1.5 %collective-permute-start.7 = (bf16[32,896]{1,0:T(8,128)(2,1)S(1)}, bf16[32,896]{1,0:T(8,128)(2,1)S(1)}, u32[]{:S(2)}, u32[]{:S(2)}) collective-permute-start(bf16[32,896]{1,0:T(8,128)(2,1)S(1)} %pad_maximum_fusion.2), channel_id=1, source_target_pairs={{0,24},{2,26},{4,28},{6,30},{8,0},{10,2},{12,4},{14,6},{16,8},{18,... | collective-permute-start | bytes 172040 | tf_op jit(solution)/shard_map/ppermute | solution.py:345
  39.8 1.6 %collective-permute-done.5.refs_3_ = bf16[32,896]{1,0:T(8,128)(2,1)S(1)} collective-permute-done((bf16[32,896]{1,0:T(8,128)(2,1)S(1)}, bf16[32,896]{1,0:T(8,128)(2,1)S(1)}, u32[]{:S(2)}, u32[]{:S(2)}) %collective-permute-start.5) | collective-permute-done | bytes 57376 | tf_op jit(solution)/shard_map/ppermute | solution.py:345
  41.4 1.6 %collective-permute-done.6.refs_4_ = bf16[32,896]{1,0:T(8,128)(2,1)S(1)} collective-permute-done((bf16[32,896]{1,0:T(8,128)(2,1)S(1)}, bf16[32,896]{1,0:T(8,128)(2,1)S(1)}, u32[]{:S(2)}, u32[]{:S(2)}) %collective-permute-start.6) | collective-permute-done | bytes 57376 | tf_op jit(solution)/shard_map/ppermute | solution.py:345
  42.9 0.1 collective-permute-done.7.refs_5_
  43.0 0.7 %shard_map.64 = (bf16[32,768]{1,0:T(8,128)(2,1)}, f32[1]{0:T(128)}) custom-call(f32[128,768]{1,0:T(8,128)S(1)} %get-tuple-element.19.own_ref, f32[8,128]{1,0:T(8,128)S(1)} %get-tuple-element.20.largest_ref, bf16[136,768]{1,0:T(8,128)(2,1)S(1)} %collective-permute-done.2.refs_0_, bf16[136,768]{1,0:T(8,128)(2,1)S(1)} %collective-permute-done.3.refs_1_, ...), custom_call_target="tpu_custom_call" | custom-call | tf_op jit(solution)/shard_map/pallas_call | solution.py:289
  (9 shorter events, 0.1 us)
Async XLA Ops:
  2.4 14.9 %all-to-all-start = ((bf16[16,40,128]{2,1,0:T(8,128)(2,1)}), bf16[16,40,128]{2,1,0:T(8,128)(2,1)S(1)}, u32[]{:S(2)}, u32[]{:S(2)}) async-start(bf16[16,40,128]{2,1,0:T(8,128)(2,1)} %shard_map.59), calls=%async_computation | async-start | bytes 327680 | tf_op jit(solution)/shard_map/all_to_all | solution.py:305
  15.9 1.2 %collective-permute-start = (f32[16,128]{1,0:T(8,128)S(1)}, f32[16,128]{1,0:T(8,128)S(1)}, u32[]{:S(2)}, u32[]{:S(2)}) collective-permute-start(f32[16,128]{1,0:T(8,128)S(1)} %get-tuple-element.14), channel_id=1, source_target_pairs={{0,1},{1,0},{2,3},{3,2},{4,5},{5,4},{6,7},{7,6},{8,9},{9,8},{10,11... | collective-permute-start | bytes 24584 | tf_op jit(solution)/shard_map/ppermute | solution.py:312
  17.3 1.4 %collective-permute-start.1 = (bf16[16,40,128]{2,1,0:T(8,128)(2,1)S(1)}, bf16[16,40,128]{2,1,0:T(8,128)(2,1)S(1)}, u32[]{:S(2)}, u32[]{:S(2)}) collective-permute-start(bf16[16,40,128]{2,1,0:T(8,128)(2,1)S(1)} %all-to-all-done.refs_0_), channel_id=1, source_target_pairs={{0,1},{1,0},{2,3},{3,2},{4,5},{5,4},{6,7},{7,6},{8,9},{9,8},{10,11... | collective-permute-start | bytes 491528 | tf_op jit(solution)/shard_map/ppermute | solution.py:324
  22.1 8.7 %collective-permute-start.4 = (bf16[136,768]{1,0:T(8,128)(2,1)}, bf16[136,768]{1,0:T(8,128)(2,1)S(1)}, u32[]{:S(2)}, u32[]{:S(2)}) collective-permute-start(bf16[136,768]{1,0:T(8,128)(2,1)} %get-tuple-element.23), channel_id=1, source_target_pairs={{0,6},{2,4},{4,2},{6,0},{8,14},{10,12},{12,10},{14,8},{16,22},{18,... | collective-permute-start | bytes 626696 | tf_op jit(solution)/shard_map/ppermute | solution.py:331
  27.2 7.6 %collective-permute-start.2 = (bf16[136,768]{1,0:T(8,128)(2,1)}, bf16[136,768]{1,0:T(8,128)(2,1)S(1)}, u32[]{:S(2)}, u32[]{:S(2)}) collective-permute-start(bf16[136,768]{1,0:T(8,128)(2,1)} %get-tuple-element.21), channel_id=1, source_target_pairs={{0,2},{2,0},{4,6},{6,4},{8,10},{10,8},{12,14},{14,12},{16,18},{18,... | collective-permute-start | bytes 626696 | tf_op jit(solution)/shard_map/ppermute | solution.py:331
  27.8 7.2 %collective-permute-start.3 = (bf16[136,768]{1,0:T(8,128)(2,1)}, bf16[136,768]{1,0:T(8,128)(2,1)S(1)}, u32[]{:S(2)}, u32[]{:S(2)}) collective-permute-start(bf16[136,768]{1,0:T(8,128)(2,1)} %get-tuple-element.22), channel_id=1, source_target_pairs={{0,4},{2,6},{4,0},{6,2},{8,12},{10,14},{12,8},{14,10},{16,20},{18,... | collective-permute-start | bytes 626696 | tf_op jit(solution)/shard_map/ppermute | solution.py:331
  35.1 6.3 %collective-permute-start.5 = (bf16[32,896]{1,0:T(8,128)(2,1)S(1)}, bf16[32,896]{1,0:T(8,128)(2,1)S(1)}, u32[]{:S(2)}, u32[]{:S(2)}) collective-permute-start(bf16[32,896]{1,0:T(8,128)(2,1)S(1)} %pad_maximum_fusion), channel_id=1, source_target_pairs={{0,8},{2,10},{4,12},{6,14},{8,16},{10,18},{12,20},{14,22},{16,24},... | collective-permute-start | bytes 172040 | tf_op jit(solution)/shard_map/ppermute | solution.py:345
  35.9 7.1 %collective-permute-start.6 = (bf16[32,896]{1,0:T(8,128)(2,1)S(1)}, bf16[32,896]{1,0:T(8,128)(2,1)S(1)}, u32[]{:S(2)}, u32[]{:S(2)}) collective-permute-start(bf16[32,896]{1,0:T(8,128)(2,1)S(1)} %pad_maximum_fusion.1), channel_id=1, source_target_pairs={{0,16},{2,18},{4,20},{6,22},{8,24},{10,26},{12,28},{14,30},{16,0},... | collective-permute-start | bytes 172040 | tf_op jit(solution)/shard_map/ppermute | solution.py:345
  38.3 4.7 %collective-permute-start.7 = (bf16[32,896]{1,0:T(8,128)(2,1)S(1)}, bf16[32,896]{1,0:T(8,128)(2,1)S(1)}, u32[]{:S(2)}, u32[]{:S(2)}) collective-permute-start(bf16[32,896]{1,0:T(8,128)(2,1)S(1)} %pad_maximum_fusion.2), channel_id=1, source_target_pairs={{0,24},{2,26},{4,28},{6,30},{8,0},{10,2},{12,4},{14,6},{16,8},{18,... | collective-permute-start | bytes 172040 | tf_op jit(solution)/shard_map/ppermute | solution.py:345

commit v6 on v5

--- a/solution.py
+++ b/solution.py
@@ -143,7 +143,7 @@
     if load:
         weight_ref, (rest_ref, *refs) = rest_ref, refs
     if away:
-        out_refs, (scaled_ref, total_ref, block_ref, sem, out_sem) = refs[:count], refs[count:]
+        out_refs, (scaled_ref, total_ref, sem) = refs[:count], refs[count:]
     else:
         own_ref, largest_ref, scaled_ref, total_ref, sem = refs
     n, _, width = kept_ref.shape
@@ -161,8 +161,8 @@
             value = jnp.broadcast_to(tail_ref[pl.ds(chip, 1), :], (SUBLANES, LANES))
             top = jnp.where(row == plane, value, top)
         if away:
-            block_ref[i, planes * rows :, :LANES] = top.astype(jnp.bfloat16)
-            block_ref[i, planes * rows :, LANES:] = jnp.zeros(
+            out_refs[i][planes * rows :, :LANES] = top.astype(jnp.bfloat16)
+            out_refs[i][planes * rows :, LANES:] = jnp.zeros(
                 (SUBLANES, ff - LANES), jnp.bfloat16
             )
         else:
@@ -184,7 +184,6 @@
             scaled_ref[i * rows : (i + 1) * rows, e * depth : (e + 1) * depth] = (
                 x * gates[:, e : e + 1]
             ).astype(jnp.bfloat16)
-    outs = []
     for i, part in enumerate((held_ref, rest_ref)):
         if load and i == 1:
             fetch.wait()
@@ -201,19 +200,10 @@
             if not away:
                 own_ref[:, at : at + TILE] = product
                 continue
-            lanes = pl.ds(at, TILE)
             for c, out_ref in enumerate(out_refs):
-                block_ref[c, : planes * rows, at : at + TILE] = product[
+                out_ref[: planes * rows, at : at + TILE] = product[
                     c * planes * rows : (c + 1) * planes * rows
                 ].astype(jnp.bfloat16)
-                outs.append(
-                    pltpu.make_async_copy(
-                        block_ref.at[c, :, lanes], out_ref.at[:, lanes], out_sem.at[len(outs)]
-                    )
-                )
-                outs[-1].start()
-    for out in outs:
-        out.wait()
 
 
 def partials(got, tail, weights, rows, experts, columns, load=False):
@@ -226,37 +216,27 @@
     held = pltpu.with_memory_space_constraint(held, pltpu.VMEM)
     rest = pltpu.with_memory_space_constraint(rest, pltpu.HBM if load else pltpu.VMEM)
     operands = (*got, tail, held, rest)
-    out_shape, out_specs = (), ()
-    if load:
-        out_shape += (pltpu.VMEM((deep, ff), rest.dtype),)
-        out_specs += (VMEM,)
+    out_shape = (pltpu.VMEM((deep, ff), rest.dtype),) if load else ()
     scratch = [
         pltpu.VMEM((count, experts * depth), jnp.bfloat16),
         pltpu.VMEM((count, ff), jnp.float32),
+        pltpu.SemaphoreType.DMA,
     ]
     if away:
         shape = (planes * rows + SUBLANES, ff)
-        out_shape += (pltpu.HBM(shape, jnp.bfloat16),) * len(columns)
-        out_specs += (HBM,) * len(columns)
-        scratch += [
-            pltpu.VMEM((len(columns), *shape), jnp.bfloat16),
-            pltpu.SemaphoreType.DMA,
-            pltpu.SemaphoreType.DMA((ff // TILE * len(columns),)),
-        ]
+        out_shape += (jax.ShapeDtypeStruct(shape, jnp.bfloat16),) * len(columns)
     else:
         out_shape += (
             jax.ShapeDtypeStruct((count, ff), jnp.float32),
             jax.ShapeDtypeStruct((SUBLANES, LANES), jnp.float32),
         )
-        out_specs += (VMEM, VMEM)
-        scratch += [pltpu.SemaphoreType.DMA]
     return pl.pallas_call(
         functools.partial(
             partial_kernel, rows=rows, experts=experts, columns=columns, load=load
         ),
         out_shape=out_shape,
         in_specs=[VMEM, VMEM, VMEM, VMEM, HBM if load else VMEM],
-        out_specs=out_specs,
+        out_specs=(VMEM,) * len(out_shape),
         scratch_shapes=scratch,
         compiler_params=params(16),
         cost_estimate=pl.CostEstimate(

time: 44 us -> 42.8 us (0.973)
  Pallas kernels: 13 us -> 11.5 us
    pallas_call x3, Pallas kernels: 7.45 us -> 5.95 us  [partials(): pl.pallas_call(functools.partial(partial_kernel, rows=rows, experts=exper...]
    ppermute x3, waiting for transfers between devices: 5.13 us -> 5.72 us  [kernels(): lax.ppermute(block, 'expert', [(i, i ^ column) for i in range(n)])]
  transfers between devices with their start and end apart: 9 -> 9, of which waited for: 9 -> 9; matrix products, arithmetic and copies ran while one was open for 0% -> 0% of each run, Pallas kernels for 17% -> 15%
where the time goes in v6:
time: 42.8 us; the launch traced here: 42.5 us
  starting transfers between devices  18.7 us (44%)
  Pallas kernels  11.5 us (27%)
  waiting for transfers between devices  11.4 us (27%)
  between operations  0.73 us (2%)
    all_to_all x1, starting transfers between devices, exchange(): lax.all_to_all(block, 'expert', split_axis=0, concat_axis=0, tiled=True,...  10.3 us
    pallas_call x3, Pallas kernels, partials(): pl.pallas_call(functools.partial(partial_kernel, rows=rows, experts=exper...  5.95 us
    ppermute x3, waiting for transfers between devices, kernels(): lax.ppermute(block, 'expert', [(i, i ^ column) for i in range(n)])  5.72 us
    ppermute x3, starting transfers between devices, kernels(): crossed.append(lax.ppermute(merged.astype(jnp.bfloat16), 'expert', pairs))  4.63 us
    ppermute x3, starting transfers between devices, kernels(): lax.ppermute(block, 'expert', [(i, i ^ column) for i in range(n)])  3.62 us
    pallas_call x1, Pallas kernels, hold(): pl.pallas_call(largest_kernel, out_shape=(pltpu.VMEM((kept, depth, ff), w...  3.17 us
    ppermute x3, waiting for transfers between devices, kernels(): crossed.append(lax.ppermute(merged.astype(jnp.bfloat16), 'expert', pairs))  2.95 us
    pallas_call x1, Pallas kernels, pack(): pl.pallas_call(pack_kernel, out_shape=pltpu.HBM(shape, jnp.bfloat16), in_...  1.73 us
  transfers between devices with their start and end apart: 9, of which 9 were waited for; matrix products, arithmetic and copies ran while one was open for 0% of the time, Pallas kernels for 15%

profile of v6, /device:TPU:0, one launch (start us, length us, event | category | flops | bytes accessed | tf_op | source)
XLA Modules:
  0.0 42.5 jit_solution(14625592218657544714)
XLA Ops:
  0.6 1.7 %shard_map.59 = bf16[16,40,128]{2,1,0:T(8,128)(2,1)} custom-call(bf16[32,4096]{1,0:T(8,128)(2,1)} %tokens_ref.1, s32[8,32]{1,0:T(8,128)} %bitcast.14, f32[8,32]{1,0:T(8,128)} %bitcast.15), custom_call_target="tpu_custom_call" | custom-call | tf_op jit(solution)/shard_map/pallas_call | solution.py:77
  2.4 10.3 %all-to-all-start = ((bf16[16,40,128]{2,1,0:T(8,128)(2,1)}), bf16[16,40,128]{2,1,0:T(8,128)(2,1)S(1)}, u32[]{:S(2)}, u32[]{:S(2)}) async-start(bf16[16,40,128]{2,1,0:T(8,128)(2,1)} %shard_map.59), calls=%async_computation | async-start | bytes 327680 | tf_op jit(solution)/shard_map/all_to_all | solution.py:285
  12.7 3.2 %shard_map.60 = (bf16[8,256,768]{2,1,0:T(8,128)(2,1)S(1)}, f32[16,128]{1,0:T(8,128)S(1)}) custom-call(bf16[16,256,768]{2,1,0:T(8,128)(2,1)} %weight_ref.1), custom_call_target="tpu_custom_call" | custom-call | flops 6291456 | bytes 6291456 | tf_op jit(solution)/shard_map/pallas_call | solution.py:113
  15.9 0.1 collective-permute-start
  16.0 1.2 %collective-permute-done = f32[16,128]{1,0:T(8,128)S(1)} collective-permute-done((f32[16,128]{1,0:T(8,128)S(1)}, f32[16,128]{1,0:T(8,128)S(1)}, u32[]{:S(2)}, u32[]{:S(2)}) %collective-permute-start) | collective-permute-done | bytes 8224 | tf_op jit(solution)/shard_map/ppermute | solution.py:292
  17.1 0.2 all-to-all-done.refs_0_
  17.3 1.4 %collective-permute-done.1.refs_1_ = bf16[16,40,128]{2,1,0:T(8,128)(2,1)S(1)} collective-permute-done((bf16[16,40,128]{2,1,0:T(8,128)(2,1)S(1)}, bf16[16,40,128]{2,1,0:T(8,128)(2,1)S(1)}, u32[]{:S(2)}, u32[]{:S(2)}) %collective-permute-start.1) | collective-permute-done | bytes 163872 | tf_op jit(solution)/shard_map/ppermute | solution.py:304
  18.7 2.7 %shard_map.61 = (bf16[2048,768]{1,0:T(8,128)(2,1)S(1)}, bf16[136,768]{1,0:T(8,128)(2,1)S(1)}) custom-call(bf16[16,40,128]{2,1,0:T(8,128)(2,1)S(1)} %all-to-all-done.refs_0_, bf16[16,40,128]{2,1,0:T(8,128)(2,1)S(1)} %collective-permute-done.1.refs_1_, f32[16,128]{1,0:T(8,128)S(1)} %max.45.refs_2_, bf16[2048,768]{1,0:T(8,128)(2,1)S(1)} %bitcast.10, ...), custom_call_target="tpu_custom_call" | custom-call | flops 805306368 | bytes 6291456 | tf_op jit(solution)/shard_map/pallas_call | solution.py:233
  21.4 2.2 %collective-permute-start.4 = (bf16[136,768]{1,0:T(8,128)(2,1)S(1)}, bf16[136,768]{1,0:T(8,128)(2,1)S(1)}, u32[]{:S(2)}, u32[]{:S(2)}) collective-permute-start(bf16[136,768]{1,0:T(8,128)(2,1)S(1)} %get-tuple-element.23), channel_id=1, source_target_pairs={{0,6},{2,4},{4,2},{6,0},{8,14},{10,12},{12,10},{14,8},{16,22},{18,... | collective-permute-start | bytes 626696 | tf_op jit(solution)/shard_map/ppermute | solution.py:311
  23.6 2.1 %shard_map.63 = (bf16[136,768]{1,0:T(8,128)(2,1)S(1)}, bf16[136,768]{1,0:T(8,128)(2,1)S(1)}) custom-call(bf16[16,40,128]{2,1,0:T(8,128)(2,1)S(1)} %all-to-all-done.refs_0_, bf16[16,40,128]{2,1,0:T(8,128)(2,1)S(1)} %collective-permute-done.1.refs_1_, f32[16,128]{1,0:T(8,128)S(1)} %max.45.refs_2_, bf16[2048,768]{1,0:T(8,128)(2,1)S(1)} %bitcast.11, ...), custom_call_target="tpu_custom_call" | custom-call | flops 1610612736 | bytes 6291456 | tf_op jit(solution)/shard_map/pallas_call | solution.py:233
  25.7 0.6 %collective-permute-start.2 = (bf16[136,768]{1,0:T(8,128)(2,1)S(1)}, bf16[136,768]{1,0:T(8,128)(2,1)S(1)}, u32[]{:S(2)}, u32[]{:S(2)}) collective-permute-start(bf16[136,768]{1,0:T(8,128)(2,1)S(1)} %get-tuple-element.21), channel_id=1, source_target_pairs={{0,2},{2,0},{4,6},{6,4},{8,10},{10,8},{12,14},{14,12},{16,18},{18,... | collective-permute-start | bytes 626696 | tf_op jit(solution)/shard_map/ppermute | solution.py:311
  26.3 0.8 %collective-permute-start.3 = (bf16[136,768]{1,0:T(8,128)(2,1)S(1)}, bf16[136,768]{1,0:T(8,128)(2,1)S(1)}, u32[]{:S(2)}, u32[]{:S(2)}) collective-permute-start(bf16[136,768]{1,0:T(8,128)(2,1)S(1)} %get-tuple-element.22), channel_id=1, source_target_pairs={{0,4},{2,6},{4,0},{6,2},{8,12},{10,14},{12,8},{14,10},{16,20},{18,... | collective-permute-start | bytes 626696 | tf_op jit(solution)/shard_map/ppermute | solution.py:311
  27.1 1.2 %shard_map.62 = (f32[128,768]{1,0:T(8,128)S(1)}, f32[8,128]{1,0:T(8,128)S(1)}) custom-call(bf16[16,40,128]{2,1,0:T(8,128)(2,1)S(1)} %all-to-all-done.refs_0_, bf16[16,40,128]{2,1,0:T(8,128)(2,1)S(1)} %collective-permute-done.1.refs_1_, f32[16,128]{1,0:T(8,128)S(1)} %max.45.refs_2_, bf16[2048,768]{1,0:T(8,128)(2,1)S(1)} %bitcast.12, ...), custom_call_target="tpu_custom_call" | custom-call | flops 805306368 | bytes 6291456 | tf_op jit(solution)/shard_map/pallas_call | solution.py:233
  28.3 2.0 %collective-permute-done.4.refs_2_ = bf16[136,768]{1,0:T(8,128)(2,1)S(1)} collective-permute-done((bf16[136,768]{1,0:T(8,128)(2,1)S(1)}, bf16[136,768]{1,0:T(8,128)(2,1)S(1)}, u32[]{:S(2)}, u32[]{:S(2)}) %collective-permute-start.4) | collective-permute-done | bytes 208928 | tf_op jit(solution)/shard_map/ppermute | solution.py:311
  30.4 3.5 %collective-permute-done.2.refs_0_ = bf16[136,768]{1,0:T(8,128)(2,1)S(1)} collective-permute-done((bf16[136,768]{1,0:T(8,128)(2,1)S(1)}, bf16[136,768]{1,0:T(8,128)(2,1)S(1)}, u32[]{:S(2)}, u32[]{:S(2)}) %collective-permute-start.2) | collective-permute-done | bytes 208928 | tf_op jit(solution)/shard_map/ppermute | solution.py:311
  33.8 0.2 collective-permute-done.3.refs_1_
  34.1 0.1 add_convert_fusion
  34.2 0.7 %collective-permute-start.5 = (bf16[32,896]{1,0:T(8,128)(2,1)S(1)}, bf16[32,896]{1,0:T(8,128)(2,1)S(1)}, u32[]{:S(2)}, u32[]{:S(2)}) collective-permute-start(bf16[32,896]{1,0:T(8,128)(2,1)S(1)} %pad_maximum_fusion), channel_id=1, source_target_pairs={{0,8},{2,10},{4,12},{6,14},{8,16},{10,18},{12,20},{14,22},{16,24},... | collective-permute-start | bytes 172040 | tf_op jit(solution)/shard_map/ppermute | solution.py:325
  34.9 2.4 %collective-permute-start.6 = (bf16[32,896]{1,0:T(8,128)(2,1)S(1)}, bf16[32,896]{1,0:T(8,128)(2,1)S(1)}, u32[]{:S(2)}, u32[]{:S(2)}) collective-permute-start(bf16[32,896]{1,0:T(8,128)(2,1)S(1)} %pad_maximum_fusion.1), channel_id=1, source_target_pairs={{0,16},{2,18},{4,20},{6,22},{8,24},{10,26},{12,28},{14,30},{16,0},... | collective-permute-start | bytes 172040 | tf_op jit(solution)/shard_map/ppermute | solution.py:325
  37.4 1.5 %collective-permute-start.7 = (bf16[32,896]{1,0:T(8,128)(2,1)S(1)}, bf16[32,896]{1,0:T(8,128)(2,1)S(1)}, u32[]{:S(2)}, u32[]{:S(2)}) collective-permute-start(bf16[32,896]{1,0:T(8,128)(2,1)S(1)} %pad_maximum_fusion.2), channel_id=1, source_target_pairs={{0,24},{2,26},{4,28},{6,30},{8,0},{10,2},{12,4},{14,6},{16,8},{18,... | collective-permute-start | bytes 172040 | tf_op jit(solution)/shard_map/ppermute | solution.py:325
  38.9 1.8 %collective-permute-done.5.refs_3_ = bf16[32,896]{1,0:T(8,128)(2,1)S(1)} collective-permute-done((bf16[32,896]{1,0:T(8,128)(2,1)S(1)}, bf16[32,896]{1,0:T(8,128)(2,1)S(1)}, u32[]{:S(2)}, u32[]{:S(2)}) %collective-permute-start.5) | collective-permute-done | bytes 57376 | tf_op jit(solution)/shard_map/ppermute | solution.py:325
  40.6 1.0 %collective-permute-done.6.refs_4_ = bf16[32,896]{1,0:T(8,128)(2,1)S(1)} collective-permute-done((bf16[32,896]{1,0:T(8,128)(2,1)S(1)}, bf16[32,896]{1,0:T(8,128)(2,1)S(1)}, u32[]{:S(2)}, u32[]{:S(2)}) %collective-permute-start.6) | collective-permute-done | bytes 57376 | tf_op jit(solution)/shard_map/ppermute | solution.py:325
  41.7 0.1 collective-permute-done.7.refs_5_
  41.8 0.7 %shard_map.64 = (bf16[32,768]{1,0:T(8,128)(2,1)}, f32[1]{0:T(128)}) custom-call(f32[128,768]{1,0:T(8,128)S(1)} %get-tuple-element.19.own_ref, f32[8,128]{1,0:T(8,128)S(1)} %get-tuple-element.20.largest_ref, bf16[136,768]{1,0:T(8,128)(2,1)S(1)} %collective-permute-done.2.refs_0_, bf16[136,768]{1,0:T(8,128)(2,1)S(1)} %collective-permute-done.3.refs_1_, ...), custom_call_target="tpu_custom_call" | custom-call | tf_op jit(solution)/shard_map/pallas_call | solution.py:269
  (9 shorter events, 0.1 us)
Async XLA Ops:
  2.4 14.9 %all-to-all-start = ((bf16[16,40,128]{2,1,0:T(8,128)(2,1)}), bf16[16,40,128]{2,1,0:T(8,128)(2,1)S(1)}, u32[]{:S(2)}, u32[]{:S(2)}) async-start(bf16[16,40,128]{2,1,0:T(8,128)(2,1)} %shard_map.59), calls=%async_computation | async-start | bytes 327680 | tf_op jit(solution)/shard_map/all_to_all | solution.py:285
  15.9 1.2 %collective-permute-start = (f32[16,128]{1,0:T(8,128)S(1)}, f32[16,128]{1,0:T(8,128)S(1)}, u32[]{:S(2)}, u32[]{:S(2)}) collective-permute-start(f32[16,128]{1,0:T(8,128)S(1)} %get-tuple-element.14), channel_id=1, source_target_pairs={{0,1},{1,0},{2,3},{3,2},{4,5},{5,4},{6,7},{7,6},{8,9},{9,8},{10,11... | collective-permute-start | bytes 24584 | tf_op jit(solution)/shard_map/ppermute | solution.py:292
  17.3 1.4 %collective-permute-start.1 = (bf16[16,40,128]{2,1,0:T(8,128)(2,1)S(1)}, bf16[16,40,128]{2,1,0:T(8,128)(2,1)S(1)}, u32[]{:S(2)}, u32[]{:S(2)}) collective-permute-start(bf16[16,40,128]{2,1,0:T(8,128)(2,1)S(1)} %all-to-all-done.refs_0_), channel_id=1, source_target_pairs={{0,1},{1,0},{2,3},{3,2},{4,5},{5,4},{6,7},{7,6},{8,9},{9,8},{10,11... | collective-permute-start | bytes 491528 | tf_op jit(solution)/shard_map/ppermute | solution.py:304
  21.4 9.0 %collective-permute-start.4 = (bf16[136,768]{1,0:T(8,128)(2,1)S(1)}, bf16[136,768]{1,0:T(8,128)(2,1)S(1)}, u32[]{:S(2)}, u32[]{:S(2)}) collective-permute-start(bf16[136,768]{1,0:T(8,128)(2,1)S(1)} %get-tuple-element.23), channel_id=1, source_target_pairs={{0,6},{2,4},{4,2},{6,0},{8,14},{10,12},{12,10},{14,8},{16,22},{18,... | collective-permute-start | bytes 626696 | tf_op jit(solution)/shard_map/ppermute | solution.py:311
  25.7 8.1 %collective-permute-start.2 = (bf16[136,768]{1,0:T(8,128)(2,1)S(1)}, bf16[136,768]{1,0:T(8,128)(2,1)S(1)}, u32[]{:S(2)}, u32[]{:S(2)}) collective-permute-start(bf16[136,768]{1,0:T(8,128)(2,1)S(1)} %get-tuple-element.21), channel_id=1, source_target_pairs={{0,2},{2,0},{4,6},{6,4},{8,10},{10,8},{12,14},{14,12},{16,18},{18,... | collective-permute-start | bytes 626696 | tf_op jit(solution)/shard_map/ppermute | solution.py:311
  26.3 7.7 %collective-permute-start.3 = (bf16[136,768]{1,0:T(8,128)(2,1)S(1)}, bf16[136,768]{1,0:T(8,128)(2,1)S(1)}, u32[]{:S(2)}, u32[]{:S(2)}) collective-permute-start(bf16[136,768]{1,0:T(8,128)(2,1)S(1)} %get-tuple-element.22), channel_id=1, source_target_pairs={{0,4},{2,6},{4,0},{6,2},{8,12},{10,14},{12,8},{14,10},{16,20},{18,... | collective-permute-start | bytes 626696 | tf_op jit(solution)/shard_map/ppermute | solution.py:311
  34.2 6.4 %collective-permute-start.5 = (bf16[32,896]{1,0:T(8,128)(2,1)S(1)}, bf16[32,896]{1,0:T(8,128)(2,1)S(1)}, u32[]{:S(2)}, u32[]{:S(2)}) collective-permute-start(bf16[32,896]{1,0:T(8,128)(2,1)S(1)} %pad_maximum_fusion), channel_id=1, source_target_pairs={{0,8},{2,10},{4,12},{6,14},{8,16},{10,18},{12,20},{14,22},{16,24},... | collective-permute-start | bytes 172040 | tf_op jit(solution)/shard_map/ppermute | solution.py:325
  34.9 6.8 %collective-permute-start.6 = (bf16[32,896]{1,0:T(8,128)(2,1)S(1)}, bf16[32,896]{1,0:T(8,128)(2,1)S(1)}, u32[]{:S(2)}, u32[]{:S(2)}) collective-permute-start(bf16[32,896]{1,0:T(8,128)(2,1)S(1)} %pad_maximum_fusion.1), channel_id=1, source_target_pairs={{0,16},{2,18},{4,20},{6,22},{8,24},{10,26},{12,28},{14,30},{16,0},... | collective-permute-start | bytes 172040 | tf_op jit(solution)/shard_map/ppermute | solution.py:325
  37.4 4.4 %collective-permute-start.7 = (bf16[32,896]{1,0:T(8,128)(2,1)S(1)}, bf16[32,896]{1,0:T(8,128)(2,1)S(1)}, u32[]{:S(2)}, u32[]{:S(2)}) collective-permute-start(bf16[32,896]{1,0:T(8,128)(2,1)S(1)} %pad_maximum_fusion.2), channel_id=1, source_target_pairs={{0,24},{2,26},{4,28},{6,30},{8,0},{10,2},{12,4},{14,6},{16,8},{18,... | collective-permute-start | bytes 172040 | tf_op jit(solution)/shard_map/ppermute | solution.py:325

commit v7 on v6

--- a/solution.py
+++ b/solution.py
@@ -10,9 +10,14 @@
 LANES = 128
 SUBLANES = 8
 PLANE = 4
+SENT = (1, 3)
 VMEM = pl.BlockSpec(memory_space=pltpu.VMEM)
 HBM = pl.BlockSpec(memory_space=pltpu.HBM)
 TILE = 256
+
+
+def flipped(index, n):
+    return index ^ (n // 2 - 1)
 
 
 def params(mebibytes):
@@ -31,7 +36,7 @@
     ]
     copies += [
         pltpu.make_async_copy(
-            tokens_ref.at[:, pl.ds(pl.multiple_of((2 * (n - 1 - i) + core) * width, LANES), width)],
+            tokens_ref.at[:, pl.ds(pl.multiple_of((2 * flipped(i, n) + core) * width, LANES), width)],
             block_ref.at[i, pl.ds(0, rows)],
             sem.at[i],
         )
@@ -129,47 +134,40 @@
     )(pltpu.with_memory_space_constraint(weights, pltpu.HBM))
 
 
-def place(column, plane):
-    index = lax.axis_index("expert")
-    planes = lax.axis_size("expert") // PLANE
-    beyond = lax.rem(lax.div(index, PLANE) + plane, planes)
-    return beyond * PLANE + jnp.bitwise_xor(lax.rem(index, PLANE), column)
-
-
-def partial_kernel(*refs, rows, experts, columns, load):
+def place(role, plane):
+    index, core = lax.axis_index("expert"), lax.axis_index("tensor")
+    beyond = jnp.bitwise_xor(lax.div(index, PLANE), plane)
+    away = {0: 0, 1: 1 + core, 2: 2 - core, 3: 3}[role]
+    return beyond * PLANE + jnp.bitwise_xor(lax.rem(index, PLANE), away)
+
+
+def partial_kernel(*refs, rows, experts, roles):
     kept_ref, swapped_ref, tail_ref, held_ref, rest_ref, *refs = refs
-    away = columns != (0,)
-    count = len(columns)
-    if load:
-        weight_ref, (rest_ref, *refs) = rest_ref, refs
-    if away:
-        out_refs, (scaled_ref, total_ref, sem) = refs[:count], refs[count:]
-    else:
-        own_ref, largest_ref, scaled_ref, total_ref, sem = refs
+    *out_refs, scaled_ref, total_ref = refs
     n, _, width = kept_ref.shape
     ff, depth, planes = held_ref.shape[1], 2 * width, n // PLANE
-    chips = [[place(column, plane) for plane in range(planes)] for column in columns]
+    chips = [[place(role, plane) for plane in range(planes)] for role in roles]
     left = lax.axis_index("tensor") == 0
     deep = experts // 2 * depth
-    if load:
-        fetch = pltpu.make_async_copy(weight_ref.at[pl.ds(deep, deep)], rest_ref, sem)
-        fetch.start()
-    for i, column in enumerate(chips):
+    blocks = []
+    for role, column in zip(roles, chips):
         row = lax.broadcasted_iota(jnp.int32, (SUBLANES, LANES), 0)
         top = jnp.zeros((SUBLANES, LANES), jnp.float32)
         for plane, chip in enumerate(column):
             value = jnp.broadcast_to(tail_ref[pl.ds(chip, 1), :], (SUBLANES, LANES))
             top = jnp.where(row == plane, value, top)
-        if away:
-            out_refs[i][planes * rows :, :LANES] = top.astype(jnp.bfloat16)
-            out_refs[i][planes * rows :, LANES:] = jnp.zeros(
+        blocks.append(out_refs.pop(0))
+        if role in SENT:
+            blocks[-1][planes * rows :, :LANES] = top.astype(jnp.bfloat16)
+            blocks[-1][planes * rows :, LANES:] = jnp.zeros(
                 (SUBLANES, ff - LANES), jnp.bfloat16
             )
         else:
-            largest_ref[...] = top
+            out_refs.pop(0)[...] = top
     for i, chip in enumerate([chip for column in chips for chip in column]):
-        kept = kept_ref[n - 1 - chip].astype(jnp.float32)
-        swapped = swapped_ref[n - 1 - chip, :rows].astype(jnp.float32)
+        at = flipped(chip, n)
+        kept = kept_ref[at].astype(jnp.float32)
+        swapped = swapped_ref[at, :rows].astype(jnp.float32)
         own = kept[:rows]
         x = jnp.concatenate([jnp.where(left, own, swapped), jnp.where(left, swapped, own)], axis=1)
         packed = kept[rows:]
@@ -185,8 +183,6 @@
                 x * gates[:, e : e + 1]
             ).astype(jnp.bfloat16)
     for i, part in enumerate((held_ref, rest_ref)):
-        if load and i == 1:
-            fetch.wait()
         for at in range(0, ff, TILE):
             product = jnp.dot(
                 scaled_ref[:, i * deep : (i + 1) * deep],
@@ -197,59 +193,47 @@
                 total_ref[:, at : at + TILE] = product
                 continue
             product += total_ref[:, at : at + TILE]
-            if not away:
-                own_ref[:, at : at + TILE] = product
-                continue
-            for c, out_ref in enumerate(out_refs):
-                out_ref[: planes * rows, at : at + TILE] = product[
+            for c, block in enumerate(blocks):
+                block[: planes * rows, at : at + TILE] = product[
                     c * planes * rows : (c + 1) * planes * rows
-                ].astype(jnp.bfloat16)
-
-
-def partials(got, tail, weights, rows, experts, columns, load=False):
+                ].astype(block.dtype)
+
+
+def partials(got, tail, weights, rows, experts, roles):
     n, _, width = got[0].shape
     depth, planes = 2 * width, n // PLANE
-    held, rest = weights
-    deep, ff = held.shape
-    away = columns != (0,)
-    count = planes * rows * len(columns)
-    held = pltpu.with_memory_space_constraint(held, pltpu.VMEM)
-    rest = pltpu.with_memory_space_constraint(rest, pltpu.HBM if load else pltpu.VMEM)
-    operands = (*got, tail, held, rest)
-    out_shape = (pltpu.VMEM((deep, ff), rest.dtype),) if load else ()
-    scratch = [
-        pltpu.VMEM((count, experts * depth), jnp.bfloat16),
-        pltpu.VMEM((count, ff), jnp.float32),
-        pltpu.SemaphoreType.DMA,
-    ]
-    if away:
-        shape = (planes * rows + SUBLANES, ff)
-        out_shape += (jax.ShapeDtypeStruct(shape, jnp.bfloat16),) * len(columns)
-    else:
-        out_shape += (
-            jax.ShapeDtypeStruct((count, ff), jnp.float32),
-            jax.ShapeDtypeStruct((SUBLANES, LANES), jnp.float32),
-        )
+    deep, ff = weights[0].shape
+    count = planes * rows * len(roles)
+    held, rest = (pltpu.with_memory_space_constraint(part, pltpu.VMEM) for part in weights)
+    out_shape = ()
+    for role in roles:
+        if role in SENT:
+            out_shape += (jax.ShapeDtypeStruct((planes * rows + SUBLANES, ff), jnp.bfloat16),)
+        else:
+            out_shape += (
+                jax.ShapeDtypeStruct((planes * rows, ff), jnp.float32),
+                jax.ShapeDtypeStruct((SUBLANES, LANES), jnp.float32),
+            )
     return pl.pallas_call(
-        functools.partial(
-            partial_kernel, rows=rows, experts=experts, columns=columns, load=load
-        ),
+        functools.partial(partial_kernel, rows=rows, experts=experts, roles=roles),
         out_shape=out_shape,
-        in_specs=[VMEM, VMEM, VMEM, VMEM, HBM if load else VMEM],
+        in_specs=[VMEM] * 5,
         out_specs=(VMEM,) * len(out_shape),
-        scratch_shapes=scratch,
+        scratch_shapes=[
+            pltpu.VMEM((count, experts * depth), jnp.bfloat16),
+            pltpu.VMEM((count, ff), jnp.float32),
+        ],
         compiler_params=params(16),
         cost_estimate=pl.CostEstimate(
             flops=2 * count * experts * depth * ff,
             bytes_accessed=4 * held.size,
             transcendentals=0,
         ),
-    )(*operands)
+    )(*got, tail, held, rest)
 
 
 def finish_kernel(own_ref, largest_ref, *refs, planes):
-    plane_refs, crossed_refs = refs[: PLANE - 1], refs[PLANE - 1 : -2]
-    out_ref, top_ref = refs[-2:]
+    plane_refs, (*crossed_refs, out_ref, top_ref) = refs[:2], refs[2:]
     rows, ff = out_ref.shape
     total = own_ref[:rows]
     top = largest_ref[:1]
@@ -278,12 +262,11 @@
     )(*operands)
 
 
-def exchange(block, parts):
+def exchange(block):
     n = lax.axis_size("expert")
-    size = n // parts
-    groups = [list(range(first + size - 1, first - 1, -1)) for first in range(0, n, size)]
+    order = [flipped(i, n) for i in range(n)]
     return lax.all_to_all(
-        block, "expert", split_axis=0, concat_axis=0, tiled=True, axis_index_groups=groups
+        block, "expert", split_axis=0, concat_axis=0, tiled=True, axis_index_groups=[order]
     )
 
 
@@ -297,23 +280,31 @@
     n = lax.axis_size("expert")
     rows = tokens.shape[0]
     experts, depth, ff = learner_weights.shape
-    got = exchange(pack(tokens, routes, route_weights, n, depth // 2), 1)
+    got = exchange(pack(tokens, routes, route_weights, n, depth // 2))
     held, largest = hold(learner_weights)
     largest = over_tensor(largest)
-    got, held, largest = lax.optimization_barrier((got, held, largest))
+    weight = learner_weights.reshape(experts * depth, ff)
+    held = held.reshape(-1, ff)
+    got, held, largest, weight = lax.optimization_barrier((got, held, largest, weight))
     got = (got, lax.ppermute(got, "tensor", [(0, 1), (1, 0)]))
-    held = held.reshape(-1, ff)
-    weight = learner_weights.reshape(experts * depth, ff)
-    rest, far = partials(got, largest, (held, weight), rows, experts, (3,), load=True)
-    side, front = partials(got, largest, (held, rest), rows, experts, (1, 2))
+    rest = weight[held.shape[0] :]
+    (across,) = partials(got, largest, (held, rest), rows, experts, (3,))
+    second, second_largest, first = partials(got, largest, (held, rest), rows, experts, (2, 1))
     own, own_largest = partials(got, largest, (held, rest), rows, experts, (0,))
-    near = [
-        lax.ppermute(block, "expert", [(i, i ^ column) for i in range(n)])
-        for column, block in ((1, side), (2, front), (3, far))
-    ]
+
+    def over_link(block, step):
+        links = [(1 + core, 2 - core)[step] for core in range(2)]
+        pairs = [(2 * i + c, 2 * (i ^ links[c]) + c) for i in range(n) for c in range(2)]
+        return lax.ppermute(block, ("expert", "tensor"), pairs)
+
+    across = over_link(across, 0).astype(jnp.float32)
+    end = n // PLANE * rows
+    maxima = jnp.pad(second_largest, ((0, 0), (0, ff - LANES)))
+    relay = jnp.concatenate([across[:end] + second, jnp.maximum(across[end:], maxima)])
+    near = [over_link(relay.astype(jnp.bfloat16), 1), over_link(first, 0)]
     planes = n // PLANE
     crossed = []
-    for plane in range(1, planes):
+    for plane in sorted(range(1, planes), key=lambda plane: (plane != 2, plane)):
         begin = plane * rows
         total = own[begin : begin + rows]
         top = own_largest[plane]
@@ -321,7 +312,7 @@
             total += block[begin : begin + rows].astype(jnp.float32)
             top = jnp.maximum(top, block[planes * rows + plane, :LANES].astype(jnp.float32))
         merged = jnp.concatenate([total, jnp.broadcast_to(top, (rows, LANES))], axis=1)
-        pairs = [(i, (i + plane * PLANE) % n) for i in range(n)]
+        pairs = [(i, i ^ (plane * PLANE)) for i in range(n)]
         crossed.append(lax.ppermute(merged.astype(jnp.bfloat16), "expert", pairs))
     return finish(own, own_largest, near, crossed, rows)
 
@@ -335,11 +326,10 @@
     gate = jnp.sum(jnp.where(chosen, route_weights[:, :, None], 0.0), axis=1)
     high = lax.reduce_precision(gate, 8, 7)
     terms = jnp.concatenate([high, gate - high], axis=1).astype(jnp.bfloat16)
-    columns = tokens.reshape(rows, n, depth).transpose(1, 0, 2)[::-1]
-    top = jnp.broadcast_to(largest[::-1, None, None], (n, rows, 1))
-    got = exchange(
-        jnp.concatenate([columns, jnp.broadcast_to(terms, (n, *terms.shape)), top], axis=2), 1
-    )
+    columns = tokens.reshape(rows, n, depth).transpose(1, 0, 2)
+    top = jnp.broadcast_to(largest[:, None, None], (n, rows, 1))
+    got = jnp.concatenate([columns, jnp.broadcast_to(terms, (n, *terms.shape)), top], axis=2)
+    got = lax.all_to_all(got, "expert", split_axis=0, concat_axis=0, tiled=True)
     weight = learner_weights.reshape(experts * depth, ff)
 
     def one(block):
@@ -351,7 +341,8 @@
         )
         return product.astype(jnp.bfloat16)
 
-    back = exchange(lax.map(one, got), 1)
+    back = lax.map(one, got)
+    back = lax.all_to_all(back, "expert", split_axis=0, concat_axis=0, tiled=True)
     combined = jnp.sum(back.astype(jnp.float32), axis=0).astype(jnp.bfloat16)
     expert_amax = jnp.max(got[:, 0, depth + 2 * experts]).astype(jnp.float32).reshape(1)
     return (combined, expert_amax)
@@ -360,7 +351,7 @@
 def shards(tokens, routes, route_weights, learner_weights):
     n, rows = lax.axis_size("expert"), tokens.shape[0]
     experts, depth, ff = learner_weights.shape
-    aligned = depth % (2 * LANES) == 0 and ff % TILE == 0 and rows % 32 == 0 and n % PLANE == 0
+    aligned = depth % (2 * LANES) == 0 and ff % TILE == 0 and rows % 32 == 0 and n in (8, 16, 32)
     fits = lax.axis_size("tensor") == 2 and rows // SUBLANES * 2 * experts <= depth // 2
     small = experts * depth * ff <= 4 << 20 and n * rows <= 1024 and n <= PLANE * SUBLANES
     form = kernels if aligned and fits and small and experts == n else plain

time: 42.8 us -> 40.5 us (0.946)
  local copies, waits for them, and re-layouts: 0.02 us -> 2.12 us
  starting transfers between devices: 18.7 us -> 16.8 us
  Pallas kernels: 11.5 us -> 10.1 us
  waiting for transfers between devices: 11.4 us -> 10.3 us
    slice x0 -> x1, local copies, waits for them, and re-layouts: none -> 2.09 us  [kernels(): rest = weight[held.shape[0]:]]
    all_to_all x1, starting transfers between devices: 10.3 us -> 8.8 us  [exchange(): lax.all_to_all(block, 'expert', split_axis=0, concat_axis=0, tiled=True,...]
    pallas_call x3, Pallas kernels: 5.95 us -> 4.51 us  [partials(): pl.pallas_call(functools.partial(partial_kernel, rows=rows, experts=exper...]
    ppermute x1, waiting for transfers between devices: 1.39 us -> 0.01 us  [kernels(): got = (got, lax.ppermute(got, 'tensor', [(0, 1), (1, 0)]))]
    all_to_all x1, waiting for transfers between devices: 0.19 us -> 1.12 us  [exchange(): lax.all_to_all(block, 'expert', split_axis=0, concat_axis=0, tiled=True,...]
    ppermute x3, waiting for transfers between devices: 5.72 us -> 5.09 us  [over_link(): return lax.ppermute(block, ('expert', 'tensor'), pairs)]
  transfers between devices with their start and end apart: 9 -> 9, of which waited for: 9 -> 8; matrix products, arithmetic and copies ran while one was open for 0% -> 6% of each run, Pallas kernels for 15% -> 16%
where the time goes in v7:
time: 40.5 us; the launch traced here: 40.2 us
  starting transfers between devices  16.8 us (41%)
  waiting for transfers between devices  10.3 us (25%)
  Pallas kernels  10.1 us (25%)
  local copies, waits for them, and re-layouts  2.12 us (5%)
  between operations  0.77 us (2%)
    all_to_all x1, starting transfers between devices, exchange(): lax.all_to_all(block, 'expert', split_axis=0, concat_axis=0, tiled=True,...  8.8 us
    ppermute x3, waiting for transfers between devices, over_link(): return lax.ppermute(block, ('expert', 'tensor'), pairs)  5.09 us
    ppermute x3, starting transfers between devices, kernels(): crossed.append(lax.ppermute(merged.astype(jnp.bfloat16), 'expert', pairs))  4.57 us
    pallas_call x3, Pallas kernels, partials(): pl.pallas_call(functools.partial(partial_kernel, rows=rows, experts=exper...  4.51 us
    ppermute x3, starting transfers between devices, over_link(): return lax.ppermute(block, ('expert', 'tensor'), pairs)  3.34 us
    pallas_call x1, Pallas kernels, hold(): pl.pallas_call(largest_kernel, out_shape=(pltpu.VMEM((kept, depth, ff), w...  3.17 us
    ppermute x3, waiting for transfers between devices, kernels(): crossed.append(lax.ppermute(merged.astype(jnp.bfloat16), 'expert', pairs))  2.89 us
    slice x1, local copies, waits for them, and re-layouts, kernels(): rest = weight[held.shape[0]:]  2.09 us
  transfers between devices with their start and end apart: 9, of which 8 were waited for; matrix products, arithmetic and copies ran while one was open for 6% of the time, Pallas kernels for 16%

profile of v7, /device:TPU:0, one launch (start us, length us, event | category | flops | bytes accessed | tf_op | source)
XLA Modules:
  0.0 40.2 jit_solution(7958741159820251601)
XLA Ops:
  0.6 1.7 %shard_map.59 = bf16[16,40,128]{2,1,0:T(8,128)(2,1)} custom-call(bf16[32,4096]{1,0:T(8,128)(2,1)} %tokens_ref.1, s32[8,32]{1,0:T(8,128)} %bitcast.14, f32[8,32]{1,0:T(8,128)} %bitcast.15), custom_call_target="tpu_custom_call" | custom-call | tf_op jit(solution)/shard_map/pallas_call | solution.py:82
  2.4 8.8 %all-to-all-start = ((bf16[16,40,128]{2,1,0:T(8,128)(2,1)}), bf16[16,40,128]{2,1,0:T(8,128)(2,1)S(1)}, u32[]{:S(2)}, u32[]{:S(2)}) async-start(bf16[16,40,128]{2,1,0:T(8,128)(2,1)} %shard_map.59), calls=%async_computation | async-start | bytes 327680 | tf_op jit(solution)/shard_map/all_to_all | solution.py:268
  11.2 3.2 %shard_map.60 = (bf16[8,256,768]{2,1,0:T(8,128)(2,1)S(1)}, f32[16,128]{1,0:T(8,128)S(1)}) custom-call(bf16[16,256,768]{2,1,0:T(8,128)(2,1)} %weight_ref.1), custom_call_target="tpu_custom_call" | custom-call | flops 6291456 | bytes 6291456 | tf_op jit(solution)/shard_map/pallas_call | solution.py:118
  14.3 0.1 collective-permute-start
  14.4 1.2 %collective-permute-done = f32[16,128]{1,0:T(8,128)S(1)} collective-permute-done((f32[16,128]{1,0:T(8,128)S(1)}, f32[16,128]{1,0:T(8,128)S(1)}, u32[]{:S(2)}, u32[]{:S(2)}) %collective-permute-start) | collective-permute-done | bytes 8224 | tf_op jit(solution)/shard_map/ppermute | solution.py:275
  15.6 1.1 %all-to-all-done.refs_0_ = bf16[16,40,128]{2,1,0:T(8,128)(2,1)S(1)} async-done(((bf16[16,40,128]{2,1,0:T(8,128)(2,1)}), bf16[16,40,128]{2,1,0:T(8,128)(2,1)S(1)}, u32[]{:S(2)}, u32[]{:S(2)}) %all-to-all-start) | async-done | bytes 163872 | tf_op jit(solution)/shard_map/all_to_all | solution.py:268
  16.7 2.1 %slice.63.refs_4_ = bf16[2048,768]{1,0:T(8,128)(2,1)S(1)} slice(bf16[4096,768]{1,0:T(8,128)(2,1)} %bitcast.13), slice={[2048:4096], [0:768]} | slice | bytes 6291456 | tf_op jit(solution)/shard_map/slice | solution.py:290
  18.8 1.2 %shard_map.62 = bf16[136,768]{1,0:T(8,128)(2,1)S(1)} custom-call(bf16[16,40,128]{2,1,0:T(8,128)(2,1)S(1)} %all-to-all-done.refs_0_, bf16[16,40,128]{2,1,0:T(8,128)(2,1)S(1)} %collective-permute-done.1.refs_1_, f32[16,128]{1,0:T(8,128)S(1)} %max.36.refs_2_, bf16[2048,768]{1,0:T(8,128)(2,1)S(1)} %bitcast.10, bf16[2048,768]{1,0:T(8,128)(2,1)S(1)} %slice.63.refs_4_), custom_call_target="tpu_custom_call" | custom-call | flops 805306368 | bytes 6291456 | tf_op jit(solution)/shard_map/pallas_call | solution.py:217
  20.1 1.5 %collective-permute-start.2 = (bf16[136,768]{1,0:T(8,128)(2,1)S(1)}, bf16[136,768]{1,0:T(8,128)(2,1)S(1)}, u32[]{:S(2)}, u32[]{:S(2)}) collective-permute-start(bf16[136,768]{1,0:T(8,128)(2,1)S(1)} %shard_map.62), channel_id=1, source_target_pairs={{0,2},{1,5},{2,0},{3,7},{4,6},{5,1},{6,4},{7,3},{8,10},{9,13},{10,... | collective-permute-start | bytes 626696 | tf_op jit(solution)/shard_map/ppermute | solution.py:298
  21.6 2.1 %shard_map.63 = (f32[128,768]{1,0:T(8,128)S(1)}, f32[8,128]{1,0:T(8,128)S(1)}, bf16[136,768]{1,0:T(8,128)(2,1)S(1)}) custom-call(bf16[16,40,128]{2,1,0:T(8,128)(2,1)S(1)} %all-to-all-done.refs_0_, bf16[16,40,128]{2,1,0:T(8,128)(2,1)S(1)} %collective-permute-done.1.refs_1_, f32[16,128]{1,0:T(8,128)S(1)} %max.36.refs_2_, bf16[2048,768]{1,0:T(8,128)(2,1)S(1)} %bitcast.11, ...), custom_call_target="tpu_custom_call" | custom-call | flops 1610612736 | bytes 6291456 | tf_op jit(solution)/shard_map/pallas_call | solution.py:217
  23.7 0.6 %collective-permute-start.4 = (bf16[136,768]{1,0:T(8,128)(2,1)S(1)}, bf16[136,768]{1,0:T(8,128)(2,1)S(1)}, u32[]{:S(2)}, u32[]{:S(2)}) collective-permute-start(bf16[136,768]{1,0:T(8,128)(2,1)S(1)} %get-tuple-element.23), channel_id=1, source_target_pairs={{0,2},{1,5},{2,0},{3,7},{4,6},{5,1},{6,4},{7,3},{8,10},{9,13},{10,... | collective-permute-start | bytes 626696 | tf_op jit(solution)/shard_map/ppermute | solution.py:298
  24.3 1.6 %collective-permute-done.2 = bf16[136,768]{1,0:T(8,128)(2,1)S(1)} collective-permute-done((bf16[136,768]{1,0:T(8,128)(2,1)S(1)}, bf16[136,768]{1,0:T(8,128)(2,1)S(1)}, u32[]{:S(2)}, u32[]{:S(2)}) %collective-permute-start.2) | collective-permute-done | bytes 208928 | tf_op jit(solution)/shard_map/ppermute | solution.py:298
  26.0 1.2 %collective-permute-start.3 = (bf16[136,768]{1,0:T(8,128)(2,1)S(1)}, bf16[136,768]{1,0:T(8,128)(2,1)S(1)}, u32[]{:S(2)}, u32[]{:S(2)}) collective-permute-start(bf16[136,768]{1,0:T(8,128)(2,1)S(1)} %pad_maximum_fusion), channel_id=1, source_target_pairs={{0,4},{1,3},{2,6},{3,1},{4,0},{5,7},{6,2},{7,5},{8,12},{9,11},{10,... | collective-permute-start | bytes 626696 | tf_op jit(solution)/shard_map/ppermute | solution.py:298
  27.2 1.2 %shard_map.61 = (f32[128,768]{1,0:T(8,128)S(1)}, f32[8,128]{1,0:T(8,128)S(1)}) custom-call(bf16[16,40,128]{2,1,0:T(8,128)(2,1)S(1)} %all-to-all-done.refs_0_, bf16[16,40,128]{2,1,0:T(8,128)(2,1)S(1)} %collective-permute-done.1.refs_1_, f32[16,128]{1,0:T(8,128)S(1)} %max.36.refs_2_, bf16[2048,768]{1,0:T(8,128)(2,1)S(1)} %bitcast.12, ...), custom_call_target="tpu_custom_call" | custom-call | flops 805306368 | bytes 6291456 | tf_op jit(solution)/shard_map/pallas_call | solution.py:217
  28.4 2.3 %collective-permute-done.4.refs_1_ = bf16[136,768]{1,0:T(8,128)(2,1)S(1)} collective-permute-done((bf16[136,768]{1,0:T(8,128)(2,1)S(1)}, bf16[136,768]{1,0:T(8,128)(2,1)S(1)}, u32[]{:S(2)}, u32[]{:S(2)}) %collective-permute-start.4) | collective-permute-done | bytes 208928 | tf_op jit(solution)/shard_map/ppermute | solution.py:298
  30.7 1.2 %collective-permute-done.3.refs_0_ = bf16[136,768]{1,0:T(8,128)(2,1)S(1)} collective-permute-done((bf16[136,768]{1,0:T(8,128)(2,1)S(1)}, bf16[136,768]{1,0:T(8,128)(2,1)S(1)}, u32[]{:S(2)}, u32[]{:S(2)}) %collective-permute-start.3) | collective-permute-done | bytes 208928 | tf_op jit(solution)/shard_map/ppermute | solution.py:298
  31.9 0.1 add_convert_fusion
  32.0 1.5 %collective-permute-start.7 = (bf16[32,896]{1,0:T(8,128)(2,1)S(1)}, bf16[32,896]{1,0:T(8,128)(2,1)S(1)}, u32[]{:S(2)}, u32[]{:S(2)}) collective-permute-start(bf16[32,896]{1,0:T(8,128)(2,1)S(1)} %pad_maximum_fusion.3), channel_id=1, source_target_pairs={{0,24},{2,26},{4,28},{6,30},{8,16},{10,18},{12,20},{14,22},{16,8},... | collective-permute-start | bytes 172040 | tf_op jit(solution)/shard_map/ppermute | solution.py:316
  33.5 0.1 collective-permute-start.6
  33.6 3.0 %collective-permute-start.5 = (bf16[32,896]{1,0:T(8,128)(2,1)S(1)}, bf16[32,896]{1,0:T(8,128)(2,1)S(1)}, u32[]{:S(2)}, u32[]{:S(2)}) collective-permute-start(bf16[32,896]{1,0:T(8,128)(2,1)S(1)} %pad_maximum_fusion.1), channel_id=1, source_target_pairs={{0,16},{2,18},{4,20},{6,22},{8,24},{10,26},{12,28},{14,30},{16,0},... | collective-permute-start | bytes 172040 | tf_op jit(solution)/shard_map/ppermute | solution.py:316
  36.7 2.0 %collective-permute-done.7.refs_4_ = bf16[32,896]{1,0:T(8,128)(2,1)S(1)} collective-permute-done((bf16[32,896]{1,0:T(8,128)(2,1)S(1)}, bf16[32,896]{1,0:T(8,128)(2,1)S(1)}, u32[]{:S(2)}, u32[]{:S(2)}) %collective-permute-start.7) | collective-permute-done | bytes 57376 | tf_op jit(solution)/shard_map/ppermute | solution.py:316
  38.7 0.5 %collective-permute-done.6.refs_3_ = bf16[32,896]{1,0:T(8,128)(2,1)S(1)} collective-permute-done((bf16[32,896]{1,0:T(8,128)(2,1)S(1)}, bf16[32,896]{1,0:T(8,128)(2,1)S(1)}, u32[]{:S(2)}, u32[]{:S(2)}) %collective-permute-start.6) | collective-permute-done | bytes 57376 | tf_op jit(solution)/shard_map/ppermute | solution.py:316
  39.2 0.4 collective-permute-done.5.refs_2_
  39.5 0.7 %shard_map.64 = (bf16[32,768]{1,0:T(8,128)(2,1)}, f32[1]{0:T(128)}) custom-call(f32[128,768]{1,0:T(8,128)S(1)} %get-tuple-element.19.own_ref, f32[8,128]{1,0:T(8,128)S(1)} %get-tuple-element.20.largest_ref, bf16[136,768]{1,0:T(8,128)(2,1)S(1)} %collective-permute-done.3.refs_0_, bf16[136,768]{1,0:T(8,128)(2,1)S(1)} %collective-permute-done.4.refs_1_, ...), custom_call_target="tpu_custom_call" | custom-call | tf_op jit(solution)/shard_map/pallas_call | solution.py:253
  (14 shorter events, 0.2 us)
Async XLA Ops:
  2.4 14.3 %all-to-all-start = ((bf16[16,40,128]{2,1,0:T(8,128)(2,1)}), bf16[16,40,128]{2,1,0:T(8,128)(2,1)S(1)}, u32[]{:S(2)}, u32[]{:S(2)}) async-start(bf16[16,40,128]{2,1,0:T(8,128)(2,1)} %shard_map.59), calls=%async_computation | async-start | bytes 327680 | tf_op jit(solution)/shard_map/all_to_all | solution.py:268
  14.3 1.2 %collective-permute-start = (f32[16,128]{1,0:T(8,128)S(1)}, f32[16,128]{1,0:T(8,128)S(1)}, u32[]{:S(2)}, u32[]{:S(2)}) collective-permute-start(f32[16,128]{1,0:T(8,128)S(1)} %get-tuple-element.14), channel_id=1, source_target_pairs={{0,1},{1,0},{2,3},{3,2},{4,5},{5,4},{6,7},{7,6},{8,9},{9,8},{10,11... | collective-permute-start | bytes 24584 | tf_op jit(solution)/shard_map/ppermute | solution.py:275
  16.7 2.1 %collective-permute-start.1 = (bf16[16,40,128]{2,1,0:T(8,128)(2,1)S(1)}, bf16[16,40,128]{2,1,0:T(8,128)(2,1)S(1)}, u32[]{:S(2)}, u32[]{:S(2)}) collective-permute-start(bf16[16,40,128]{2,1,0:T(8,128)(2,1)S(1)} %all-to-all-done.refs_0_), channel_id=1, source_target_pairs={{0,1},{1,0},{2,3},{3,2},{4,5},{5,4},{6,7},{7,6},{8,9},{9,8},{10,11... | collective-permute-start | bytes 491528 | tf_op jit(solution)/shard_map/ppermute | solution.py:289
  20.1 5.9 %collective-permute-start.2 = (bf16[136,768]{1,0:T(8,128)(2,1)S(1)}, bf16[136,768]{1,0:T(8,128)(2,1)S(1)}, u32[]{:S(2)}, u32[]{:S(2)}) collective-permute-start(bf16[136,768]{1,0:T(8,128)(2,1)S(1)} %shard_map.62), channel_id=1, source_target_pairs={{0,2},{1,5},{2,0},{3,7},{4,6},{5,1},{6,4},{7,3},{8,10},{9,13},{10,... | collective-permute-start | bytes 626696 | tf_op jit(solution)/shard_map/ppermute | solution.py:298
  23.7 7.1 %collective-permute-start.4 = (bf16[136,768]{1,0:T(8,128)(2,1)S(1)}, bf16[136,768]{1,0:T(8,128)(2,1)S(1)}, u32[]{:S(2)}, u32[]{:S(2)}) collective-permute-start(bf16[136,768]{1,0:T(8,128)(2,1)S(1)} %get-tuple-element.23), channel_id=1, source_target_pairs={{0,2},{1,5},{2,0},{3,7},{4,6},{5,1},{6,4},{7,3},{8,10},{9,13},{10,... | collective-permute-start | bytes 626696 | tf_op jit(solution)/shard_map/ppermute | solution.py:298
  26.0 5.9 %collective-permute-start.3 = (bf16[136,768]{1,0:T(8,128)(2,1)S(1)}, bf16[136,768]{1,0:T(8,128)(2,1)S(1)}, u32[]{:S(2)}, u32[]{:S(2)}) collective-permute-start(bf16[136,768]{1,0:T(8,128)(2,1)S(1)} %pad_maximum_fusion), channel_id=1, source_target_pairs={{0,4},{1,3},{2,6},{3,1},{4,0},{5,7},{6,2},{7,5},{8,12},{9,11},{10,... | collective-permute-start | bytes 626696 | tf_op jit(solution)/shard_map/ppermute | solution.py:298
  32.0 6.6 %collective-permute-start.7 = (bf16[32,896]{1,0:T(8,128)(2,1)S(1)}, bf16[32,896]{1,0:T(8,128)(2,1)S(1)}, u32[]{:S(2)}, u32[]{:S(2)}) collective-permute-start(bf16[32,896]{1,0:T(8,128)(2,1)S(1)} %pad_maximum_fusion.3), channel_id=1, source_target_pairs={{0,24},{2,26},{4,28},{6,30},{8,16},{10,18},{12,20},{14,22},{16,8},... | collective-permute-start | bytes 172040 | tf_op jit(solution)/shard_map/ppermute | solution.py:316
  33.5 5.7 %collective-permute-start.6 = (bf16[32,896]{1,0:T(8,128)(2,1)S(1)}, bf16[32,896]{1,0:T(8,128)(2,1)S(1)}, u32[]{:S(2)}, u32[]{:S(2)}) collective-permute-start(bf16[32,896]{1,0:T(8,128)(2,1)S(1)} %pad_maximum_fusion.2), channel_id=1, source_target_pairs={{0,8},{2,10},{4,12},{6,14},{8,0},{10,2},{12,4},{14,6},{16,24},{18,... | collective-permute-start | bytes 172040 | tf_op jit(solution)/shard_map/ppermute | solution.py:316
  33.6 5.9 %collective-permute-start.5 = (bf16[32,896]{1,0:T(8,128)(2,1)S(1)}, bf16[32,896]{1,0:T(8,128)(2,1)S(1)}, u32[]{:S(2)}, u32[]{:S(2)}) collective-permute-start(bf16[32,896]{1,0:T(8,128)(2,1)S(1)} %pad_maximum_fusion.1), channel_id=1, source_target_pairs={{0,16},{2,18},{4,20},{6,22},{8,24},{10,26},{12,28},{14,30},{16,0},... | collective-permute-start | bytes 172040 | tf_op jit(solution)/shard_map/ppermute | solution.py:316

commit v8 on v7

--- a/solution.py
+++ b/solution.py
@@ -241,10 +241,13 @@
         total += ref[:rows].astype(jnp.float32)
         maxima = ref[planes * rows :, :LANES].astype(jnp.float32)
         top = jnp.maximum(top, maxima[:1])
+    wide, tall = ff // LANES, rows // SUBLANES
+    tiles = [jnp.zeros((SUBLANES, LANES), jnp.float32)] * (wide * tall)
     for ref in crossed_refs:
-        total += ref[:, :ff].astype(jnp.float32)
-        top = jnp.maximum(top, ref[:, ff:].astype(jnp.float32)[:1])
-    out_ref[...] = total.astype(jnp.bfloat16)
+        tiles = [tile + ref[i].astype(jnp.float32) for i, tile in enumerate(tiles)]
+        top = jnp.maximum(top, ref[wide * tall].astype(jnp.float32)[:1])
+    crossed = [jnp.concatenate(tiles[i * wide : (i + 1) * wide], axis=1) for i in range(tall)]
+    out_ref[...] = (total + jnp.concatenate(crossed)).astype(jnp.bfloat16)
     top_ref[0] = jnp.max(top)
 
 
@@ -311,7 +314,9 @@
         for block in near:
             total += block[begin : begin + rows].astype(jnp.float32)
             top = jnp.maximum(top, block[planes * rows + plane, :LANES].astype(jnp.float32))
-        merged = jnp.concatenate([total, jnp.broadcast_to(top, (rows, LANES))], axis=1)
+        tiles = total.reshape(rows // SUBLANES, SUBLANES, ff // LANES, LANES)
+        tiles = tiles.transpose(0, 2, 1, 3).reshape(-1, SUBLANES, LANES)
+        merged = jnp.concatenate([tiles, jnp.broadcast_to(top, (1, SUBLANES, LANES))])
         pairs = [(i, i ^ (plane * PLANE)) for i in range(n)]
         crossed.append(lax.ppermute(merged.astype(jnp.bfloat16), "expert", pairs))
     return finish(own, own_largest, near, crossed, rows)

time: 40.5 us -> 40.2 us (level)
  no operation moved by 1% of the time
where the time goes in v8:
time: 40.2 us; the launch traced here: 39.9 us
  starting transfers between devices  16.8 us (42%)
  Pallas kernels  10.1 us (25%)
  waiting for transfers between devices  9.97 us (25%)
  local copies, waits for them, and re-layouts  2.1 us (5%)
  between operations  0.77 us (2%)
    all_to_all x1, starting transfers between devices, exchange(): lax.all_to_all(block, 'expert', split_axis=0, concat_axis=0, tiled=True,...  8.8 us
    ppermute x3, waiting for transfers between devices, over_link(): return lax.ppermute(block, ('expert', 'tensor'), pairs)  5.09 us
    ppermute x3, starting transfers between devices, kernels(): crossed.append(lax.ppermute(merged.astype(jnp.bfloat16), 'expert', pairs))  4.56 us
    pallas_call x3, Pallas kernels, partials(): pl.pallas_call(functools.partial(partial_kernel, rows=rows, experts=exper...  4.51 us
    ppermute x3, starting transfers between devices, over_link(): return lax.ppermute(block, ('expert', 'tensor'), pairs)  3.34 us
    pallas_call x1, Pallas kernels, hold(): pl.pallas_call(largest_kernel, out_shape=(pltpu.VMEM((kept, depth, ff), w...  3.17 us
    ppermute x3, waiting for transfers between devices, kernels(): crossed.append(lax.ppermute(merged.astype(jnp.bfloat16), 'expert', pairs))  2.59 us
    slice x1, local copies, waits for them, and re-layouts, kernels(): rest = weight[held.shape[0]:]  2.09 us
  transfers between devices with their start and end apart: 9, of which 8 were waited for; matrix products, arithmetic and copies ran while one was open for 6% of the time, Pallas kernels for 16%

profile of v8, /device:TPU:0, one launch (start us, length us, event | category | flops | bytes accessed | tf_op | source)
XLA Modules:
  0.0 39.9 jit_solution(10443002678464984287)
XLA Ops:
  0.6 1.7 %shard_map.59 = bf16[16,40,128]{2,1,0:T(8,128)(2,1)} custom-call(bf16[32,4096]{1,0:T(8,128)(2,1)} %tokens_ref.1, s32[8,32]{1,0:T(8,128)} %bitcast.32, f32[8,32]{1,0:T(8,128)} %bitcast.33), custom_call_target="tpu_custom_call" | custom-call | tf_op jit(solution)/shard_map/pallas_call | solution.py:82
  2.4 8.8 %all-to-all-start = ((bf16[16,40,128]{2,1,0:T(8,128)(2,1)}), bf16[16,40,128]{2,1,0:T(8,128)(2,1)S(1)}, u32[]{:S(2)}, u32[]{:S(2)}) async-start(bf16[16,40,128]{2,1,0:T(8,128)(2,1)} %shard_map.59), calls=%async_computation | async-start | bytes 327680 | tf_op jit(solution)/shard_map/all_to_all | solution.py:271
  11.2 3.2 %shard_map.60 = (bf16[8,256,768]{2,1,0:T(8,128)(2,1)S(1)}, f32[16,128]{1,0:T(8,128)S(1)}) custom-call(bf16[16,256,768]{2,1,0:T(8,128)(2,1)} %weight_ref.1), custom_call_target="tpu_custom_call" | custom-call | flops 6291456 | bytes 6291456 | tf_op jit(solution)/shard_map/pallas_call | solution.py:118
  14.3 0.1 collective-permute-start
  14.4 1.2 %collective-permute-done = f32[16,128]{1,0:T(8,128)S(1)} collective-permute-done((f32[16,128]{1,0:T(8,128)S(1)}, f32[16,128]{1,0:T(8,128)S(1)}, u32[]{:S(2)}, u32[]{:S(2)}) %collective-permute-start) | collective-permute-done | bytes 8224 | tf_op jit(solution)/shard_map/ppermute | solution.py:278
  15.6 1.1 %all-to-all-done.refs_0_ = bf16[16,40,128]{2,1,0:T(8,128)(2,1)S(1)} async-done(((bf16[16,40,128]{2,1,0:T(8,128)(2,1)}), bf16[16,40,128]{2,1,0:T(8,128)(2,1)S(1)}, u32[]{:S(2)}, u32[]{:S(2)}) %all-to-all-start) | async-done | bytes 163872 | tf_op jit(solution)/shard_map/all_to_all | solution.py:271
  16.7 2.1 %slice.63.refs_4_ = bf16[2048,768]{1,0:T(8,128)(2,1)S(1)} slice(bf16[4096,768]{1,0:T(8,128)(2,1)} %bitcast.28), slice={[2048:4096], [0:768]} | slice | bytes 6291456 | tf_op jit(solution)/shard_map/slice | solution.py:293
  18.8 1.2 %shard_map.62 = bf16[136,768]{1,0:T(8,128)(2,1)S(1)} custom-call(bf16[16,40,128]{2,1,0:T(8,128)(2,1)S(1)} %all-to-all-done.refs_0_, bf16[16,40,128]{2,1,0:T(8,128)(2,1)S(1)} %collective-permute-done.1.refs_1_, f32[16,128]{1,0:T(8,128)S(1)} %max.36.refs_2_, bf16[2048,768]{1,0:T(8,128)(2,1)S(1)} %bitcast.25, bf16[2048,768]{1,0:T(8,128)(2,1)S(1)} %slice.63.refs_4_), custom_call_target="tpu_custom_call" | custom-call | flops 805306368 | bytes 6291456 | tf_op jit(solution)/shard_map/pallas_call | solution.py:217
  20.1 1.5 %collective-permute-start.2 = (bf16[136,768]{1,0:T(8,128)(2,1)S(1)}, bf16[136,768]{1,0:T(8,128)(2,1)S(1)}, u32[]{:S(2)}, u32[]{:S(2)}) collective-permute-start(bf16[136,768]{1,0:T(8,128)(2,1)S(1)} %shard_map.62), channel_id=1, source_target_pairs={{0,2},{1,5},{2,0},{3,7},{4,6},{5,1},{6,4},{7,3},{8,10},{9,13},{10,... | collective-permute-start | bytes 626696 | tf_op jit(solution)/shard_map/ppermute | solution.py:301
  21.6 2.1 %shard_map.63 = (f32[128,768]{1,0:T(8,128)S(1)}, f32[8,128]{1,0:T(8,128)S(1)}, bf16[136,768]{1,0:T(8,128)(2,1)S(1)}) custom-call(bf16[16,40,128]{2,1,0:T(8,128)(2,1)S(1)} %all-to-all-done.refs_0_, bf16[16,40,128]{2,1,0:T(8,128)(2,1)S(1)} %collective-permute-done.1.refs_1_, f32[16,128]{1,0:T(8,128)S(1)} %max.36.refs_2_, bf16[2048,768]{1,0:T(8,128)(2,1)S(1)} %bitcast.26, ...), custom_call_target="tpu_custom_call" | custom-call | flops 1610612736 | bytes 6291456 | tf_op jit(solution)/shard_map/pallas_call | solution.py:217
  23.7 0.6 %collective-permute-start.4 = (bf16[136,768]{1,0:T(8,128)(2,1)S(1)}, bf16[136,768]{1,0:T(8,128)(2,1)S(1)}, u32[]{:S(2)}, u32[]{:S(2)}) collective-permute-start(bf16[136,768]{1,0:T(8,128)(2,1)S(1)} %get-tuple-element.23), channel_id=1, source_target_pairs={{0,2},{1,5},{2,0},{3,7},{4,6},{5,1},{6,4},{7,3},{8,10},{9,13},{10,... | collective-permute-start | bytes 626696 | tf_op jit(solution)/shard_map/ppermute | solution.py:301
  24.3 1.6 %collective-permute-done.2 = bf16[136,768]{1,0:T(8,128)(2,1)S(1)} collective-permute-done((bf16[136,768]{1,0:T(8,128)(2,1)S(1)}, bf16[136,768]{1,0:T(8,128)(2,1)S(1)}, u32[]{:S(2)}, u32[]{:S(2)}) %collective-permute-start.2) | collective-permute-done | bytes 208928 | tf_op jit(solution)/shard_map/ppermute | solution.py:301
  26.0 1.2 %collective-permute-start.3 = (bf16[136,768]{1,0:T(8,128)(2,1)S(1)}, bf16[136,768]{1,0:T(8,128)(2,1)S(1)}, u32[]{:S(2)}, u32[]{:S(2)}) collective-permute-start(bf16[136,768]{1,0:T(8,128)(2,1)S(1)} %pad_maximum_fusion), channel_id=1, source_target_pairs={{0,4},{1,3},{2,6},{3,1},{4,0},{5,7},{6,2},{7,5},{8,12},{9,11},{10,... | collective-permute-start | bytes 626696 | tf_op jit(solution)/shard_map/ppermute | solution.py:301
  27.2 1.2 %shard_map.61 = (f32[128,768]{1,0:T(8,128)S(1)}, f32[8,128]{1,0:T(8,128)S(1)}) custom-call(bf16[16,40,128]{2,1,0:T(8,128)(2,1)S(1)} %all-to-all-done.refs_0_, bf16[16,40,128]{2,1,0:T(8,128)(2,1)S(1)} %collective-permute-done.1.refs_1_, f32[16,128]{1,0:T(8,128)S(1)} %max.36.refs_2_, bf16[2048,768]{1,0:T(8,128)(2,1)S(1)} %bitcast.27, ...), custom_call_target="tpu_custom_call" | custom-call | flops 805306368 | bytes 6291456 | tf_op jit(solution)/shard_map/pallas_call | solution.py:217
  28.4 2.3 %collective-permute-done.4.refs_1_ = bf16[136,768]{1,0:T(8,128)(2,1)S(1)} collective-permute-done((bf16[136,768]{1,0:T(8,128)(2,1)S(1)}, bf16[136,768]{1,0:T(8,128)(2,1)S(1)}, u32[]{:S(2)}, u32[]{:S(2)}) %collective-permute-start.4) | collective-permute-done | bytes 208928 | tf_op jit(solution)/shard_map/ppermute | solution.py:301
  30.7 1.2 %collective-permute-done.3.refs_0_ = bf16[136,768]{1,0:T(8,128)(2,1)S(1)} collective-permute-done((bf16[136,768]{1,0:T(8,128)(2,1)S(1)}, bf16[136,768]{1,0:T(8,128)(2,1)S(1)}, u32[]{:S(2)}, u32[]{:S(2)}) %collective-permute-start.3) | collective-permute-done | bytes 208928 | tf_op jit(solution)/shard_map/ppermute | solution.py:301
  31.9 0.1 add_convert_fusion
  32.0 1.5 %collective-permute-start.7 = (bf16[25,8,128]{2,1,0:T(8,128)(2,1)S(1)}, bf16[25,8,128]{2,1,0:T(8,128)(2,1)S(1)}, u32[]{:S(2)}, u32[]{:S(2)}) collective-permute-start(bf16[25,8,128]{2,1,0:T(8,128)(2,1)S(1)} %pad_maximum_fusion.3), channel_id=1, source_target_pairs={{0,24},{2,26},{4,28},{6,30},{8,16},{10,18},{12,20},{14,22},{16,8},... | collective-permute-start | bytes 153608 | tf_op jit(solution)/shard_map/ppermute | solution.py:321
  33.5 0.1 collective-permute-start.6
  33.6 3.0 %collective-permute-start.5 = (bf16[25,8,128]{2,1,0:T(8,128)(2,1)S(1)}, bf16[25,8,128]{2,1,0:T(8,128)(2,1)S(1)}, u32[]{:S(2)}, u32[]{:S(2)}) collective-permute-start(bf16[25,8,128]{2,1,0:T(8,128)(2,1)S(1)} %pad_maximum_fusion.1), channel_id=1, source_target_pairs={{0,16},{2,18},{4,20},{6,22},{8,24},{10,26},{12,28},{14,30},{16,0},... | collective-permute-start | bytes 153608 | tf_op jit(solution)/shard_map/ppermute | solution.py:321
  36.6 1.9 %collective-permute-done.7.refs_4_ = bf16[25,8,128]{2,1,0:T(8,128)(2,1)S(1)} collective-permute-done((bf16[25,8,128]{2,1,0:T(8,128)(2,1)S(1)}, bf16[25,8,128]{2,1,0:T(8,128)(2,1)S(1)}, u32[]{:S(2)}, u32[]{:S(2)}) %collective-permute-start.7) | collective-permute-done | bytes 51232 | tf_op jit(solution)/shard_map/ppermute | solution.py:321
  38.5 0.3 collective-permute-done.6.refs_3_
  38.8 0.4 collective-permute-done.5.refs_2_
  39.2 0.7 %shard_map.64 = (bf16[32,768]{1,0:T(8,128)(2,1)}, f32[1]{0:T(128)}) custom-call(f32[128,768]{1,0:T(8,128)S(1)} %get-tuple-element.19.own_ref, f32[8,128]{1,0:T(8,128)S(1)} %get-tuple-element.20.largest_ref, bf16[136,768]{1,0:T(8,128)(2,1)S(1)} %collective-permute-done.3.refs_0_, bf16[136,768]{1,0:T(8,128)(2,1)S(1)} %collective-permute-done.4.refs_1_, ...), custom_call_target="tpu_custom_call" | custom-call | tf_op jit(solution)/shard_map/pallas_call | solution.py:256
  (14 shorter events, 0.1 us)
Async XLA Ops:
  2.4 14.3 %all-to-all-start = ((bf16[16,40,128]{2,1,0:T(8,128)(2,1)}), bf16[16,40,128]{2,1,0:T(8,128)(2,1)S(1)}, u32[]{:S(2)}, u32[]{:S(2)}) async-start(bf16[16,40,128]{2,1,0:T(8,128)(2,1)} %shard_map.59), calls=%async_computation | async-start | bytes 327680 | tf_op jit(solution)/shard_map/all_to_all | solution.py:271
  14.3 1.2 %collective-permute-start = (f32[16,128]{1,0:T(8,128)S(1)}, f32[16,128]{1,0:T(8,128)S(1)}, u32[]{:S(2)}, u32[]{:S(2)}) collective-permute-start(f32[16,128]{1,0:T(8,128)S(1)} %get-tuple-element.14), channel_id=1, source_target_pairs={{0,1},{1,0},{2,3},{3,2},{4,5},{5,4},{6,7},{7,6},{8,9},{9,8},{10,11... | collective-permute-start | bytes 24584 | tf_op jit(solution)/shard_map/ppermute | solution.py:278
  16.7 2.1 %collective-permute-start.1 = (bf16[16,40,128]{2,1,0:T(8,128)(2,1)S(1)}, bf16[16,40,128]{2,1,0:T(8,128)(2,1)S(1)}, u32[]{:S(2)}, u32[]{:S(2)}) collective-permute-start(bf16[16,40,128]{2,1,0:T(8,128)(2,1)S(1)} %all-to-all-done.refs_0_), channel_id=1, source_target_pairs={{0,1},{1,0},{2,3},{3,2},{4,5},{5,4},{6,7},{7,6},{8,9},{9,8},{10,11... | collective-permute-start | bytes 491528 | tf_op jit(solution)/shard_map/ppermute | solution.py:292
  20.1 5.9 %collective-permute-start.2 = (bf16[136,768]{1,0:T(8,128)(2,1)S(1)}, bf16[136,768]{1,0:T(8,128)(2,1)S(1)}, u32[]{:S(2)}, u32[]{:S(2)}) collective-permute-start(bf16[136,768]{1,0:T(8,128)(2,1)S(1)} %shard_map.62), channel_id=1, source_target_pairs={{0,2},{1,5},{2,0},{3,7},{4,6},{5,1},{6,4},{7,3},{8,10},{9,13},{10,... | collective-permute-start | bytes 626696 | tf_op jit(solution)/shard_map/ppermute | solution.py:301
  23.7 7.1 %collective-permute-start.4 = (bf16[136,768]{1,0:T(8,128)(2,1)S(1)}, bf16[136,768]{1,0:T(8,128)(2,1)S(1)}, u32[]{:S(2)}, u32[]{:S(2)}) collective-permute-start(bf16[136,768]{1,0:T(8,128)(2,1)S(1)} %get-tuple-element.23), channel_id=1, source_target_pairs={{0,2},{1,5},{2,0},{3,7},{4,6},{5,1},{6,4},{7,3},{8,10},{9,13},{10,... | collective-permute-start | bytes 626696 | tf_op jit(solution)/shard_map/ppermute | solution.py:301
  26.0 5.9 %collective-permute-start.3 = (bf16[136,768]{1,0:T(8,128)(2,1)S(1)}, bf16[136,768]{1,0:T(8,128)(2,1)S(1)}, u32[]{:S(2)}, u32[]{:S(2)}) collective-permute-start(bf16[136,768]{1,0:T(8,128)(2,1)S(1)} %pad_maximum_fusion), channel_id=1, source_target_pairs={{0,4},{1,3},{2,6},{3,1},{4,0},{5,7},{6,2},{7,5},{8,12},{9,11},{10,... | collective-permute-start | bytes 626696 | tf_op jit(solution)/shard_map/ppermute | solution.py:301
  32.0 6.5 %collective-permute-start.7 = (bf16[25,8,128]{2,1,0:T(8,128)(2,1)S(1)}, bf16[25,8,128]{2,1,0:T(8,128)(2,1)S(1)}, u32[]{:S(2)}, u32[]{:S(2)}) collective-permute-start(bf16[25,8,128]{2,1,0:T(8,128)(2,1)S(1)} %pad_maximum_fusion.3), channel_id=1, source_target_pairs={{0,24},{2,26},{4,28},{6,30},{8,16},{10,18},{12,20},{14,22},{16,8},... | collective-permute-start | bytes 153608 | tf_op jit(solution)/shard_map/ppermute | solution.py:321
  33.5 5.3 %collective-permute-start.6 = (bf16[25,8,128]{2,1,0:T(8,128)(2,1)S(1)}, bf16[25,8,128]{2,1,0:T(8,128)(2,1)S(1)}, u32[]{:S(2)}, u32[]{:S(2)}) collective-permute-start(bf16[25,8,128]{2,1,0:T(8,128)(2,1)S(1)} %pad_maximum_fusion.2), channel_id=1, source_target_pairs={{0,8},{2,10},{4,12},{6,14},{8,0},{10,2},{12,4},{14,6},{16,24},{18,... | collective-permute-start | bytes 153608 | tf_op jit(solution)/shard_map/ppermute | solution.py:321
  33.6 5.6 %collective-permute-start.5 = (bf16[25,8,128]{2,1,0:T(8,128)(2,1)S(1)}, bf16[25,8,128]{2,1,0:T(8,128)(2,1)S(1)}, u32[]{:S(2)}, u32[]{:S(2)}) collective-permute-start(bf16[25,8,128]{2,1,0:T(8,128)(2,1)S(1)} %pad_maximum_fusion.1), channel_id=1, source_target_pairs={{0,16},{2,18},{4,20},{6,22},{8,24},{10,26},{12,28},{14,30},{16,0},... | collective-permute-start | bytes 153608 | tf_op jit(solution)/shard_map/ppermute | solution.py:321

commit v9 on v7

--- a/solution.py
+++ b/solution.py
@@ -158,10 +158,7 @@
             top = jnp.where(row == plane, value, top)
         blocks.append(out_refs.pop(0))
         if role in SENT:
-            blocks[-1][planes * rows :, :LANES] = top.astype(jnp.bfloat16)
-            blocks[-1][planes * rows :, LANES:] = jnp.zeros(
-                (SUBLANES, ff - LANES), jnp.bfloat16
-            )
+            blocks[-1][blocks[-1].shape[0] - 1] = top.astype(jnp.bfloat16)
         else:
             out_refs.pop(0)[...] = top
     for i, chip in enumerate([chip for column in chips for chip in column]):
@@ -193,10 +190,16 @@
                 total_ref[:, at : at + TILE] = product
                 continue
             product += total_ref[:, at : at + TILE]
-            for c, block in enumerate(blocks):
-                block[: planes * rows, at : at + TILE] = product[
-                    c * planes * rows : (c + 1) * planes * rows
-                ].astype(block.dtype)
+            for c, (role, block) in enumerate(zip(roles, blocks)):
+                piece = product[c * planes * rows : (c + 1) * planes * rows]
+                if role not in SENT:
+                    block[:, at : at + TILE] = piece
+                    continue
+                for r in range(planes * rows // SUBLANES):
+                    for lane in range(0, TILE, LANES):
+                        block[r * (ff // LANES) + (at + lane) // LANES] = piece[
+                            r * SUBLANES : (r + 1) * SUBLANES, lane : lane + LANES
+                        ].astype(block.dtype)
 
 
 def partials(got, tail, weights, rows, experts, roles):
@@ -208,7 +211,8 @@
     out_shape = ()
     for role in roles:
         if role in SENT:
-            out_shape += (jax.ShapeDtypeStruct((planes * rows + SUBLANES, ff), jnp.bfloat16),)
+            tiles = planes * rows * ff // (SUBLANES * LANES) + 1
+            out_shape += (jax.ShapeDtypeStruct((tiles, SUBLANES, LANES), jnp.bfloat16),)
         else:
             out_shape += (
                 jax.ShapeDtypeStruct((planes * rows, ff), jnp.float32),
@@ -232,26 +236,24 @@
     )(*got, tail, held, rest)
 
 
-def finish_kernel(own_ref, largest_ref, *refs, planes):
+def finish_kernel(own_ref, largest_ref, *refs):
     plane_refs, (*crossed_refs, out_ref, top_ref) = refs[:2], refs[2:]
     rows, ff = out_ref.shape
-    total = own_ref[:rows]
+    wide, tall = ff // LANES, rows // SUBLANES
     top = largest_ref[:1]
-    for ref in plane_refs:
-        total += ref[:rows].astype(jnp.float32)
-        maxima = ref[planes * rows :, :LANES].astype(jnp.float32)
-        top = jnp.maximum(top, maxima[:1])
-    for ref in crossed_refs:
-        total += ref[:, :ff].astype(jnp.float32)
-        top = jnp.maximum(top, ref[:, ff:].astype(jnp.float32)[:1])
-    out_ref[...] = total.astype(jnp.bfloat16)
+    tiles = [jnp.zeros((SUBLANES, LANES), jnp.float32)] * (wide * tall)
+    for ref in (*plane_refs, *crossed_refs):
+        tiles = [tile + ref[i].astype(jnp.float32) for i, tile in enumerate(tiles)]
+        top = jnp.maximum(top, ref[ref.shape[0] - 1].astype(jnp.float32)[:1])
+    total = [jnp.concatenate(tiles[i * wide : (i + 1) * wide], axis=1) for i in range(tall)]
+    out_ref[...] = (own_ref[:rows] + jnp.concatenate(total)).astype(jnp.bfloat16)
     top_ref[0] = jnp.max(top)
 
 
 def finish(own, largest, near, crossed, rows):
     operands = (own, largest, *near, *crossed)
     return pl.pallas_call(
-        functools.partial(finish_kernel, planes=len(crossed) + 1),
+        finish_kernel,
         out_shape=(
             jax.ShapeDtypeStruct((rows, own.shape[1]), jnp.bfloat16),
             jax.ShapeDtypeStruct((1,), jnp.float32),
@@ -297,21 +299,26 @@
         pairs = [(2 * i + c, 2 * (i ^ links[c]) + c) for i in range(n) for c in range(2)]
         return lax.ppermute(block, ("expert", "tensor"), pairs)
 
+    def tiles_of(block):
+        tiles = block.reshape(-1, SUBLANES, ff // LANES, LANES)
+        return tiles.transpose(0, 2, 1, 3).reshape(-1, SUBLANES, LANES)
+
     across = over_link(across, 0).astype(jnp.float32)
-    end = n // PLANE * rows
-    maxima = jnp.pad(second_largest, ((0, 0), (0, ff - LANES)))
-    relay = jnp.concatenate([across[:end] + second, jnp.maximum(across[end:], maxima)])
+    relay = jnp.concatenate(
+        [across[:-1] + tiles_of(second), jnp.maximum(across[-1:], second_largest[None])]
+    )
     near = [over_link(relay.astype(jnp.bfloat16), 1), over_link(first, 0)]
     planes = n // PLANE
+    size = rows * ff // (SUBLANES * LANES)
+    own_tiles = tiles_of(own)
     crossed = []
     for plane in sorted(range(1, planes), key=lambda plane: (plane != 2, plane)):
-        begin = plane * rows
-        total = own[begin : begin + rows]
+        total = own_tiles[plane * size : (plane + 1) * size]
         top = own_largest[plane]
         for block in near:
-            total += block[begin : begin + rows].astype(jnp.float32)
-            top = jnp.maximum(top, block[planes * rows + plane, :LANES].astype(jnp.float32))
-        merged = jnp.concatenate([total, jnp.broadcast_to(top, (rows, LANES))], axis=1)
+            total += block[plane * size : (plane + 1) * size].astype(jnp.float32)
+            top = jnp.maximum(top, block[-1, plane].astype(jnp.float32))
+        merged = jnp.concatenate([total, jnp.broadcast_to(top, (1, SUBLANES, LANES))])
         pairs = [(i, i ^ (plane * PLANE)) for i in range(n)]
         crossed.append(lax.ppermute(merged.astype(jnp.bfloat16), "expert", pairs))
     return finish(own, own_largest, near, crossed, rows)

time: 40.5 us -> 39.8 us (0.983)
  waiting for transfers between devices: 10.3 us -> 9.75 us
where the time goes in v9:
time: 39.8 us; the launch traced here: 39.6 us
  starting transfers between devices  16.8 us (42%)
  Pallas kernels  9.94 us (25%)
  waiting for transfers between devices  9.75 us (24%)
  local copies, waits for them, and re-layouts  2.12 us (5%)
  between operations  0.77 us (2%)
    all_to_all x1, starting transfers between devices, exchange(): lax.all_to_all(block, 'expert', split_axis=0, concat_axis=0, tiled=True,...  8.8 us
    ppermute x3, waiting for transfers between devices, over_link(): return lax.ppermute(block, ('expert', 'tensor'), pairs)  4.94 us
    ppermute x3, starting transfers between devices, kernels(): crossed.append(lax.ppermute(merged.astype(jnp.bfloat16), 'expert', pairs))  4.56 us
    pallas_call x3, Pallas kernels, partials(): pl.pallas_call(functools.partial(partial_kernel, rows=rows, experts=exper...  4.37 us
    ppermute x3, starting transfers between devices, over_link(): return lax.ppermute(block, ('expert', 'tensor'), pairs)  3.35 us
    pallas_call x1, Pallas kernels, hold(): pl.pallas_call(largest_kernel, out_shape=(pltpu.VMEM((kept, depth, ff), w...  3.17 us
    ppermute x3, waiting for transfers between devices, kernels(): crossed.append(lax.ppermute(merged.astype(jnp.bfloat16), 'expert', pairs))  2.53 us
    slice x1, local copies, waits for them, and re-layouts, kernels(): rest = weight[held.shape[0]:]  2.09 us
  transfers between devices with their start and end apart: 9, of which 8 were waited for; matrix products, arithmetic and copies ran while one was open for 6% of the time, Pallas kernels for 16%

profile of v9, /device:TPU:0, one launch (start us, length us, event | category | flops | bytes accessed | tf_op | source)
XLA Modules:
  0.0 39.6 jit_solution(829019328296066469)
XLA Ops:
  0.6 1.7 %shard_map.59 = bf16[16,40,128]{2,1,0:T(8,128)(2,1)} custom-call(bf16[32,4096]{1,0:T(8,128)(2,1)} %tokens_ref.1, s32[8,32]{1,0:T(8,128)} %bitcast.98, f32[8,32]{1,0:T(8,128)} %bitcast.99), custom_call_target="tpu_custom_call" | custom-call | tf_op jit(solution)/shard_map/pallas_call | solution.py:82
  2.4 8.8 %all-to-all-start = ((bf16[16,40,128]{2,1,0:T(8,128)(2,1)}), bf16[16,40,128]{2,1,0:T(8,128)(2,1)S(1)}, u32[]{:S(2)}, u32[]{:S(2)}) async-start(bf16[16,40,128]{2,1,0:T(8,128)(2,1)} %shard_map.59), calls=%async_computation | async-start | bytes 327680 | tf_op jit(solution)/shard_map/all_to_all | solution.py:270
  11.2 3.2 %shard_map.60 = (bf16[8,256,768]{2,1,0:T(8,128)(2,1)S(1)}, f32[16,128]{1,0:T(8,128)S(1)}) custom-call(bf16[16,256,768]{2,1,0:T(8,128)(2,1)} %weight_ref.1), custom_call_target="tpu_custom_call" | custom-call | flops 6291456 | bytes 6291456 | tf_op jit(solution)/shard_map/pallas_call | solution.py:118
  14.3 0.1 collective-permute-start
  14.4 1.2 %collective-permute-done = f32[16,128]{1,0:T(8,128)S(1)} collective-permute-done((f32[16,128]{1,0:T(8,128)S(1)}, f32[16,128]{1,0:T(8,128)S(1)}, u32[]{:S(2)}, u32[]{:S(2)}) %collective-permute-start) | collective-permute-done | bytes 8224 | tf_op jit(solution)/shard_map/ppermute | solution.py:277
  15.6 1.1 %all-to-all-done.refs_0_ = bf16[16,40,128]{2,1,0:T(8,128)(2,1)S(1)} async-done(((bf16[16,40,128]{2,1,0:T(8,128)(2,1)}), bf16[16,40,128]{2,1,0:T(8,128)(2,1)S(1)}, u32[]{:S(2)}, u32[]{:S(2)}) %all-to-all-start) | async-done | bytes 163872 | tf_op jit(solution)/shard_map/all_to_all | solution.py:270
  16.7 2.1 %slice.72.refs_4_ = bf16[2048,768]{1,0:T(8,128)(2,1)S(1)} slice(bf16[4096,768]{1,0:T(8,128)(2,1)} %bitcast.97), slice={[2048:4096], [0:768]} | slice | bytes 6291456 | tf_op jit(solution)/shard_map/slice | solution.py:292
  18.8 1.2 %shard_map.62 = bf16[97,8,128]{2,1,0:T(8,128)(2,1)S(1)} custom-call(bf16[16,40,128]{2,1,0:T(8,128)(2,1)S(1)} %all-to-all-done.refs_0_, bf16[16,40,128]{2,1,0:T(8,128)(2,1)S(1)} %collective-permute-done.1.refs_1_, f32[16,128]{1,0:T(8,128)S(1)} %max.24.refs_2_, bf16[2048,768]{1,0:T(8,128)(2,1)S(1)} %bitcast.92, bf16[2048,768]{1,0:T(8,128)(2,1)S(1)} %slice.72.refs_4_), custom_call_target="tpu_custom_call" | custom-call | flops 805306368 | bytes 6291456 | tf_op jit(solution)/shard_map/pallas_call | solution.py:221
  20.0 1.5 %collective-permute-start.2 = (bf16[97,8,128]{2,1,0:T(8,128)(2,1)S(1)}, bf16[97,8,128]{2,1,0:T(8,128)(2,1)S(1)}, u32[]{:S(2)}, u32[]{:S(2)}) collective-permute-start(bf16[97,8,128]{2,1,0:T(8,128)(2,1)S(1)} %shard_map.62), channel_id=1, source_target_pairs={{0,2},{1,5},{2,0},{3,7},{4,6},{5,1},{6,4},{7,3},{8,10},{9,13},{10,... | collective-permute-start | bytes 595976 | tf_op jit(solution)/shard_map/ppermute | solution.py:300
  21.5 2.0 %shard_map.63 = (f32[128,768]{1,0:T(8,128)S(1)}, f32[8,128]{1,0:T(8,128)S(1)}, bf16[97,8,128]{2,1,0:T(8,128)(2,1)S(1)}) custom-call(bf16[16,40,128]{2,1,0:T(8,128)(2,1)S(1)} %all-to-all-done.refs_0_, bf16[16,40,128]{2,1,0:T(8,128)(2,1)S(1)} %collective-permute-done.1.refs_1_, f32[16,128]{1,0:T(8,128)S(1)} %max.24.refs_2_, bf16[2048,768]{1,0:T(8,128)(2,1)S(1)} %bitcast.93, ...), custom_call_target="tpu_custom_call" | custom-call | flops 1610612736 | bytes 6291456 | tf_op jit(solution)/shard_map/pallas_call | solution.py:221
  23.6 0.6 %collective-permute-start.4 = (bf16[97,8,128]{2,1,0:T(8,128)(2,1)S(1)}, bf16[97,8,128]{2,1,0:T(8,128)(2,1)S(1)}, u32[]{:S(2)}, u32[]{:S(2)}) collective-permute-start(bf16[97,8,128]{2,1,0:T(8,128)(2,1)S(1)} %get-tuple-element.23), channel_id=1, source_target_pairs={{0,2},{1,5},{2,0},{3,7},{4,6},{5,1},{6,4},{7,3},{8,10},{9,13},{10,... | collective-permute-start | bytes 595976 | tf_op jit(solution)/shard_map/ppermute | solution.py:300
  24.2 1.2 %shard_map.61 = (f32[128,768]{1,0:T(8,128)S(1)}, f32[8,128]{1,0:T(8,128)S(1)}) custom-call(bf16[16,40,128]{2,1,0:T(8,128)(2,1)S(1)} %all-to-all-done.refs_0_, bf16[16,40,128]{2,1,0:T(8,128)(2,1)S(1)} %collective-permute-done.1.refs_1_, f32[16,128]{1,0:T(8,128)S(1)} %max.24.refs_2_, bf16[2048,768]{1,0:T(8,128)(2,1)S(1)} %bitcast.94, ...), custom_call_target="tpu_custom_call" | custom-call | flops 805306368 | bytes 6291456 | tf_op jit(solution)/shard_map/pallas_call | solution.py:221
  25.4 0.4 %collective-permute-done.2 = bf16[97,8,128]{2,1,0:T(8,128)(2,1)S(1)} collective-permute-done((bf16[97,8,128]{2,1,0:T(8,128)(2,1)S(1)}, bf16[97,8,128]{2,1,0:T(8,128)(2,1)S(1)}, u32[]{:S(2)}, u32[]{:S(2)}) %collective-permute-start.2) | collective-permute-done | bytes 198688 | tf_op jit(solution)/shard_map/ppermute | solution.py:300
  25.9 1.2 %collective-permute-start.3 = (bf16[97,8,128]{2,1,0:T(8,128)(2,1)S(1)}, bf16[97,8,128]{2,1,0:T(8,128)(2,1)S(1)}, u32[]{:S(2)}, u32[]{:S(2)}) collective-permute-start(bf16[97,8,128]{2,1,0:T(8,128)(2,1)S(1)} %pad_maximum_fusion), channel_id=1, source_target_pairs={{0,4},{1,3},{2,6},{3,1},{4,0},{5,7},{6,2},{7,5},{8,12},{9,11},{10,... | collective-permute-start | bytes 595976 | tf_op jit(solution)/shard_map/ppermute | solution.py:300
  27.1 3.4 %collective-permute-done.4.refs_1_ = bf16[97,8,128]{2,1,0:T(8,128)(2,1)S(1)} collective-permute-done((bf16[97,8,128]{2,1,0:T(8,128)(2,1)S(1)}, bf16[97,8,128]{2,1,0:T(8,128)(2,1)S(1)}, u32[]{:S(2)}, u32[]{:S(2)}) %collective-permute-start.4) | collective-permute-done | bytes 198688 | tf_op jit(solution)/shard_map/ppermute | solution.py:300
  30.5 1.2 %collective-permute-done.3.refs_0_ = bf16[97,8,128]{2,1,0:T(8,128)(2,1)S(1)} collective-permute-done((bf16[97,8,128]{2,1,0:T(8,128)(2,1)S(1)}, bf16[97,8,128]{2,1,0:T(8,128)(2,1)S(1)}, u32[]{:S(2)}, u32[]{:S(2)}) %collective-permute-start.3) | collective-permute-done | bytes 198688 | tf_op jit(solution)/shard_map/ppermute | solution.py:300
  31.7 0.1 fusion.2
  31.7 1.5 %collective-permute-start.7 = (bf16[25,8,128]{2,1,0:T(8,128)(2,1)S(1)}, bf16[25,8,128]{2,1,0:T(8,128)(2,1)S(1)}, u32[]{:S(2)}, u32[]{:S(2)}) collective-permute-start(bf16[25,8,128]{2,1,0:T(8,128)(2,1)S(1)} %pad_maximum_fusion.3), channel_id=1, source_target_pairs={{0,24},{2,26},{4,28},{6,30},{8,16},{10,18},{12,20},{14,22},{16,8},... | collective-permute-start | bytes 153608 | tf_op jit(solution)/shard_map/ppermute | solution.py:323
  33.2 0.1 collective-permute-start.6
  33.3 3.0 %collective-permute-start.5 = (bf16[25,8,128]{2,1,0:T(8,128)(2,1)S(1)}, bf16[25,8,128]{2,1,0:T(8,128)(2,1)S(1)}, u32[]{:S(2)}, u32[]{:S(2)}) collective-permute-start(bf16[25,8,128]{2,1,0:T(8,128)(2,1)S(1)} %pad_maximum_fusion.1), channel_id=1, source_target_pairs={{0,16},{2,18},{4,20},{6,22},{8,24},{10,26},{12,28},{14,30},{16,0},... | collective-permute-start | bytes 153608 | tf_op jit(solution)/shard_map/ppermute | solution.py:323
  36.4 1.8 %collective-permute-done.7.refs_4_ = bf16[25,8,128]{2,1,0:T(8,128)(2,1)S(1)} collective-permute-done((bf16[25,8,128]{2,1,0:T(8,128)(2,1)S(1)}, bf16[25,8,128]{2,1,0:T(8,128)(2,1)S(1)}, u32[]{:S(2)}, u32[]{:S(2)}) %collective-permute-start.7) | collective-permute-done | bytes 51232 | tf_op jit(solution)/shard_map/ppermute | solution.py:323
  38.2 0.3 collective-permute-done.6.refs_3_
  38.5 0.4 collective-permute-done.5.refs_2_
  38.9 0.7 %shard_map.64 = (bf16[32,768]{1,0:T(8,128)(2,1)}, f32[1]{0:T(128)}) custom-call(f32[128,768]{1,0:T(8,128)S(1)} %get-tuple-element.19.own_ref, f32[8,128]{1,0:T(8,128)S(1)} %get-tuple-element.20.largest_ref, bf16[97,8,128]{2,1,0:T(8,128)(2,1)S(1)} %collective-permute-done.3.refs_0_, bf16[97,8,128]{2,1,0:T(8,128)(2,1)S(1)} %collective-permute-done.4.refs_1_, ...), custom_call_target="tpu_custom_call" | custom-call | tf_op jit(solution)/shard_map/pallas_call | solution.py:255
  (15 shorter events, 0.2 us)
Async XLA Ops:
  2.4 14.3 %all-to-all-start = ((bf16[16,40,128]{2,1,0:T(8,128)(2,1)}), bf16[16,40,128]{2,1,0:T(8,128)(2,1)S(1)}, u32[]{:S(2)}, u32[]{:S(2)}) async-start(bf16[16,40,128]{2,1,0:T(8,128)(2,1)} %shard_map.59), calls=%async_computation | async-start | bytes 327680 | tf_op jit(solution)/shard_map/all_to_all | solution.py:270
  14.3 1.2 %collective-permute-start = (f32[16,128]{1,0:T(8,128)S(1)}, f32[16,128]{1,0:T(8,128)S(1)}, u32[]{:S(2)}, u32[]{:S(2)}) collective-permute-start(f32[16,128]{1,0:T(8,128)S(1)} %get-tuple-element.14), channel_id=1, source_target_pairs={{0,1},{1,0},{2,3},{3,2},{4,5},{5,4},{6,7},{7,6},{8,9},{9,8},{10,11... | collective-permute-start | bytes 24584 | tf_op jit(solution)/shard_map/ppermute | solution.py:277
  16.7 2.1 %collective-permute-start.1 = (bf16[16,40,128]{2,1,0:T(8,128)(2,1)S(1)}, bf16[16,40,128]{2,1,0:T(8,128)(2,1)S(1)}, u32[]{:S(2)}, u32[]{:S(2)}) collective-permute-start(bf16[16,40,128]{2,1,0:T(8,128)(2,1)S(1)} %all-to-all-done.refs_0_), channel_id=1, source_target_pairs={{0,1},{1,0},{2,3},{3,2},{4,5},{5,4},{6,7},{7,6},{8,9},{9,8},{10,11... | collective-permute-start | bytes 491528 | tf_op jit(solution)/shard_map/ppermute | solution.py:291
  20.0 5.8 %collective-permute-start.2 = (bf16[97,8,128]{2,1,0:T(8,128)(2,1)S(1)}, bf16[97,8,128]{2,1,0:T(8,128)(2,1)S(1)}, u32[]{:S(2)}, u32[]{:S(2)}) collective-permute-start(bf16[97,8,128]{2,1,0:T(8,128)(2,1)S(1)} %shard_map.62), channel_id=1, source_target_pairs={{0,2},{1,5},{2,0},{3,7},{4,6},{5,1},{6,4},{7,3},{8,10},{9,13},{10,... | collective-permute-start | bytes 595976 | tf_op jit(solution)/shard_map/ppermute | solution.py:300
  23.6 6.9 %collective-permute-start.4 = (bf16[97,8,128]{2,1,0:T(8,128)(2,1)S(1)}, bf16[97,8,128]{2,1,0:T(8,128)(2,1)S(1)}, u32[]{:S(2)}, u32[]{:S(2)}) collective-permute-start(bf16[97,8,128]{2,1,0:T(8,128)(2,1)S(1)} %get-tuple-element.23), channel_id=1, source_target_pairs={{0,2},{1,5},{2,0},{3,7},{4,6},{5,1},{6,4},{7,3},{8,10},{9,13},{10,... | collective-permute-start | bytes 595976 | tf_op jit(solution)/shard_map/ppermute | solution.py:300
  25.9 5.8 %collective-permute-start.3 = (bf16[97,8,128]{2,1,0:T(8,128)(2,1)S(1)}, bf16[97,8,128]{2,1,0:T(8,128)(2,1)S(1)}, u32[]{:S(2)}, u32[]{:S(2)}) collective-permute-start(bf16[97,8,128]{2,1,0:T(8,128)(2,1)S(1)} %pad_maximum_fusion), channel_id=1, source_target_pairs={{0,4},{1,3},{2,6},{3,1},{4,0},{5,7},{6,2},{7,5},{8,12},{9,11},{10,... | collective-permute-start | bytes 595976 | tf_op jit(solution)/shard_map/ppermute | solution.py:300
  31.7 6.5 %collective-permute-start.7 = (bf16[25,8,128]{2,1,0:T(8,128)(2,1)S(1)}, bf16[25,8,128]{2,1,0:T(8,128)(2,1)S(1)}, u32[]{:S(2)}, u32[]{:S(2)}) collective-permute-start(bf16[25,8,128]{2,1,0:T(8,128)(2,1)S(1)} %pad_maximum_fusion.3), channel_id=1, source_target_pairs={{0,24},{2,26},{4,28},{6,30},{8,16},{10,18},{12,20},{14,22},{16,8},... | collective-permute-start | bytes 153608 | tf_op jit(solution)/shard_map/ppermute | solution.py:323
  33.2 5.3 %collective-permute-start.6 = (bf16[25,8,128]{2,1,0:T(8,128)(2,1)S(1)}, bf16[25,8,128]{2,1,0:T(8,128)(2,1)S(1)}, u32[]{:S(2)}, u32[]{:S(2)}) collective-permute-start(bf16[25,8,128]{2,1,0:T(8,128)(2,1)S(1)} %pad_maximum_fusion.2), channel_id=1, source_target_pairs={{0,8},{2,10},{4,12},{6,14},{8,0},{10,2},{12,4},{14,6},{16,24},{18,... | collective-permute-start | bytes 153608 | tf_op jit(solution)/shard_map/ppermute | solution.py:323
  33.3 5.5 %collective-permute-start.5 = (bf16[25,8,128]{2,1,0:T(8,128)(2,1)S(1)}, bf16[25,8,128]{2,1,0:T(8,128)(2,1)S(1)}, u32[]{:S(2)}, u32[]{:S(2)}) collective-permute-start(bf16[25,8,128]{2,1,0:T(8,128)(2,1)S(1)} %pad_maximum_fusion.1), channel_id=1, source_target_pairs={{0,16},{2,18},{4,20},{6,22},{8,24},{10,26},{12,28},{14,30},{16,0},... | collective-permute-start | bytes 153608 | tf_op jit(solution)/shard_map/ppermute | solution.py:323

commit v10 on v9

--- a/solution.py
+++ b/solution.py
@@ -63,9 +63,9 @@
     packed = jnp.concatenate(terms, axis=1).astype(jnp.bfloat16)
     for i in range(n):
         block_ref[i, rows:, :] = packed
-    group = n // 4
+    group = n // 8
     outs = []
-    for i in range(4):
+    for i in range(8):
         part = pl.ds(i * group, group)
         for copy in copies[2 + i * group : 2 + (i + 1) * group]:
             copy.wait()
@@ -89,7 +89,7 @@
             pltpu.VMEM((choices, rows), jnp.int32),
             pltpu.VMEM((choices, rows), jnp.float32),
             pltpu.SemaphoreType.DMA((n + 2,)),
-            pltpu.SemaphoreType.DMA((4,)),
+            pltpu.SemaphoreType.DMA((8,)),
         ],
         compiler_params=params(8),
     )(*(pltpu.with_memory_space_constraint(operand, pltpu.HBM) for operand in operands))

time: 39.8 us -> 39.9 us (level)
  no operation moved by 1% of the time
where the time goes in v10:
time: 39.9 us; the launch traced here: 39.6 us
  starting transfers between devices  16.8 us (42%)
  Pallas kernels  9.97 us (25%)
  waiting for transfers between devices  9.76 us (24%)
  local copies, waits for them, and re-layouts  2.12 us (5%)
  between operations  0.77 us (2%)
    all_to_all x1, starting transfers between devices, exchange(): lax.all_to_all(block, 'expert', split_axis=0, concat_axis=0, tiled=True,...  8.8 us
    ppermute x3, waiting for transfers between devices, over_link(): return lax.ppermute(block, ('expert', 'tensor'), pairs)  4.95 us
    ppermute x3, starting transfers between devices, kernels(): crossed.append(lax.ppermute(merged.astype(jnp.bfloat16), 'expert', pairs))  4.56 us
    pallas_call x3, Pallas kernels, partials(): pl.pallas_call(functools.partial(partial_kernel, rows=rows, experts=exper...  4.37 us
    ppermute x3, starting transfers between devices, over_link(): return lax.ppermute(block, ('expert', 'tensor'), pairs)  3.34 us
    pallas_call x1, Pallas kernels, hold(): pl.pallas_call(largest_kernel, out_shape=(pltpu.VMEM((kept, depth, ff), w...  3.17 us
    ppermute x3, waiting for transfers between devices, kernels(): crossed.append(lax.ppermute(merged.astype(jnp.bfloat16), 'expert', pairs))  2.52 us
    slice x1, local copies, waits for them, and re-layouts, kernels(): rest = weight[held.shape[0]:]  2.09 us
  transfers between devices with their start and end apart: 9, of which 8 were waited for; matrix products, arithmetic and copies ran while one was open for 6% of the time, Pallas kernels for 16%

profile of v10, /device:TPU:0, one launch (start us, length us, event | category | flops | bytes accessed | tf_op | source)
XLA Modules:
  0.0 39.6 jit_solution(3430204566032286371)
XLA Ops:
  0.6 1.8 %shard_map.59 = bf16[16,40,128]{2,1,0:T(8,128)(2,1)} custom-call(bf16[32,4096]{1,0:T(8,128)(2,1)} %tokens_ref.1, s32[8,32]{1,0:T(8,128)} %bitcast.98, f32[8,32]{1,0:T(8,128)} %bitcast.99), custom_call_target="tpu_custom_call" | custom-call | tf_op jit(solution)/shard_map/pallas_call | solution.py:82
  2.4 8.8 %all-to-all-start = ((bf16[16,40,128]{2,1,0:T(8,128)(2,1)}), bf16[16,40,128]{2,1,0:T(8,128)(2,1)S(1)}, u32[]{:S(2)}, u32[]{:S(2)}) async-start(bf16[16,40,128]{2,1,0:T(8,128)(2,1)} %shard_map.59), calls=%async_computation | async-start | bytes 327680 | tf_op jit(solution)/shard_map/all_to_all | solution.py:270
  11.2 3.2 %shard_map.60 = (bf16[8,256,768]{2,1,0:T(8,128)(2,1)S(1)}, f32[16,128]{1,0:T(8,128)S(1)}) custom-call(bf16[16,256,768]{2,1,0:T(8,128)(2,1)} %weight_ref.1), custom_call_target="tpu_custom_call" | custom-call | flops 6291456 | bytes 6291456 | tf_op jit(solution)/shard_map/pallas_call | solution.py:118
  14.4 0.1 collective-permute-start
  14.5 1.2 %collective-permute-done = f32[16,128]{1,0:T(8,128)S(1)} collective-permute-done((f32[16,128]{1,0:T(8,128)S(1)}, f32[16,128]{1,0:T(8,128)S(1)}, u32[]{:S(2)}, u32[]{:S(2)}) %collective-permute-start) | collective-permute-done | bytes 8224 | tf_op jit(solution)/shard_map/ppermute | solution.py:277
  15.6 1.1 %all-to-all-done.refs_0_ = bf16[16,40,128]{2,1,0:T(8,128)(2,1)S(1)} async-done(((bf16[16,40,128]{2,1,0:T(8,128)(2,1)}), bf16[16,40,128]{2,1,0:T(8,128)(2,1)S(1)}, u32[]{:S(2)}, u32[]{:S(2)}) %all-to-all-start) | async-done | bytes 163872 | tf_op jit(solution)/shard_map/all_to_all | solution.py:270
  16.7 2.1 %slice.72.refs_4_ = bf16[2048,768]{1,0:T(8,128)(2,1)S(1)} slice(bf16[4096,768]{1,0:T(8,128)(2,1)} %bitcast.97), slice={[2048:4096], [0:768]} | slice | bytes 6291456 | tf_op jit(solution)/shard_map/slice | solution.py:292
  18.9 1.2 %shard_map.62 = bf16[97,8,128]{2,1,0:T(8,128)(2,1)S(1)} custom-call(bf16[16,40,128]{2,1,0:T(8,128)(2,1)S(1)} %all-to-all-done.refs_0_, bf16[16,40,128]{2,1,0:T(8,128)(2,1)S(1)} %collective-permute-done.1.refs_1_, f32[16,128]{1,0:T(8,128)S(1)} %max.24.refs_2_, bf16[2048,768]{1,0:T(8,128)(2,1)S(1)} %bitcast.92, bf16[2048,768]{1,0:T(8,128)(2,1)S(1)} %slice.72.refs_4_), custom_call_target="tpu_custom_call" | custom-call | flops 805306368 | bytes 6291456 | tf_op jit(solution)/shard_map/pallas_call | solution.py:221
  20.1 1.5 %collective-permute-start.2 = (bf16[97,8,128]{2,1,0:T(8,128)(2,1)S(1)}, bf16[97,8,128]{2,1,0:T(8,128)(2,1)S(1)}, u32[]{:S(2)}, u32[]{:S(2)}) collective-permute-start(bf16[97,8,128]{2,1,0:T(8,128)(2,1)S(1)} %shard_map.62), channel_id=1, source_target_pairs={{0,2},{1,5},{2,0},{3,7},{4,6},{5,1},{6,4},{7,3},{8,10},{9,13},{10,... | collective-permute-start | bytes 595976 | tf_op jit(solution)/shard_map/ppermute | solution.py:300
  21.6 2.0 %shard_map.63 = (f32[128,768]{1,0:T(8,128)S(1)}, f32[8,128]{1,0:T(8,128)S(1)}, bf16[97,8,128]{2,1,0:T(8,128)(2,1)S(1)}) custom-call(bf16[16,40,128]{2,1,0:T(8,128)(2,1)S(1)} %all-to-all-done.refs_0_, bf16[16,40,128]{2,1,0:T(8,128)(2,1)S(1)} %collective-permute-done.1.refs_1_, f32[16,128]{1,0:T(8,128)S(1)} %max.24.refs_2_, bf16[2048,768]{1,0:T(8,128)(2,1)S(1)} %bitcast.93, ...), custom_call_target="tpu_custom_call" | custom-call | flops 1610612736 | bytes 6291456 | tf_op jit(solution)/shard_map/pallas_call | solution.py:221
  23.6 0.6 %collective-permute-start.4 = (bf16[97,8,128]{2,1,0:T(8,128)(2,1)S(1)}, bf16[97,8,128]{2,1,0:T(8,128)(2,1)S(1)}, u32[]{:S(2)}, u32[]{:S(2)}) collective-permute-start(bf16[97,8,128]{2,1,0:T(8,128)(2,1)S(1)} %get-tuple-element.23), channel_id=1, source_target_pairs={{0,2},{1,5},{2,0},{3,7},{4,6},{5,1},{6,4},{7,3},{8,10},{9,13},{10,... | collective-permute-start | bytes 595976 | tf_op jit(solution)/shard_map/ppermute | solution.py:300
  24.2 1.2 %shard_map.61 = (f32[128,768]{1,0:T(8,128)S(1)}, f32[8,128]{1,0:T(8,128)S(1)}) custom-call(bf16[16,40,128]{2,1,0:T(8,128)(2,1)S(1)} %all-to-all-done.refs_0_, bf16[16,40,128]{2,1,0:T(8,128)(2,1)S(1)} %collective-permute-done.1.refs_1_, f32[16,128]{1,0:T(8,128)S(1)} %max.24.refs_2_, bf16[2048,768]{1,0:T(8,128)(2,1)S(1)} %bitcast.94, ...), custom_call_target="tpu_custom_call" | custom-call | flops 805306368 | bytes 6291456 | tf_op jit(solution)/shard_map/pallas_call | solution.py:221
  25.4 0.4 %collective-permute-done.2 = bf16[97,8,128]{2,1,0:T(8,128)(2,1)S(1)} collective-permute-done((bf16[97,8,128]{2,1,0:T(8,128)(2,1)S(1)}, bf16[97,8,128]{2,1,0:T(8,128)(2,1)S(1)}, u32[]{:S(2)}, u32[]{:S(2)}) %collective-permute-start.2) | collective-permute-done | bytes 198688 | tf_op jit(solution)/shard_map/ppermute | solution.py:300
  25.9 1.2 %collective-permute-start.3 = (bf16[97,8,128]{2,1,0:T(8,128)(2,1)S(1)}, bf16[97,8,128]{2,1,0:T(8,128)(2,1)S(1)}, u32[]{:S(2)}, u32[]{:S(2)}) collective-permute-start(bf16[97,8,128]{2,1,0:T(8,128)(2,1)S(1)} %pad_maximum_fusion), channel_id=1, source_target_pairs={{0,4},{1,3},{2,6},{3,1},{4,0},{5,7},{6,2},{7,5},{8,12},{9,11},{10,... | collective-permute-start | bytes 595976 | tf_op jit(solution)/shard_map/ppermute | solution.py:300
  27.1 3.4 %collective-permute-done.4.refs_1_ = bf16[97,8,128]{2,1,0:T(8,128)(2,1)S(1)} collective-permute-done((bf16[97,8,128]{2,1,0:T(8,128)(2,1)S(1)}, bf16[97,8,128]{2,1,0:T(8,128)(2,1)S(1)}, u32[]{:S(2)}, u32[]{:S(2)}) %collective-permute-start.4) | collective-permute-done | bytes 198688 | tf_op jit(solution)/shard_map/ppermute | solution.py:300
  30.5 1.2 %collective-permute-done.3.refs_0_ = bf16[97,8,128]{2,1,0:T(8,128)(2,1)S(1)} collective-permute-done((bf16[97,8,128]{2,1,0:T(8,128)(2,1)S(1)}, bf16[97,8,128]{2,1,0:T(8,128)(2,1)S(1)}, u32[]{:S(2)}, u32[]{:S(2)}) %collective-permute-start.3) | collective-permute-done | bytes 198688 | tf_op jit(solution)/shard_map/ppermute | solution.py:300
  31.7 0.1 fusion.2
  31.8 1.5 %collective-permute-start.7 = (bf16[25,8,128]{2,1,0:T(8,128)(2,1)S(1)}, bf16[25,8,128]{2,1,0:T(8,128)(2,1)S(1)}, u32[]{:S(2)}, u32[]{:S(2)}) collective-permute-start(bf16[25,8,128]{2,1,0:T(8,128)(2,1)S(1)} %pad_maximum_fusion.3), channel_id=1, source_target_pairs={{0,24},{2,26},{4,28},{6,30},{8,16},{10,18},{12,20},{14,22},{16,8},... | collective-permute-start | bytes 153608 | tf_op jit(solution)/shard_map/ppermute | solution.py:323
  33.3 0.1 collective-permute-start.6
  33.4 3.0 %collective-permute-start.5 = (bf16[25,8,128]{2,1,0:T(8,128)(2,1)S(1)}, bf16[25,8,128]{2,1,0:T(8,128)(2,1)S(1)}, u32[]{:S(2)}, u32[]{:S(2)}) collective-permute-start(bf16[25,8,128]{2,1,0:T(8,128)(2,1)S(1)} %pad_maximum_fusion.1), channel_id=1, source_target_pairs={{0,16},{2,18},{4,20},{6,22},{8,24},{10,26},{12,28},{14,30},{16,0},... | collective-permute-start | bytes 153608 | tf_op jit(solution)/shard_map/ppermute | solution.py:323
  36.4 1.8 %collective-permute-done.7.refs_4_ = bf16[25,8,128]{2,1,0:T(8,128)(2,1)S(1)} collective-permute-done((bf16[25,8,128]{2,1,0:T(8,128)(2,1)S(1)}, bf16[25,8,128]{2,1,0:T(8,128)(2,1)S(1)}, u32[]{:S(2)}, u32[]{:S(2)}) %collective-permute-start.7) | collective-permute-done | bytes 51232 | tf_op jit(solution)/shard_map/ppermute | solution.py:323
  38.2 0.3 collective-permute-done.6.refs_3_
  38.5 0.4 collective-permute-done.5.refs_2_
  38.9 0.7 %shard_map.64 = (bf16[32,768]{1,0:T(8,128)(2,1)}, f32[1]{0:T(128)}) custom-call(f32[128,768]{1,0:T(8,128)S(1)} %get-tuple-element.19.own_ref, f32[8,128]{1,0:T(8,128)S(1)} %get-tuple-element.20.largest_ref, bf16[97,8,128]{2,1,0:T(8,128)(2,1)S(1)} %collective-permute-done.3.refs_0_, bf16[97,8,128]{2,1,0:T(8,128)(2,1)S(1)} %collective-permute-done.4.refs_1_, ...), custom_call_target="tpu_custom_call" | custom-call | tf_op jit(solution)/shard_map/pallas_call | solution.py:255
  (15 shorter events, 0.2 us)
Async XLA Ops:
  2.4 14.3 %all-to-all-start = ((bf16[16,40,128]{2,1,0:T(8,128)(2,1)}), bf16[16,40,128]{2,1,0:T(8,128)(2,1)S(1)}, u32[]{:S(2)}, u32[]{:S(2)}) async-start(bf16[16,40,128]{2,1,0:T(8,128)(2,1)} %shard_map.59), calls=%async_computation | async-start | bytes 327680 | tf_op jit(solution)/shard_map/all_to_all | solution.py:270
  14.4 1.2 %collective-permute-start = (f32[16,128]{1,0:T(8,128)S(1)}, f32[16,128]{1,0:T(8,128)S(1)}, u32[]{:S(2)}, u32[]{:S(2)}) collective-permute-start(f32[16,128]{1,0:T(8,128)S(1)} %get-tuple-element.14), channel_id=1, source_target_pairs={{0,1},{1,0},{2,3},{3,2},{4,5},{5,4},{6,7},{7,6},{8,9},{9,8},{10,11... | collective-permute-start | bytes 24584 | tf_op jit(solution)/shard_map/ppermute | solution.py:277
  16.7 2.1 %collective-permute-start.1 = (bf16[16,40,128]{2,1,0:T(8,128)(2,1)S(1)}, bf16[16,40,128]{2,1,0:T(8,128)(2,1)S(1)}, u32[]{:S(2)}, u32[]{:S(2)}) collective-permute-start(bf16[16,40,128]{2,1,0:T(8,128)(2,1)S(1)} %all-to-all-done.refs_0_), channel_id=1, source_target_pairs={{0,1},{1,0},{2,3},{3,2},{4,5},{5,4},{6,7},{7,6},{8,9},{9,8},{10,11... | collective-permute-start | bytes 491528 | tf_op jit(solution)/shard_map/ppermute | solution.py:291
  20.1 5.8 %collective-permute-start.2 = (bf16[97,8,128]{2,1,0:T(8,128)(2,1)S(1)}, bf16[97,8,128]{2,1,0:T(8,128)(2,1)S(1)}, u32[]{:S(2)}, u32[]{:S(2)}) collective-permute-start(bf16[97,8,128]{2,1,0:T(8,128)(2,1)S(1)} %shard_map.62), channel_id=1, source_target_pairs={{0,2},{1,5},{2,0},{3,7},{4,6},{5,1},{6,4},{7,3},{8,10},{9,13},{10,... | collective-permute-start | bytes 595976 | tf_op jit(solution)/shard_map/ppermute | solution.py:300
  23.6 6.9 %collective-permute-start.4 = (bf16[97,8,128]{2,1,0:T(8,128)(2,1)S(1)}, bf16[97,8,128]{2,1,0:T(8,128)(2,1)S(1)}, u32[]{:S(2)}, u32[]{:S(2)}) collective-permute-start(bf16[97,8,128]{2,1,0:T(8,128)(2,1)S(1)} %get-tuple-element.23), channel_id=1, source_target_pairs={{0,2},{1,5},{2,0},{3,7},{4,6},{5,1},{6,4},{7,3},{8,10},{9,13},{10,... | collective-permute-start | bytes 595976 | tf_op jit(solution)/shard_map/ppermute | solution.py:300
  25.9 5.8 %collective-permute-start.3 = (bf16[97,8,128]{2,1,0:T(8,128)(2,1)S(1)}, bf16[97,8,128]{2,1,0:T(8,128)(2,1)S(1)}, u32[]{:S(2)}, u32[]{:S(2)}) collective-permute-start(bf16[97,8,128]{2,1,0:T(8,128)(2,1)S(1)} %pad_maximum_fusion), channel_id=1, source_target_pairs={{0,4},{1,3},{2,6},{3,1},{4,0},{5,7},{6,2},{7,5},{8,12},{9,11},{10,... | collective-permute-start | bytes 595976 | tf_op jit(solution)/shard_map/ppermute | solution.py:300
  31.8 6.4 %collective-permute-start.7 = (bf16[25,8,128]{2,1,0:T(8,128)(2,1)S(1)}, bf16[25,8,128]{2,1,0:T(8,128)(2,1)S(1)}, u32[]{:S(2)}, u32[]{:S(2)}) collective-permute-start(bf16[25,8,128]{2,1,0:T(8,128)(2,1)S(1)} %pad_maximum_fusion.3), channel_id=1, source_target_pairs={{0,24},{2,26},{4,28},{6,30},{8,16},{10,18},{12,20},{14,22},{16,8},... | collective-permute-start | bytes 153608 | tf_op jit(solution)/shard_map/ppermute | solution.py:323
  33.3 5.3 %collective-permute-start.6 = (bf16[25,8,128]{2,1,0:T(8,128)(2,1)S(1)}, bf16[25,8,128]{2,1,0:T(8,128)(2,1)S(1)}, u32[]{:S(2)}, u32[]{:S(2)}) collective-permute-start(bf16[25,8,128]{2,1,0:T(8,128)(2,1)S(1)} %pad_maximum_fusion.2), channel_id=1, source_target_pairs={{0,8},{2,10},{4,12},{6,14},{8,0},{10,2},{12,4},{14,6},{16,24},{18,... | collective-permute-start | bytes 153608 | tf_op jit(solution)/shard_map/ppermute | solution.py:323
  33.4 5.5 %collective-permute-start.5 = (bf16[25,8,128]{2,1,0:T(8,128)(2,1)S(1)}, bf16[25,8,128]{2,1,0:T(8,128)(2,1)S(1)}, u32[]{:S(2)}, u32[]{:S(2)}) collective-permute-start(bf16[25,8,128]{2,1,0:T(8,128)(2,1)S(1)} %pad_maximum_fusion.1), channel_id=1, source_target_pairs={{0,16},{2,18},{4,20},{6,22},{8,24},{10,26},{12,28},{14,30},{16,0},... | collective-permute-start | bytes 153608 | tf_op jit(solution)/shard_map/ppermute | solution.py:323
